TPU v7x, 32 devices: a whole 2x2x4 slice. The times are simulated.
32 devices in a mesh: dp: 8 (over z, y), tensor: 4 (over x, core).
Axes of the slice: x: 2, y: 2, z: 4, core: 2. Of those that a mesh axis runs over, the one named last changes fastest.
Arguments:
- tokens: bfloat16 [2, 1536, 2048], P(None, ('dp', 'tensor')), may hold values from -6 to 6
- depth: int32 [2, 1536], P(None, 'dp'), may hold values from 1 to 3, as said below
- lengths: int32 [2, 8, 3], P(None, 'dp'), may hold values from 1 to 128, 192 in all within a row
- cotangent: bfloat16 [2, 1536, 2048], P(None, ('dp', 'tensor')), may hold values from -6 to 6
- w_query: bfloat16 [2048, 2048], P('dp', 'tensor'), may hold values from -0.125 to 0.125
- w_key: bfloat16 [2048, 256], P('dp', 'tensor'), may hold values from -0.125 to 0.125
- w_value: bfloat16 [2048, 256], P('dp', 'tensor'), may hold values from -0.125 to 0.125
- w_out: bfloat16 [2048, 2048], P('tensor', 'dp'), may hold values from -0.75 to 0.75
- w_gate: bfloat16 [2048, 5632], P('dp', 'tensor'), may hold values from -0.125 to 0.125
- w_up: bfloat16 [2048, 5632], P('dp', 'tensor'), may hold values from -0.125 to 0.125
- w_down: bfloat16 [5632, 2048], P('tensor', 'dp'), may hold values from -0.15625 to 0.15625
- attn_gain: float32 [2048], P(('dp', 'tensor')), may hold values from 0.5 to 1.5
- mlp_gain: float32 [2048], P(('dp', 'tensor')), may hold values from 0.5 to 1.5
Outputs:
- activations: bfloat16 [2, 1536, 2048], P(None, ('dp', 'tensor'))
- tokens_grad: float32 [2, 1536, 2048], P(None, ('dp', 'tensor'))
- w_query_grad: float32 [2048, 2048], P('dp', 'tensor')
- w_key_grad: float32 [2048, 256], P('dp', 'tensor')
- w_value_grad: float32 [2048, 256], P('dp', 'tensor')
- w_out_grad: float32 [2048, 2048], P('tensor', 'dp')
- w_gate_grad: float32 [2048, 5632], P('dp', 'tensor')
- w_up_grad: float32 [2048, 5632], P('dp', 'tensor')
- w_down_grad: float32 [5632, 2048], P('tensor', 'dp')
- attn_gain_grad: float32 [2048], P(('dp', 'tensor'))
- mlp_gain_grad: float32 [2048], P(('dp', 'tensor'))
Inputs may be any that keep to these rules, and one draw needn't show every extreme that they name: Within each micro-batch and the 192 rows of each dp index, at most 144 rows have depth 2 or more and at most 72 have depth 3; in every micro-batch some dp index has exactly 144 and some exactly 72.
All inputs are finite; a program needn't handle non-finite values.
Results may differ from a plain program's by a relative error of at most 0.035.
Values may be sent and summed in bfloat16 or wider, within the bound.
A program may use at most 256 MiB of HBM per device.

v0:
```python
import jax
import jax.numpy as jnp
from jax import lax
from jax.sharding import PartitionSpec as P

HQ = 32
KVH = 4
HS = 64
MB = 2
RECUR = 3
DEPTH_TWO_LIMIT = 144
DEPTH_THREE_LIMIT = 72


def normalize(hidden, gain):
    inverse = lax.rsqrt(jnp.mean(hidden * hidden, axis=-1, keepdims=True) + 1e-05)
    return hidden * inverse * gain


def norm_back(source, gain, upstream, residual):
    inverse = lax.rsqrt(jnp.mean(source * source, axis=-1, keepdims=True) + 1e-05)
    unit = source * inverse
    gain_part = jnp.sum(upstream * unit, axis=0)
    scaled = upstream * gain
    update = inverse * (scaled - unit * jnp.mean(scaled * unit, axis=-1, keepdims=True))
    return (residual + update, gain_part)


def turned(values):
    half = values.shape[-1] // 2
    return jnp.concatenate([-values[..., half:], values[..., :half]], axis=-1)


def rotate(values, cosine, sine):
    return values * cosine + turned(values) * sine


def unrotate(values, cosine, sine):
    return values * cosine - turned(values) * sine


def layout(lengths_row, compact_rows):
    rows = jnp.arange(compact_rows, dtype=jnp.int32)
    ends = jnp.cumsum(lengths_row)
    starts = ends - lengths_row
    member = ((rows[:, None] >= starts[None, :]) & (rows[:, None] < ends[None, :])).astype(
        jnp.int32
    )
    numbers = jnp.arange(lengths_row.shape[0], dtype=jnp.int32)
    document = jnp.sum(member * numbers[None, :], axis=1)
    offset = rows - jnp.sum(member * starts[None, :], axis=1)
    freqs = 10000.0 ** (-jnp.arange(0, HS, 2).astype(jnp.float32) / HS)
    angles = offset.astype(jnp.float32)[:, None] * freqs[None, :]
    angles = jnp.concatenate([angles, angles], axis=-1)
    return (document, jnp.cos(angles), jnp.sin(angles))


def matmul(left, right):
    return jnp.dot(left, right, preferred_element_type=jnp.float32)


def left_times(left, right):
    return jnp.einsum("ca,cb->ab", left, right, preferred_element_type=jnp.float32)


def right_times(left, right):
    return jnp.einsum("cb,ab->ca", left, right, preferred_element_type=jnp.float32)


def masked_scores(query, key, allowed, scale):
    attention_scores = (
        jnp.einsum("ckgd,skd->kgcs", query, key, preferred_element_type=jnp.float32) * scale
    )
    return jnp.where(allowed[None, None], attention_scores, -1e30)


def attend(query, key, value, allowed, scale):
    attention_scores = masked_scores(query, key, allowed, scale)
    largest = jnp.max(attention_scores, axis=-1, keepdims=True)
    raised = jnp.exp(attention_scores - largest)
    totals = jnp.sum(raised, axis=-1, keepdims=True)
    shares = (raised / totals).astype(jnp.bfloat16)
    attended = jnp.einsum("kgcs,skd->ckgd", shares, value, preferred_element_type=jnp.float32)
    return (attended.astype(jnp.bfloat16), largest + jnp.log(totals))


def attend_back(query, key, value, allowed, scale, total_log, attended_grad):
    attention_scores = masked_scores(query, key, allowed, scale)
    shares = jnp.exp(attention_scores - total_log)
    shares_grad = jnp.einsum(
        "ckgd,skd->kgcs", attended_grad, value, preferred_element_type=jnp.float32
    )
    value_grad = jnp.einsum(
        "kgcs,ckgd->skd",
        shares.astype(jnp.bfloat16),
        attended_grad,
        preferred_element_type=jnp.float32,
    )
    spread = jnp.sum(shares * shares_grad, axis=-1, keepdims=True)
    score_grad = (shares * (shares_grad - spread)).astype(jnp.bfloat16)
    query_grad = (
        jnp.einsum("kgcs,skd->ckgd", score_grad, key, preferred_element_type=jnp.float32) * scale
    )
    key_grad = (
        jnp.einsum("kgcs,ckgd->skd", score_grad, query, preferred_element_type=jnp.float32) * scale
    )
    return (query_grad, key_grad, value_grad)


def spread_rows(values):
    return lax.all_gather(values, "tensor", axis=0, tiled=True)


def collect_rows(values):
    return lax.psum_scatter(
        values.astype(jnp.bfloat16), "tensor", scatter_dimension=0, tiled=True
    ).astype(jnp.float32)


def scatter_gradients(values):
    return lax.all_gather(values, "tensor", axis=0, tiled=True)


def collect_grads(values):
    return lax.psum_scatter(
        values.astype(jnp.bfloat16), "tensor", scatter_dimension=0, tiled=True
    ).astype(jnp.float32)


def shards(
    tokens,
    depth,
    lengths,
    cotangent,
    w_query,
    w_key,
    w_value,
    w_out,
    w_gate,
    w_up,
    w_down,
    attn_gain,
    mlp_gain,
):
    attn_scale, mlp_scale = (
        lax.all_gather(attn_gain, ("dp", "tensor"), axis=0, tiled=True),
        lax.all_gather(mlp_gain, ("dp", "tensor"), axis=0, tiled=True),
    )
    local_rows = tokens.shape[1]
    width = tokens.shape[2]
    compact_rows = depth.shape[1]
    tensor_index = lax.axis_index("tensor")
    start_row = tensor_index * local_rows
    scale = HS ** (-0.5)
    group = HQ // KVH
    level_limits = (compact_rows, DEPTH_TWO_LIMIT, DEPTH_THREE_LIMIT)
    results = []
    input_grads = []
    grad_total = None
    attn_gain_grad = jnp.zeros((width,), jnp.float32)
    mlp_gain_grad = jnp.zeros((width,), jnp.float32)
    for batch in range(MB):
        gathered = (
            lax.all_gather(w_query, "dp", axis=0, tiled=True),
            lax.all_gather(w_key, "dp", axis=0, tiled=True),
            lax.all_gather(w_value, "dp", axis=0, tiled=True),
            lax.all_gather(w_out, "dp", axis=1, tiled=True),
            lax.all_gather(w_gate, "dp", axis=0, tiled=True),
            lax.all_gather(w_up, "dp", axis=0, tiled=True),
            lax.all_gather(w_down, "dp", axis=1, tiled=True),
        )
        query_weight, key_weight, value_weight, out_weight, gate_weight, up_weight, down_weight = (
            gathered
        )
        kv_local = key_weight.shape[1] // HS
        depth_row = depth[batch]
        local_depth = lax.dynamic_slice_in_dim(depth_row, start_row, local_rows)
        document, cosine, sine = layout(lengths[batch, 0], compact_rows)
        hidden = tokens[batch].astype(jnp.float32)
        saved = []
        for recursion_level in range(1, RECUR + 1):
            token_limit = level_limits[recursion_level - 1]
            active = depth_row >= recursion_level
            chosen = jnp.nonzero(active, size=token_limit, fill_value=0)[0].astype(jnp.int32)
            present = jnp.arange(token_limit) < jnp.sum(active.astype(jnp.int32))
            chosen_doc = document[chosen]
            allowed = (chosen_doc[:, None] == chosen_doc[None, :]) & (
                chosen[None, :] <= chosen[:, None]
            ) & present[None, :] | jnp.eye(token_limit, dtype=bool)
            cos_rows = cosine[chosen][:, None, :]
            sin_rows = sine[chosen][:, None, :]
            present_col = present.astype(jnp.float32)[:, None]
            normed = spread_rows(normalize(hidden, attn_scale).astype(jnp.bfloat16))[chosen]
            query = rotate(
                matmul(normed, query_weight).reshape(token_limit, -1, HS), cos_rows, sin_rows
            )
            query = query.astype(jnp.bfloat16).reshape(token_limit, kv_local, group, HS)
            key = rotate(
                matmul(normed, key_weight).reshape(token_limit, kv_local, HS), cos_rows, sin_rows
            ).astype(jnp.bfloat16)
            value = (
                matmul(normed, value_weight).astype(jnp.bfloat16).reshape(token_limit, kv_local, HS)
            )
            attended, total_log = attend(query, key, value, allowed, scale)
            attended = attended.reshape(token_limit, -1)
            branch = matmul(attended, out_weight) * present_col
            first = hidden + collect_rows(
                jnp.zeros((compact_rows, width), jnp.float32).at[chosen].add(branch)
            )
            mixed = spread_rows(normalize(first, mlp_scale).astype(jnp.bfloat16))[chosen]
            gate = matmul(mixed, gate_weight)
            upward = matmul(mixed, up_weight)
            product = (jax.nn.silu(gate) * upward).astype(jnp.bfloat16)
            branch = matmul(product, down_weight) * present_col
            saved.append(
                (
                    hidden,
                    first,
                    chosen,
                    present,
                    allowed,
                    cos_rows,
                    sin_rows,
                    normed,
                    query,
                    key,
                    value,
                    total_log,
                    attended,
                    mixed,
                    gate,
                    upward,
                    product,
                )
            )
            hidden = first + collect_rows(
                jnp.zeros((compact_rows, width), jnp.float32).at[chosen].add(branch)
            )
        results.append(hidden.astype(jnp.bfloat16))
        grad = cotangent[batch].astype(jnp.float32)
        weight_grads = [jnp.zeros(matrix.shape, jnp.float32) for matrix in gathered]
        for recursion_level in range(RECUR, 0, -1):
            (
                before,
                first,
                chosen,
                present,
                allowed,
                cos_rows,
                sin_rows,
                normed,
                query,
                key,
                value,
                total_log,
                attended,
                mixed,
                gate,
                upward,
                product,
            ) = saved[recursion_level - 1]
            token_limit = chosen.shape[0]
            present_low = present.astype(jnp.bfloat16)[:, None]
            lane_gate = (local_depth >= recursion_level).astype(jnp.float32)[:, None]
            down_grad = (
                scatter_gradients((lane_gate * grad).astype(jnp.bfloat16))[chosen] * present_low
            )
            weight_grads[6] = weight_grads[6] + left_times(product, down_grad)
            product_grad = right_times(down_grad, down_weight)
            sigma = jax.nn.sigmoid(gate)
            gate_grad = (product_grad * upward * sigma * (1.0 + gate * (1.0 - sigma))).astype(
                jnp.bfloat16
            )
            up_grad = (product_grad * gate * sigma).astype(jnp.bfloat16)
            weight_grads[4] = weight_grads[4] + left_times(mixed, gate_grad)
            weight_grads[5] = weight_grads[5] + left_times(mixed, up_grad)
            mixed_grad = right_times(gate_grad, gate_weight) + right_times(up_grad, up_weight)
            local_mixed = collect_grads(
                jnp.zeros((compact_rows, width), jnp.float32).at[chosen].add(mixed_grad)
            )
            grad, gain_part = norm_back(first, mlp_scale, local_mixed, grad)
            mlp_gain_grad = mlp_gain_grad + gain_part
            out_grad = (
                scatter_gradients((lane_gate * grad).astype(jnp.bfloat16))[chosen] * present_low
            )
            weight_grads[3] = weight_grads[3] + left_times(attended, out_grad)
            attended_grad = (
                right_times(out_grad, out_weight)
                .astype(jnp.bfloat16)
                .reshape(token_limit, kv_local, group, HS)
            )
            query_grad, key_grad, value_grad = attend_back(
                query, key, value, allowed, scale, total_log, attended_grad
            )
            query_grad = (
                unrotate(query_grad.reshape(token_limit, -1, HS), cos_rows, sin_rows)
                .astype(jnp.bfloat16)
                .reshape(token_limit, -1)
            )
            key_grad = (
                unrotate(key_grad, cos_rows, sin_rows).astype(jnp.bfloat16).reshape(token_limit, -1)
            )
            value_grad = value_grad.astype(jnp.bfloat16).reshape(token_limit, -1)
            weight_grads[0] = weight_grads[0] + left_times(normed, query_grad)
            weight_grads[1] = weight_grads[1] + left_times(normed, key_grad)
            weight_grads[2] = weight_grads[2] + left_times(normed, value_grad)
            normed_grad = (
                right_times(query_grad, query_weight)
                + right_times(key_grad, key_weight)
                + right_times(value_grad, value_weight)
            )
            local_normed = collect_grads(
                jnp.zeros((compact_rows, width), jnp.float32).at[chosen].add(normed_grad)
            )
            grad, gain_part = norm_back(before, attn_scale, local_normed, grad)
            attn_gain_grad = attn_gain_grad + gain_part
        input_grads.append(grad)
        grad_total = (
            tuple(weight_grads)
            if grad_total is None
            else tuple((left + right for left, right in zip(grad_total, weight_grads)))
        )
    grad_total = (
        lax.psum_scatter(
            grad_total[0].astype(jnp.bfloat16), "dp", scatter_dimension=0, tiled=True
        ).astype(jnp.float32),
        lax.psum_scatter(
            grad_total[1].astype(jnp.bfloat16), "dp", scatter_dimension=0, tiled=True
        ).astype(jnp.float32),
        lax.psum_scatter(
            grad_total[2].astype(jnp.bfloat16), "dp", scatter_dimension=0, tiled=True
        ).astype(jnp.float32),
        lax.psum_scatter(
            grad_total[3].astype(jnp.bfloat16), "dp", scatter_dimension=1, tiled=True
        ).astype(jnp.float32),
        lax.psum_scatter(
            grad_total[4].astype(jnp.bfloat16), "dp", scatter_dimension=0, tiled=True
        ).astype(jnp.float32),
        lax.psum_scatter(
            grad_total[5].astype(jnp.bfloat16), "dp", scatter_dimension=0, tiled=True
        ).astype(jnp.float32),
        lax.psum_scatter(
            grad_total[6].astype(jnp.bfloat16), "dp", scatter_dimension=1, tiled=True
        ).astype(jnp.float32),
    )
    gain_sums = (
        lax.psum_scatter(attn_gain_grad, ("dp", "tensor"), scatter_dimension=0, tiled=True),
        lax.psum_scatter(mlp_gain_grad, ("dp", "tensor"), scatter_dimension=0, tiled=True),
    )
    return (jnp.stack(results), jnp.stack(input_grads)) + tuple(grad_total) + tuple(gain_sums)


def solution(mesh):
    in_specs = (
        P(None, ("dp", "tensor"), None),
        P(None, "dp"),
        P(None, "dp", None),
        P(None, ("dp", "tensor"), None),
        P("dp", "tensor"),
        P("dp", "tensor"),
        P("dp", "tensor"),
        P("tensor", "dp"),
        P("dp", "tensor"),
        P("dp", "tensor"),
        P("tensor", "dp"),
        P(("dp", "tensor")),
        P(("dp", "tensor")),
    )
    out_specs = (
        P(None, ("dp", "tensor"), None),
        P(None, ("dp", "tensor"), None),
        P("dp", "tensor"),
        P("dp", "tensor"),
        P("dp", "tensor"),
        P("tensor", "dp"),
        P("dp", "tensor"),
        P("dp", "tensor"),
        P("tensor", "dp"),
        P(("dp", "tensor")),
        P(("dp", "tensor")),
    )
    return jax.shard_map(shards, mesh=mesh, in_specs=in_specs, out_specs=out_specs, check_vma=False)
```

profile of v0, /device:TPU:0, one launch (start us, length us, event | category | flops | bytes accessed | tf_op | source)
XLA Modules:
  0.0 2096.5 jit_solution(3866548439069942979)
XLA Ops:
  26.4 43.9 %all-reduce.15 = (f32[2048]{0:T(1024)}, f32[2048]{0:T(1024)S(1)}) all-reduce(f32[2048]{0:T(1024)S(1)} %dynamic-update-slice, f32[2048]{0:T(1024)S(1)} %dynamic-update-slice.1), channel_id=1, replica_groups=mesh['dp'=8,'tensor'=4] {'dp','tensor'}, use_global_device_ids=true, to_apply=%add.10 | all-reduce | flops 4096 | bytes 32768
  71.2 9.4 all_gather.107
  82.0 31.5 %all_gather.108 = bf16[2048,64]{0,1:T(8,128)(2,1)S(1)} all-gather(bf16[256,64]{0,1:T(8,128)(2,1)S(1)} %copy-done.355), channel_id=1, replica_groups=mesh['dp'=8,'tensor'=4] {'dp'}, dimensions={0}, use_global_device_ids=true | all-gather | bytes 294912 | tf_op jit(solution)/shard_map/all_gather | solution.py:166
  115.4 30.8 %all_gather.109 = bf16[2048,64]{0,1:T(8,128)(2,1)S(1)} all-gather(bf16[256,64]{0,1:T(8,128)(2,1)S(1)} %copy-done.356), channel_id=1, replica_groups=mesh['dp'=8,'tensor'=4] {'dp'}, dimensions={0}, use_global_device_ids=true | all-gather | bytes 294912 | tf_op jit(solution)/shard_map/all_gather | solution.py:165
  149.7 7.6 all_gather.121
  215.8 18.6 reduce-scatter.44.cloned.1.call-done
  237.5 8.6 all_gather.113
  248.3 80.8 %all-gather.10.cloned.1.call-done = bf16[2048,1408]{1,0:T(8,128)(2,1)} async-done(((bf16[256,1408]{1,0:T(8,128)(2,1)}), bf16[2048,1408]{1,0:T(8,128)(2,1)}) %all-gather.10.cloned.1.call-update) | async-done | bytes 5767184 | tf_op jit(solution)/shard_map/all_gather | solution.py:168
  334.3 87.6 %all-gather.12.cloned.1.call-done = bf16[2048,1408]{1,0:T(8,128)(2,1)} async-done(((bf16[256,1408]{1,0:T(8,128)(2,1)}), bf16[2048,1408]{1,0:T(8,128)(2,1)}) %all-gather.12.cloned.1.call-update) | async-done | bytes 5767184 | tf_op jit(solution)/shard_map/all_gather | solution.py:169
  427.6 88.2 %all-gather.14.cloned.1.call-done = bf16[1408,2048]{1,0:T(8,128)(2,1)} async-done(((bf16[1408,256]{1,0:T(8,128)(2,1)}), bf16[1408,2048]{1,0:T(8,128)(2,1)}) %all-gather.14.cloned.1.call-update) | async-done | bytes 5767184 | tf_op jit(solution)/shard_map/all_gather | solution.py:170
  528.7 9.0 all_gather.122
  575.9 6.3 reduce-scatter.46.cloned.1.call-done
  586.6 8.4 all_gather.117
  647.0 8.6 all_gather.118
  676.4 9.2 all_gather.127
  707.2 9.2 all_gather.119
  734.1 9.1 all_gather.123
  771.5 9.2 all_gather.120
  808.5 22.1 %reduce-scatter.56.cloned.1.call-done = bf16[48,2048]{1,0:T(8,128)(2,1)} async-done(((bf16[192,2048]{1,0:T(8,128)(2,1)}), bf16[48,2048]{1,0:T(8,128)(2,1)}) %reduce-scatter.56.cloned.1.call-update) | async-done | bytes 196624 | tf_op jit(solution)/shard_map/reduce_scatter | solution.py:125
  832.7 8.6 all_gather.124
  867.4 18.3 reduce-scatter.50.cloned.1.call-done
  887.8 8.6 all_gather.125
  914.4 8.7 all_gather.133
  925.3 12.8 reduce-scatter.52.cloned.1.call-done
  940.3 8.5 all_gather.126
  970.2 23.1 %reduce-scatter.68.cloned.1.call-done = bf16[48,2048]{1,0:T(8,128)(2,1)} async-done(((bf16[192,2048]{1,0:T(8,128)(2,1)}), bf16[48,2048]{1,0:T(8,128)(2,1)}) %reduce-scatter.68.cloned.1.call-update) | async-done | bytes 196624 | tf_op jit(solution)/shard_map/reduce_scatter | solution.py:125
  997.0 8.7 all_gather.128
  1033.0 9.2 all_gather.134
  1051.2 22.6 %reduce-scatter.42.cloned.1.call-done = bf16[48,2048]{1,0:T(8,128)(2,1)} async-done(((bf16[192,2048]{1,0:T(8,128)(2,1)}), bf16[48,2048]{1,0:T(8,128)(2,1)}) %reduce-scatter.42.cloned.1.call-update) | async-done | bytes 196624 | tf_op jit(solution)/shard_map/reduce_scatter | solution.py:115
  1076.0 8.2 all_gather.129
  1116.4 11.4 reduce-scatter.60.cloned.1.call-done
  1131.3 8.2 all_gather.130
  1168.1 16.1 reduce-scatter.62.cloned.1.call-done
  1186.1 24.6 %reduce-scatter.54.cloned.1.call-done = bf16[48,2048]{1,0:T(8,128)(2,1)} async-done(((bf16[192,2048]{1,0:T(8,128)(2,1)}), bf16[48,2048]{1,0:T(8,128)(2,1)}) %reduce-scatter.54.cloned.1.call-update) | async-done | bytes 196624 | tf_op jit(solution)/shard_map/reduce_scatter | solution.py:115
  1212.9 8.5 all_gather.135
  1245.9 19.7 reduce-scatter.72.cloned.1.call-done
  1268.8 8.2 all_gather.136
  1296.3 8.9 all_gather.131
  1329.7 9.1 all_gather.137
  1340.9 6.0 multiply_convert_fusion.2
  1371.7 12.2 reduce-scatter.76.cloned.1.call-done
  1388.0 8.4 all_gather.138
  1406.1 8.7 all_gather.132
  1463.5 6.0 fusion.449
  1478.9 6.0 fusion.452
  1484.9 6.2 fusion.450
  1491.1 6.1 fusion.453
  1497.2 6.1 fusion.451
  1503.3 21.6 %add_convert_fusion.2 = bf16[2048,1408]{1,0:T(8,128)(2,1)} fusion(f32[2048,1408]{1,0:T(8,128)} %fusion.452, f32[2048,1408]{1,0:T(8,128)} %fusion.453, f32[2048,1408]{1,0:T(8,128)} %fusion.451, f32[2048,1408]{1,0:T(8,128)} %fusion.449, f32[2048,1408]{1,0:T(8,128)} %fusion.450, bf16[192,2048]{1,0:T(8,128)(2,1)S(1)} %copy-done.86, ...), kind=kOutput, calls=%fused_computation.74 | convolution fusion | flops 1124597760 | bytes 64765952 | tf_op jit(solution)/shard_map/ca,cb->ab/dot_general | solution.py:63
  1525.9 6.0 fusion.454
  1531.9 6.0 fusion.457
  1537.9 6.2 fusion.455
  1544.0 6.1 fusion.458
  1550.1 6.1 fusion.456
  1556.2 21.8 %add_convert_fusion.1 = bf16[2048,1408]{1,0:T(8,128)(2,1)} fusion(f32[2048,1408]{1,0:T(8,128)} %fusion.457, f32[2048,1408]{1,0:T(8,128)} %fusion.458, f32[2048,1408]{1,0:T(8,128)} %fusion.456, f32[2048,1408]{1,0:T(8,128)} %fusion.454, f32[2048,1408]{1,0:T(8,128)} %fusion.455, bf16[192,2048]{1,0:T(8,128)(2,1)S(1)} %copy-done.86, ...), kind=kOutput, calls=%fused_computation.73 | convolution fusion | flops 1124597760 | bytes 64765952 | tf_op jit(solution)/shard_map/ca,cb->ab/dot_general | solution.py:63
  1579.1 6.0 fusion.276
  1585.1 6.0 fusion.269
  1593.0 6.0 fusion.155
  1605.0 18.7 add_convert_fusion
  1630.1 39.9 %all-reduce.14 = (f32[2048]{0:T(1024)S(1)}, f32[2048]{0:T(1024)S(1)}) all-reduce(f32[2048]{0:T(1024)S(1)} %add_add_fusion.1, f32[2048]{0:T(1024)S(1)} %add_add_fusion), channel_id=33, replica_groups=mesh['dp'=8,'tensor'=4] {'dp','tensor'}, use_global_device_ids=true, to_apply=%region_143.144.clone | all-reduce | flops 4096 | bytes 32768
  1679.0 68.6 %reduce-scatter.86.cloned.1.call-done = bf16[512,256]{1,0:T(8,128)(2,1)} async-done(((bf16[512,2048]{1,0:T(8,128)(2,1)}), bf16[512,256]{1,0:T(8,128)(2,1)}) %reduce-scatter.86.cloned.1.call-update) | async-done | bytes 262160 | tf_op jit(solution)/shard_map/reduce_scatter | solution.py:333
  1749.4 110.8 %reduce-scatter.88.cloned.1.call-done = bf16[256,1408]{1,0:T(8,128)(2,1)} async-done(((bf16[2048,1408]{1,0:T(8,128)(2,1)}), bf16[256,1408]{1,0:T(8,128)(2,1)}) %reduce-scatter.88.cloned.1.call-update) | async-done | bytes 720912 | tf_op jit(solution)/shard_map/reduce_scatter | solution.py:336
  1862.6 111.1 %reduce-scatter.90.cloned.1.call-done = bf16[256,1408]{1,0:T(8,128)(2,1)} async-done(((bf16[2048,1408]{1,0:T(8,128)(2,1)}), bf16[256,1408]{1,0:T(8,128)(2,1)}) %reduce-scatter.90.cloned.1.call-update) | async-done | bytes 720912 | tf_op jit(solution)/shard_map/reduce_scatter | solution.py:339
  1976.0 111.4 %reduce-scatter.92.cloned.1.call-done = bf16[1408,256]{1,0:T(8,128)(2,1)} async-done(((bf16[1408,2048]{1,0:T(8,128)(2,1)}), bf16[1408,256]{1,0:T(8,128)(2,1)}) %reduce-scatter.92.cloned.1.call-update) | async-done | bytes 720912 | tf_op jit(solution)/shard_map/reduce_scatter | solution.py:342
  (1645 shorter events, 708.0 us)
Async XLA Ops:
  7.2 63.2 %copy-start.22 = (bf16[2,48,2048]{2,1,0:T(8,128)(2,1)S(1)}, bf16[2,48,2048]{2,1,0:T(8,128)(2,1)}, u32[]{:S(2)}) copy-start(bf16[2,48,2048]{2,1,0:T(8,128)(2,1)} %param.13) | copy-start | bytes 1179652
  7.2 160.9 %all-gather.6.cloned.1.call-start = ((), (), s32[]{:S(2)}) async-start(), calls=%async_computation.31 | async-start | bytes 2359296 | tf_op jit(solution)/shard_map/all_gather | solution.py:164
  7.9 74.0 %copy-start.355 = (bf16[256,64]{0,1:T(8,128)(2,1)S(1)}, bf16[256,64]{0,1:T(8,128)(2,1)}, u32[]{:S(2)}) copy-start(bf16[256,64]{0,1:T(8,128)(2,1)} %param.19) | copy-start | bytes 98308
  8.0 168.4 %all-gather.8.cloned.1.call-start = ((), (), s32[]{:S(2)}) async-start(), calls=%async_computation.32 | async-start | bytes 2359296 | tf_op jit(solution)/shard_map/all_gather | solution.py:167
  8.7 207.1 %reduce-scatter.32.cloned.1.call-start = ((), (), s32[]{:S(2)}) async-start(), calls=%async_computation.33 | async-start | bytes 983040 | tf_op jit(solution)/shard_map/reduce_scatter | solution.py:115
  18.4 96.3 %copy-start.43 = (f32[192,64]{1,0:T(8,128)}, f32[192,64]{1,0:T(8,128)S(1)}, u32[]{:S(2)}) copy-start(f32[192,64]{1,0:T(8,128)S(1)} %get-tuple-element.138) | copy-start | bytes 147460
  18.4 127.9 %copy-start.40 = (f32[192,64]{1,0:T(8,128)}, f32[192,64]{1,0:T(8,128)S(1)}, u32[]{:S(2)}) copy-start(f32[192,64]{1,0:T(8,128)S(1)} %get-tuple-element.137) | copy-start | bytes 147460
  70.3 1315.6 %copy-start.132 = (f32[2048]{0:T(1024)}, f32[2048]{0:T(1024)S(1)}, u32[]{:S(2)}) copy-start(f32[2048]{0:T(1024)S(1)} %get-tuple-element.60) | copy-start | bytes 24580
  70.3 44.3 %copy-start.383 = (f32[48]{0:T(128)}, f32[48]{0:T(128)S(1)}, u32[]{:S(2)}) copy-start(f32[48]{0:T(128)S(1)} %get-tuple-element.242) | copy-start | bytes 580
  81.9 75.4 %copy-start.422 = (s32[192]{0:T(256)}, s32[192]{0:T(256)S(1)}, u32[]{:S(2)}) copy-start(s32[192]{0:T(256)S(1)} %get-tuple-element.81) | copy-start | bytes 2308
  81.9 66.1 %copy-start.361 = (s32[1024]{0:T(1024)}, s32[1024]{0:T(1024)S(1)}, u32[]{:S(2)}) copy-start(s32[1024]{0:T(1024)S(1)} %pad_clamp_fusion.5) | copy-start | bytes 12292
  114.6 53.5 %copy-start.13 = (bf16[192,2048]{1,0:T(8,128)(2,1)}, bf16[192,2048]{1,0:T(8,128)(2,1)S(1)}, u32[]{:S(2)}) copy-start(bf16[192,2048]{1,0:T(8,128)(2,1)S(1)} %gather_fusion) | copy-start | bytes 2359300
  115.4 55.1 %copy-start.213 = (f32[192,64]{0,1:T(8,128)}, f32[192,64]{0,1:T(8,128)S(1)}, u32[]{:S(2)}) copy-start(f32[192,64]{0,1:T(8,128)S(1)} %copy.371) | copy-start | bytes 147460
  185.5 48.9 %reduce-scatter.44.cloned.1.call-start = ((), (), s32[]{:S(2)}) async-start(), calls=%async_computation.42 | async-start | bytes 983040 | tf_op jit(solution)/shard_map/reduce_scatter | solution.py:115
  207.3 121.8 %all-gather.10.cloned.1.call-start = ((), (), s32[]{:S(2)}) async-start(), calls=%async_computation.34 | async-start | bytes 6488064 | tf_op jit(solution)/shard_map/all_gather | solution.py:168
  207.9 214.1 %all-gather.12.cloned.1.call-start = ((), (), s32[]{:S(2)}) async-start(), calls=%async_computation.35 | async-start | bytes 6488064 | tf_op jit(solution)/shard_map/all_gather | solution.py:169
  208.5 307.4 %all-gather.14.cloned.1.call-start = ((), (), s32[]{:S(2)}) async-start(), calls=%async_computation.36 | async-start | bytes 6488064 | tf_op jit(solution)/shard_map/all_gather | solution.py:170
  209.2 366.7 %reduce-scatter.34.cloned.1.call-start = ((), (), s32[]{:S(2)}) async-start(), calls=%async_computation.37 | async-start | bytes 983040 | tf_op jit(solution)/shard_map/reduce_scatter | solution.py:115
  248.3 173.7 %copy-start.79 = (bf16[192,2048]{1,0:T(8,128)(2,1)S(1)}, bf16[192,2048]{1,0:T(8,128)(2,1)}, u32[]{:S(2)}) copy-start(bf16[192,2048]{1,0:T(8,128)(2,1)} %gather_fusion.4) | copy-start | bytes 2359300
  334.3 181.5 %copy-start.332 = (f32[192]{0:T(256)S(1)}, f32[192]{0:T(256)}, u32[]{:S(2)}) copy-start(f32[192]{0:T(256)} %get-tuple-element.235) | copy-start | bytes 2308
  528.6 53.5 %reduce-scatter.46.cloned.1.call-start = ((), (), s32[]{:S(2)}) async-start(), calls=%async_computation.43 | async-start | bytes 983040 | tf_op jit(solution)/shard_map/reduce_scatter | solution.py:115
  560.7 84.1 %reduce-scatter.36.cloned.1.call-start = ((), (), s32[]{:S(2)}) async-start(), calls=%async_computation.38 | async-start | bytes 983040 | tf_op jit(solution)/shard_map/reduce_scatter | solution.py:115
  620.9 83.5 %reduce-scatter.38.cloned.1.call-start = ((), (), s32[]{:S(2)}) async-start(), calls=%async_computation.39 | async-start | bytes 983040 | tf_op jit(solution)/shard_map/reduce_scatter | solution.py:115
  676.3 93.0 %reduce-scatter.40.cloned.1.call-start = ((), (), s32[]{:S(2)}) async-start(), calls=%async_computation.40 | async-start | bytes 983040 | tf_op jit(solution)/shard_map/reduce_scatter | solution.py:115
  734.0 72.9 %reduce-scatter.48.cloned.1.call-start = ((), (), s32[]{:S(2)}) async-start(), calls=%async_computation.44 | async-start | bytes 983040 | tf_op jit(solution)/shard_map/reduce_scatter | solution.py:115
  769.2 61.4 %reduce-scatter.56.cloned.1.call-start = ((), (), s32[]{:S(2)}) async-start(), calls=%async_computation.48 | async-start | bytes 983040 | tf_op jit(solution)/shard_map/reduce_scatter | solution.py:125
  806.8 78.8 %reduce-scatter.50.cloned.1.call-start = ((), (), s32[]{:S(2)}) async-start(), calls=%async_computation.45 | async-start | bytes 983040 | tf_op jit(solution)/shard_map/reduce_scatter | solution.py:115
  861.8 76.3 %reduce-scatter.52.cloned.1.call-start = ((), (), s32[]{:S(2)}) async-start(), calls=%async_computation.46 | async-start | bytes 983040 | tf_op jit(solution)/shard_map/reduce_scatter | solution.py:115
  886.9 108.2 %copy-start.61 = (f32[48,2048]{1,0:T(8,128)}, f32[48,2048]{1,0:T(8,128)S(1)}, u32[]{:S(2)}) copy-start(f32[48,2048]{1,0:T(8,128)S(1)} %get-tuple-element.76) | copy-start | bytes 1179652
  914.3 79.0 %reduce-scatter.68.cloned.1.call-start = ((), (), s32[]{:S(2)}) async-start(), calls=%async_computation.54 | async-start | bytes 983040 | tf_op jit(solution)/shard_map/reduce_scatter | solution.py:125
  939.2 55.8 %copy-start.399 = (f32[48]{0:T(128)}, f32[48]{0:T(128)S(1)}, u32[]{:S(2)}) copy-start(f32[48]{0:T(128)S(1)} %add_rsqrt_fusion) | copy-start | bytes 580
  969.5 80.0 %reduce-scatter.58.cloned.1.call-start = ((), (), s32[]{:S(2)}) async-start(), calls=%async_computation.49 | async-start | bytes 983040 | tf_op jit(solution)/shard_map/reduce_scatter | solution.py:125
  1023.9 49.8 %reduce-scatter.42.cloned.1.call-start = ((), (), s32[]{:S(2)}) async-start(), calls=%async_computation.41 | async-start | bytes 983040 | tf_op jit(solution)/shard_map/reduce_scatter | solution.py:115
  1024.8 61.4 %copy-start.429 = (bf16[144]{0:T(256)(128)(2,1)}, bf16[144]{0:T(256)(128)(2,1)S(1)}, u32[]{:S(2)}) copy-start(bf16[144]{0:T(256)(128)(2,1)S(1)} %fusion.392) | copy-start | bytes 868
  1032.9 94.9 %reduce-scatter.60.cloned.1.call-start = ((), (), s32[]{:S(2)}) async-start(), calls=%async_computation.50 | async-start | bytes 983040 | tf_op jit(solution)/shard_map/reduce_scatter | solution.py:125
  1104.0 64.1 %reduce-scatter.70.cloned.1.call-start = ((), (), s32[]{:S(2)}) async-start(), calls=%async_computation.55 | async-start | bytes 983040 | tf_op jit(solution)/shard_map/reduce_scatter | solution.py:125
  1116.4 67.8 %reduce-scatter.62.cloned.1.call-start = ((), (), s32[]{:S(2)}) async-start(), calls=%async_computation.51 | async-start | bytes 983040 | tf_op jit(solution)/shard_map/reduce_scatter | solution.py:125
  1160.4 50.3 %reduce-scatter.54.cloned.1.call-start = ((), (), s32[]{:S(2)}) async-start(), calls=%async_computation.47 | async-start | bytes 983040 | tf_op jit(solution)/shard_map/reduce_scatter | solution.py:115
  1167.3 98.4 %reduce-scatter.72.cloned.1.call-start = ((), (), s32[]{:S(2)}) async-start(), calls=%async_computation.56 | async-start | bytes 983040 | tf_op jit(solution)/shard_map/reduce_scatter | solution.py:125
  1168.0 110.8 %copy-start.433 = (bf16[144]{0:T(256)(128)(2,1)}, bf16[144]{0:T(256)(128)(2,1)S(1)}, u32[]{:S(2)}) copy-start(bf16[144]{0:T(256)(128)(2,1)S(1)} %fusion.396) | copy-start | bytes 868
  1241.8 84.9 %reduce-scatter.74.cloned.1.call-start = ((), (), s32[]{:S(2)}) async-start(), calls=%async_computation.57 | async-start | bytes 983040 | tf_op jit(solution)/shard_map/reduce_scatter | solution.py:125
  1296.3 75.4 %reduce-scatter.64.cloned.1.call-start = ((), (), s32[]{:S(2)}) async-start(), calls=%async_computation.52 | async-start | bytes 983040 | tf_op jit(solution)/shard_map/reduce_scatter | solution.py:125
  1326.7 57.3 %reduce-scatter.76.cloned.1.call-start = ((), (), s32[]{:S(2)}) async-start(), calls=%async_computation.58 | async-start | bytes 983040 | tf_op jit(solution)/shard_map/reduce_scatter | solution.py:125
  1329.7 56.2 %copy-start.119 = (f32[48,2048]{1,0:T(8,128)}, f32[48,2048]{1,0:T(8,128)S(1)}, u32[]{:S(2)}) copy-start(f32[48,2048]{1,0:T(8,128)S(1)} %get-tuple-element.66) | copy-start | bytes 1179652
  1360.1 265.5 %reduce-scatter.82.cloned.1.call-start = ((), (), s32[]{:S(2)}) async-start(), calls=%async_computation.61 | async-start | bytes 294912 | tf_op jit(solution)/shard_map/reduce_scatter | solution.py:327
  1428.8 198.3 %reduce-scatter.84.cloned.1.call-start = ((), (), s32[]{:S(2)}) async-start(), calls=%async_computation.62 | async-start | bytes 294912 | tf_op jit(solution)/shard_map/reduce_scatter | solution.py:330
  1432.0 196.5 %reduce-scatter.78.cloned.1.call-start = ((), (), s32[]{:S(2)}) async-start(), calls=%async_computation.59 | async-start | bytes 983040 | tf_op jit(solution)/shard_map/reduce_scatter | solution.py:125
  1443.9 184.6 %reduce-scatter.66.cloned.1.call-start = ((), (), s32[]{:S(2)}) async-start(), calls=%async_computation.53 | async-start | bytes 983040 | tf_op jit(solution)/shard_map/reduce_scatter | solution.py:125
  1454.6 222.6 %reduce-scatter.80.cloned.1.call-start = ((), (), s32[]{:S(2)}) async-start(), calls=%async_computation.60 | async-start | bytes 2359296 | tf_op jit(solution)/shard_map/reduce_scatter | solution.py:324
  1462.6 285.1 %reduce-scatter.86.cloned.1.call-start = ((), (), s32[]{:S(2)}) async-start(), calls=%async_computation.63 | async-start | bytes 2359296 | tf_op jit(solution)/shard_map/reduce_scatter | solution.py:333
  1477.9 382.3 %reduce-scatter.88.cloned.1.call-start = ((), (), s32[]{:S(2)}) async-start(), calls=%async_computation.64 | async-start | bytes 6488064 | tf_op jit(solution)/shard_map/reduce_scatter | solution.py:336
  1525.0 448.8 %reduce-scatter.90.cloned.1.call-start = ((), (), s32[]{:S(2)}) async-start(), calls=%async_computation.65 | async-start | bytes 6488064 | tf_op jit(solution)/shard_map/reduce_scatter | solution.py:339
  1578.1 509.3 %reduce-scatter.92.cloned.1.call-start = ((), (), s32[]{:S(2)}) async-start(), calls=%async_computation.66 | async-start | bytes 6488064 | tf_op jit(solution)/shard_map/reduce_scatter | solution.py:342
  1623.8 47.3 %copy-start.90 = (bf16[48,2048]{1,0:T(8,128)(2,1)S(1)}, bf16[48,2048]{1,0:T(8,128)(2,1)}, u32[]{:S(2)}) copy-start(bf16[48,2048]{1,0:T(8,128)(2,1)} %reduce-scatter.44.cloned.1.call-done) | copy-start | bytes 589828
  1623.8 47.3 %copy-start.120 = (f32[48,2048]{1,0:T(8,128)S(1)}, f32[48,2048]{1,0:T(8,128)}, u32[]{:S(2)}) copy-start(f32[48,2048]{1,0:T(8,128)} %copy-done.119) | copy-start | bytes 1179652
  1623.8 47.3 %copy-start.133 = (f32[2048]{0:T(1024)S(1)}, f32[2048]{0:T(1024)}, u32[]{:S(2)}) copy-start(f32[2048]{0:T(1024)} %copy-done.132) | copy-start | bytes 24580
  1623.9 47.3 %copy-start.201 = (bf16[48,2048]{1,0:T(8,128)(2,1)S(1)}, bf16[48,2048]{1,0:T(8,128)(2,1)}, u32[]{:S(2)}) copy-start(bf16[48,2048]{1,0:T(8,128)(2,1)} %reduce-scatter.76.cloned.1.call-done) | copy-start | bytes 589828
  1623.9 47.3 %copy-start.382 = (f32[48]{0:T(128)S(1)}, f32[48]{0:T(128)}, u32[]{:S(2)}) copy-start(f32[48]{0:T(128)} %copy-done.380) | copy-start | bytes 580
  1623.9 47.3 %copy-start.439 = (f32[48]{0:T(128)S(1)}, f32[48]{0:T(128)}, u32[]{:S(2)}) copy-start(f32[48]{0:T(128)} %copy-done.438) | copy-start | bytes 580
  1625.5 46.9 %copy-start.88 = (bf16[48,2048]{1,0:T(8,128)(2,1)S(1)}, bf16[48,2048]{1,0:T(8,128)(2,1)}, u32[]{:S(2)}) copy-start(bf16[48,2048]{1,0:T(8,128)(2,1)} %reduce-scatter.32.cloned.1.call-done) | copy-start | bytes 589828
  1625.5 46.9 %copy-start.118 = (f32[48,2048]{1,0:T(8,128)S(1)}, f32[48,2048]{1,0:T(8,128)}, u32[]{:S(2)}) copy-start(f32[48,2048]{1,0:T(8,128)} %get-tuple-element.62) | copy-start | bytes 1179652
  1625.5 46.9 %copy-start.200 = (bf16[48,2048]{1,0:T(8,128)(2,1)S(1)}, bf16[48,2048]{1,0:T(8,128)(2,1)}, u32[]{:S(2)}) copy-start(bf16[48,2048]{1,0:T(8,128)(2,1)} %reduce-scatter.64.cloned.1.call-done) | copy-start | bytes 589828
  1625.5 46.9 %copy-start.379 = (f32[48]{0:T(128)S(1)}, f32[48]{0:T(128)}, u32[]{:S(2)}) copy-start(f32[48]{0:T(128)} %copy-done.377) | copy-start | bytes 580
  1625.5 46.9 %copy-start.437 = (f32[48]{0:T(128)S(1)}, f32[48]{0:T(128)}, u32[]{:S(2)}) copy-start(f32[48]{0:T(128)} %copy-done.436) | copy-start | bytes 580
  (460 other events, 3046.9 us)
Sparse Core Ops, SparseCore 0:
  10.2 52.3 all-gather.5
  64.6 52.1 all-gather.7
  185.6 22.2 reduce-scatter.31
  211.0 23.2 reduce-scatter.43
  236.4 92.6 all-gather.9
  331.1 90.8 all-gather.11
  424.0 91.7 all-gather.13
  528.8 21.4 reduce-scatter.33
  560.8 21.3 reduce-scatter.45
  621.1 23.6 reduce-scatter.35
  676.5 23.6 reduce-scatter.37
  734.1 23.6 reduce-scatter.39
  769.4 23.6 reduce-scatter.47
  806.9 23.6 reduce-scatter.55
  862.0 23.6 reduce-scatter.49
  914.4 23.6 reduce-scatter.51
  969.6 23.6 reduce-scatter.67
  1024.0 23.6 reduce-scatter.57
  1050.4 23.2 reduce-scatter.41
  1104.1 23.6 reduce-scatter.59
  1130.5 23.2 reduce-scatter.69
  1160.5 23.6 reduce-scatter.61
  1187.4 23.2 reduce-scatter.53
  1242.0 23.6 reduce-scatter.71
  1296.4 23.6 reduce-scatter.73
  1326.8 23.7 reduce-scatter.63
  1360.2 23.6 reduce-scatter.75
  1428.9 62.0 reduce-scatter.81
  1494.3 60.6 reduce-scatter.83
  1557.4 22.2 reduce-scatter.77
  1582.4 23.2 reduce-scatter.65
  1609.2 67.9 reduce-scatter.79
  1680.6 67.0 reduce-scatter.85
  1751.3 108.9 reduce-scatter.87
  1863.9 109.7 reduce-scatter.89
  1977.2 110.1 reduce-scatter.91
where the time goes:
time: 2110 us; the launch traced here: 2100 us
  waiting for transfers between devices  875 us (41%)
  matrix products  403 us (19%)
  blocking collectives  355 us (17%)
  other arithmetic  282 us (13%)
  local copies, waits for them, and re-layouts  158 us (7%)
    dot_general x42, matrix products, left_times(): jnp.einsum('ca,cb->ab', left, right, preferred_element_type=jnp.float32)  175 us
    reduce_scatter x1, waiting for transfers between devices, shards(): lax.psum_scatter(grad_total[6].astype(jnp.bfloat16), 'dp', scatter_dimens...  111 us
    reduce_scatter x1, waiting for transfers between devices, shards(): lax.psum_scatter(grad_total[5].astype(jnp.bfloat16), 'dp', scatter_dimens...  111 us
    reduce_scatter x1, waiting for transfers between devices, shards(): lax.psum_scatter(grad_total[4].astype(jnp.bfloat16), 'dp', scatter_dimens...  111 us
    dot_general x42, matrix products, matmul(): return jnp.dot(left, right, preferred_element_type=jnp.float32)  105 us
    all_gather x12, blocking collectives, spread_rows(): return lax.all_gather(values, 'tensor', axis=0, tiled=True)  105 us
    reduce_scatter x12, waiting for transfers between devices, collect_rows(): lax.psum_scatter(values.astype(jnp.bfloat16), 'tensor', scatter_dimension...  105 us
    reduce_scatter x12, waiting for transfers between devices, collect_grads(): lax.psum_scatter(values.astype(jnp.bfloat16), 'tensor', scatter_dimension...  105 us
  transfers between devices with their start and end apart: 36, of which 21 were waited for; matrix products, arithmetic and copies ran while one was open for 26% of the time, Pallas kernels for 0%

commit v1 on v0

v1 whole, which is shorter than its diff:
```python
import functools

import jax
import jax.numpy as jnp
import numpy as np
from jax import lax
from jax.experimental import pallas as pl
from jax.experimental.pallas import tpu as pltpu
from jax.sharding import PartitionSpec as P

HQ = 32
KVH = 4
HS = 64
MB = 2
RECUR = 3
SCALE = HS ** (-0.5)
F32 = jnp.float32
BF = jnp.bfloat16
MESH = pl.DeviceIdType.MESH
NN = (((1,), (0,)), ((), ()))
NT = (((1,), (1,)), ((), ()))
TN = (((0,), (0,)), ((), ()))

OWN = (96, 80, 48)
PIECES = ((0, 24, 0), (24, 24, 1), (48, 16, 0), (64, 16, 1), (80, 8, 0), (88, 8, 1))
T = 4
DC = 512
OC = 256
HEADS = 4


def own_table():
    batch, place, seen = [], [], [0, 0]
    for _, rows, b in PIECES:
        for _ in range(rows):
            batch.append(b)
            place.append(seen[b])
            seen[b] += 1
    return np.array(batch), np.array(place)


def split_batches(values, own):
    halves = ([], [])
    for owner in range(T):
        for start, rows, b in PIECES:
            if start < own:
                halves[b].append(values[owner * own + start : owner * own + start + rows])
    return [jnp.concatenate(half, axis=0) for half in halves]


def join_batches(halves, own):
    rows_out, at = [], [0, 0]
    for owner in range(T):
        for start, rows, b in PIECES:
            if start < own:
                rows_out.append(halves[b][at[b] : at[b] + rows])
                at[b] += rows
    return jnp.concatenate(rows_out, axis=0)


def dot(left, right, dims):
    return lax.dot_general(left, right, dims, preferred_element_type=F32)


def swap_halves(tile):
    lane = lax.broadcasted_iota(jnp.int32, tile.shape, 1)
    return jnp.where((lane & 63) < 32, pltpu.roll(tile, 96, 1), pltpu.roll(tile, 32, 1))


def attention_shares(query, key, allowed):
    rows = query.shape[0]
    group = query.shape[1] // HS
    stacked = stack_heads(query)
    scores = dot(stacked, key, NT).reshape(group, rows, rows) * SCALE
    scores = jnp.where(allowed[None] > 0, scores, -1e30)
    raised = jnp.exp(scores - jnp.max(scores, axis=-1, keepdims=True))
    return stacked, raised * (1.0 / jnp.sum(raised, axis=-1, keepdims=True))


def stack_heads(values):
    group = values.shape[1] // HS
    return jnp.concatenate([values[:, h * HS : (h + 1) * HS] for h in range(group)], axis=0)


def unstack_heads(values, rows):
    group = values.shape[0] // rows
    return jnp.concatenate([values[h * rows : (h + 1) * rows] for h in range(group)], axis=1)


def mean_square(values):
    return jnp.mean(values * values, axis=-1, keepdims=True)


class Place:
    def __init__(self, n):
        self.n = n
        self.line = n // 2
        self.dp = lax.axis_index("dp")
        self.t = lax.axis_index("tensor")
        self.a = self.dp // 2
        self.b = lax.rem(self.dp, 2)
        self.hi = self.t // 2
        self.lo = lax.rem(self.t, 2)
        self.has_right = self.a < self.line - 1
        self.has_left = self.a > 0
        self.mate = (self.a * 2 + 1 - self.b, self.t)
        self.right = (jnp.minimum(self.dp + 2, n - 1), self.t)
        self.left = (jnp.maximum(self.dp - 2, 0), self.t)
        self.near = (self.dp, self.hi * 2 + 1 - self.lo)
        self.far = (self.dp, (1 - self.hi) * 2 + self.lo)
        self.diag = (self.dp, (1 - self.hi) * 2 + 1 - self.lo)

    def barrier(self, along):
        sem = pltpu.get_barrier_semaphore()

        def greet(device):
            pl.semaphore_signal(sem, inc=1, device_id=device, device_id_type=MESH)

        for device in (self.near, self.far, self.diag):
            greet(device)
        expected = 3
        if along:
            greet(self.mate)
            pl.when(self.has_right)(lambda: greet(self.right))
            pl.when(self.has_left)(lambda: greet(self.left))
            expected = 4 + self.has_right.astype(jnp.int32) + self.has_left.astype(jnp.int32)
        pl.semaphore_wait(sem, expected)


def remote(src, dst, send, recv, device):
    return pltpu.make_async_remote_copy(
        src_ref=src, dst_ref=dst, send_sem=send, recv_sem=recv, device_id=device, device_id_type=MESH
    )


class LineGather:
    def __init__(self, place, pieces, sems):
        self.p = place
        self.pieces = pieces
        self.local, self.msend, self.mrecv, self.rsend, self.rrecv, self.lsend, self.lrecv = sems

    def toward_left(self, w, k, src, chunk):
        dst = self.pieces[w][1](chunk)
        return remote(src, dst, self.lsend.at[w, k], self.lrecv.at[w, k], self.p.left)

    def toward_right(self, w, k, src, chunk):
        dst = self.pieces[w][1](chunk)
        return remote(src, dst, self.rsend.at[w, k], self.rrecv.at[w, k], self.p.right)

    def toward_mate(self, w, k, src, chunk):
        dst = self.pieces[w][1](chunk)
        return remote(src, dst, self.msend.at[w, k], self.mrecv.at[w, k], self.p.mate)

    def own(self, w):
        p = self.p
        src, dst = self.pieces[w]
        pltpu.make_async_copy(src, dst(p.dp), self.local.at[w]).start()
        pl.when(p.has_left)(lambda: self.toward_left(w, 0, src, p.dp).start())
        pl.when(p.has_right)(lambda: self.toward_right(w, 0, src, p.dp).start())
        self.toward_mate(w, p.a, src, p.dp).start()

    def step(self, w, k):
        p = self.p
        dst = self.pieces[w][1]

        @pl.when(p.a + k < p.line)
        def _():
            chunk = p.dp + 2 * k
            self.toward_left(w, k - 1, dst(chunk), chunk).wait_recv()
            pl.when(p.has_left)(lambda: self.toward_left(w, k, dst(chunk), chunk).start())
            self.toward_mate(w, p.a + k, dst(chunk), chunk).start()

        @pl.when(p.a - k >= 0)
        def _():
            chunk = p.dp - 2 * k
            self.toward_right(w, k - 1, dst(chunk), chunk).wait_recv()
            pl.when(p.has_right)(lambda: self.toward_right(w, k, dst(chunk), chunk).start())
            self.toward_mate(w, p.a - k, dst(chunk), chunk).start()

    def steps(self, w):
        for k in range(1, self.p.line):
            self.step(w, k)

    def arrive(self, w):
        p = self.p
        src, dst = self.pieces[w]
        pltpu.make_async_copy(src, dst(p.dp), self.local.at[w]).wait()
        for i in range(p.line):
            chunk = 2 * i + 1 - p.b
            self.toward_mate(w, i, dst(chunk), chunk).wait_recv()

    def drain(self, w):
        p = self.p
        dst = self.pieces[w][1]
        for i in range(p.line):
            self.toward_mate(w, i, dst(p.dp), p.dp).wait_send()
            pl.when(p.has_left & (p.a + i < p.line))(lambda: self.toward_left(w, i, dst(p.dp), p.dp).wait_send())
            pl.when(p.has_right & (p.a - i >= 0))(lambda: self.toward_right(w, i, dst(p.dp), p.dp).wait_send())


class Rows:
    def __init__(self, place, part, relay, sums, sems):
        self.p = place
        self.part, self.relay, self.sums = part, relay, sums
        self.s1, self.q1, self.s2, self.q2, self.gs, self.gr = sems

    def first_copy(self, i, own, c):
        p = self.p
        cols = pl.ds(pl.multiple_of(c * DC, DC), DC)
        return remote(
            self.part.at[:, 1 - p.lo, pl.ds(0, own), cols],
            self.sums[i][0].at[:, :, cols],
            self.s1.at[i, c],
            self.q1.at[i, c],
            p.near,
        )

    def second_copy(self, i, own, c):
        p = self.p
        cols = pl.ds(pl.multiple_of(c * DC, DC), DC)
        return remote(
            self.relay.at[pl.ds(0, own), cols],
            self.sums[i][1].at[:, cols],
            self.s2.at[i, c],
            self.q2.at[i, c],
            p.far,
        )

    def reduce(self, i, own, tile, finish):
        p = self.p
        part, relay = self.part, self.relay
        r1, r2 = self.sums[i]
        chunks = part.shape[-1] // DC

        @pl.loop(0, chunks)
        def _(c):
            cols = pl.ds(pl.multiple_of(c * DC, DC), DC)
            part[:, :, 0:own, cols] = tile(cols).astype(BF).reshape(2, 2, own, DC)
            self.first_copy(i, own, c).start()

        @pl.loop(0, chunks)
        def _(c):
            cols = pl.ds(pl.multiple_of(c * DC, DC), DC)
            self.first_copy(i, own, c).wait_recv()
            mine = part[1 - p.hi, p.lo, 0:own, cols].astype(F32)
            relay[0:own, cols] = (mine + r1[1 - p.hi, :, cols].astype(F32)).astype(BF)
            self.second_copy(i, own, c).start()

        @pl.loop(0, chunks)
        def _(c):
            cols = pl.ds(pl.multiple_of(c * DC, DC), DC)
            self.second_copy(i, own, c).wait_recv()
            mine = part[p.hi, p.lo, 0:own, cols].astype(F32)
            finish(cols, mine + r1[p.hi, :, cols].astype(F32) + r2[:, cols].astype(F32))

        @pl.loop(0, chunks)
        def _(c):
            self.first_copy(i, own, c).wait_send()
            self.second_copy(i, own, c).wait_send()

    def gather_copy(self, i, buffer, which):
        p = self.p
        here = buffer.at[p.hi, p.lo]
        if which == 0:
            return remote(here, here, self.gs.at[i, 0], self.gr.at[i, 0], p.far)
        if which == 1:
            return remote(here, here, self.gs.at[i, 1], self.gr.at[i, 1], p.near)
        there = buffer.at[1 - p.hi, p.lo]
        return remote(there, there, self.gs.at[i, 2], self.gr.at[i, 2], p.near)

    def gather_start(self, i, buffer):
        self.gather_copy(i, buffer, 0).start()
        self.gather_copy(i, buffer, 1).start()

    def gather_finish(self, i, buffer):
        self.gather_copy(i, buffer, 0).wait_recv()
        self.gather_copy(i, buffer, 2).start()
        self.gather_copy(i, buffer, 1).wait_recv()
        self.gather_copy(i, buffer, 2).wait_recv()
        for which in range(3):
            self.gather_copy(i, buffer, which).wait_send()


def peers_copy(place, src, dst, send, recv, which):
    device = (place.near, place.far, place.diag)[which]
    return remote(src, dst.at[place.t], send.at[which], recv.at[which], device)


def gain_row(gathered, n, row, width):
    each = width // (n * T)
    tiles = []
    for j in range(width // 128):
        total = None
        for i in range(128 // each):
            number = j * (128 // each) + i
            block = gathered[number % T, number // T][row : row + 1]
            total = block if total is None else total + block
        tiles.append(total)
    return jnp.concatenate(tiles, axis=1)


QKV, WO, GU, WD = 0, 640, 1152, 3968
COLS = 5376
RANGES = ((0, 640), (640, 512), (1152, 1536), (2688, 1280), (3968, 768), (4736, 640))


def forward_kernel(n, *refs):
    it = iter(refs)
    (tokens, cotangent, weights, gains, perm, cosine, sine) = [next(it) for _ in range(7)]
    allowed = [next(it) for _ in range(RECUR)]
    act_own = next(it)
    w_out, gain_out, fin_out, cot_own, cot_all = [next(it) for _ in range(5)]
    names = ("normed", "qkv", "att", "mixed", "gu", "prod", "hidden", "first")
    saved_out = [dict((k, next(it)) for k in names) for _ in range(RECUR)]
    w = next(it)
    gbuf, gall = next(it), next(it)
    tok, cot = next(it), next(it)
    saved = [dict((k, next(it)) for k in names) for _ in range(RECUR)]
    after, fin, cown = next(it), next(it), next(it)
    part, relay = next(it), next(it)
    sums = [(next(it), next(it)) for _ in range(2 * RECUR)]
    line_sems = [next(it) for _ in range(7)]
    row_sems = [next(it) for _ in range(6)]
    tsend, trecv, outsem = next(it), next(it), next(it)

    p = Place(n)
    rows_chunk = weights.shape[0]
    width = tokens.shape[-1]

    def piece(start, size):
        return (
            weights.at[:, pl.ds(start, size)],
            lambda chunk: w.at[pl.ds(pl.multiple_of(chunk * rows_chunk, rows_chunk), rows_chunk), pl.ds(start, size)],
        )

    pieces = [(gains, lambda chunk: gbuf.at[chunk])] + [piece(*r) for r in RANGES]
    line = LineGather(p, pieces, line_sems)
    rows = Rows(p, part, relay, sums, row_sems)
    writes = []

    def write(src, dst):
        copy = pltpu.make_async_copy(src, dst, outsem.at[len(writes)])
        copy.start()
        writes.append(copy)

    p.barrier(True)
    line.own(0)
    line.own(1)
    own_copies = []
    for which in range(3):
        peers_copy(p, tokens, tok, tsend.at[0], trecv.at[0], which).start()
    pltpu.make_async_copy(tokens, tok.at[p.t], tsend.at[0, 3]).start()
    line.own(2)
    for which in range(3):
        peers_copy(p, cotangent, cot, tsend.at[1], trecv.at[1], which).start()
    pltpu.make_async_copy(cotangent, cot.at[p.t], tsend.at[1, 3]).start()
    line.own(3)
    line.steps(0)
    line.arrive(0)
    for which in range(3):
        peers_copy(p, gbuf, gall, tsend.at[2], trecv.at[2], which).start()
    pltpu.make_async_copy(gbuf, gall.at[p.t], tsend.at[2, 3]).start()

    def wait_peers(i, src, dst):
        for which in range(3):
            copy = peers_copy(p, src, dst, tsend.at[i], trecv.at[i], which)
            copy.wait_recv()
            copy.wait_send()
        pltpu.make_async_copy(src, dst.at[p.t], tsend.at[i, 3]).wait()

    wait_peers(2, gbuf, gall)
    gain_out[0:1, :] = gain_row(gall, n, 0, width)
    gain_out[1:2, :] = gain_row(gall, n, 1, width)
    gain_out[2:8, :] = jnp.zeros((6, width), F32)

    wait_peers(0, tokens, tok)

    own = OWN[0]
    mine = perm[pl.ds(pl.multiple_of(p.t * own, own), own), :]
    saved[0]["hidden"][...] = dot(mine, tok[...].reshape(T * own, width), NN)

    @pl.loop(0, T)
    def _(owner):
        picked = perm[pl.ds(pl.multiple_of(owner * own, own), own), :]
        hidden = dot(picked, tok[...].reshape(T * own, width), NN)
        inverse = lax.rsqrt(mean_square(hidden) + 1e-05)
        saved[0]["normed"][owner] = (hidden * inverse * gain_out[0:1, :]).astype(BF)

    wait_peers(1, cotangent, cot)
    cown[...] = dot(mine, cot[...].reshape(T * own, width), NN)
    write(cown, cot_own)

    line.steps(1)
    line.own(4)
    line.steps(2)
    line.arrive(1)

    for level in range(RECUR):
        own = OWN[level]
        count = T * own
        half = count // 2
        s = saved[level]
        if level:
            rows.gather_finish(2 * level - 1, s["normed"].reshape(2, 2, own, width))
        x = s["normed"][...].reshape(count, width)
        qkv = dot(x, w[:, QKV : QKV + 640], NN)
        cos = jnp.concatenate([cosine[owner * OWN[0] : owner * OWN[0] + own, :] for owner in range(T)], axis=0)
        sin = jnp.concatenate([sine[owner * OWN[0] : owner * OWN[0] + own, :] for owner in range(T)], axis=0)
        tiles = []
        for j in range(5):
            tile = qkv[:, j * 128 : (j + 1) * 128]
            turned = tile * cos + swap_halves(tile) * sin
            if j == 4:
                lane = lax.broadcasted_iota(jnp.int32, tile.shape, 1)
                turned = jnp.where(lane < HS, turned, tile)
            tiles.append(turned)
        rotated = jnp.concatenate(tiles, axis=1)
        s["qkv"][...] = rotated.astype(BF)
        write(s["qkv"], saved_out[level]["qkv"])
        heads = []
        for b, block in enumerate(split_batches(rotated, own)):
            query, key, value = (
                block[:, 0:512].astype(BF),
                block[:, 512:576].astype(BF),
                block[:, 576:640].astype(BF),
            )
            _, shares = attention_shares(query, key, allowed[level][b])
            out = dot(shares.astype(BF).reshape(8 * half, half), value, NN)
            heads.append(unstack_heads(out, half))
        s["att"][...] = join_batches(heads, own).astype(BF)
        write(s["att"], saved_out[level]["att"])
        if level == 0:
            line.own(5)
            line.steps(3)
            line.arrive(2)
        present = act_own[level, 0:own, :]

        def attention_tile(cols):
            return dot(s["att"][...], w[cols, WO : WO + 512], NT)

        def attention_finish(cols, total):
            s["first"][:, cols] = s["hidden"][:, cols] + present * total

        rows.reduce(2 * level, own, attention_tile, attention_finish)
        first = s["first"][...]
        inverse = lax.rsqrt(mean_square(first) + 1e-05)
        s["mixed"][p.t] = (first * inverse * gain_out[1:2, :]).astype(BF)
        mixed = s["mixed"].reshape(2, 2, own, width)
        rows.gather_start(2 * level, mixed)
        write(s["first"], saved_out[level]["first"])
        if level == 0:
            line.own(6)
            line.steps(4)
            line.arrive(3)
        rows.gather_finish(2 * level, mixed)
        write(s["mixed"], saved_out[level]["mixed"])

        def gate_up(start, stop):
            @pl.loop(start, stop)
            def _(j):
                cols = pl.ds(pl.multiple_of(j * 256, 256), 256)
                wcols = pl.ds(pl.multiple_of(GU + j * 256, 128), 256)
                pair = dot(s["mixed"][...].reshape(count, width), w[:, wcols], NN)
                s["gu"][:, cols] = pair.astype(BF)
                gate = pair[:, 0:128]
                s["prod"][:, pl.ds(pl.multiple_of(j * 128, 128), 128)] = (
                    gate * jax.nn.sigmoid(gate) * pair[:, 128:256]
                ).astype(BF)

        gate_up(0, 6)
        if level == 0:
            line.steps(5)
            line.arrive(4)
        gate_up(6, 11)
        write(s["gu"], saved_out[level]["gu"])
        write(s["prod"], saved_out[level]["prod"])
        if level == 0:
            line.steps(6)
            line.arrive(5)
            line.arrive(6)
            write(w, w_out)

        def mlp_tile(cols):
            return dot(s["prod"][...], w[cols, WD : WD + 1408], NT)

        def mlp_finish(cols, total):
            after[0:own, cols] = s["first"][:, cols] + present * total

        rows.reduce(2 * level + 1, own, mlp_tile, mlp_finish)
        if level < RECUR - 1:
            deeper = OWN[level + 1]
            hidden = after[0:deeper, :]
            saved[level + 1]["hidden"][...] = hidden
            inverse = lax.rsqrt(mean_square(hidden) + 1e-05)
            saved[level + 1]["normed"][p.t] = (hidden * inverse * gain_out[0:1, :]).astype(BF)
            rows.gather_start(2 * level + 1, saved[level + 1]["normed"].reshape(2, 2, deeper, width))
            fin[deeper:own, :] = after[deeper:own, :].astype(BF)
        else:
            fin[0:own, :] = after[0:own, :].astype(BF)
        write(s["hidden"], saved_out[level]["hidden"])
        write(s["normed"], saved_out[level]["normed"])
        if level == 0:
            deepest = OWN[RECUR - 1]

            @pl.loop(0, T)
            def _(owner):
                picked = perm[pl.ds(pl.multiple_of(owner * OWN[0], 32), deepest), :]
                cot_all[owner] = dot(picked, cot[...].reshape(T * OWN[0], width), NN).astype(BF)

    write(fin, fin_out)
    for i in range(len(pieces)):
        line.drain(i)
    for copy in writes:
        copy.wait()


def static_tables():
    batch, place = own_table()
    batch_q = np.tile(batch, T)
    rank_q = np.concatenate([place * T + t for t in range(T)])
    level_ranks = []
    for own in OWN:
        level_ranks.append(np.concatenate([np.arange(own // 2) * T + t for t in range(T)]))
    return batch_q.astype(np.int32), rank_q.astype(np.int32), [r.astype(np.int32) for r in level_ranks]


def prologue(depth, lengths, tensor_index):
    batch_q, rank_q, level_ranks = static_tables()
    rows = depth.shape[1]
    local = rows // T
    index = jnp.arange(rows, dtype=jnp.int32)
    earlier = (depth[:, None, :] > depth[:, :, None]) | (
        (depth[:, None, :] == depth[:, :, None]) & (index[None, None, :] < index[None, :, None])
    )
    rank = jnp.sum(earlier.astype(jnp.int32), axis=2)
    rank_col = rank.reshape(MB, T, local).transpose(1, 0, 2).reshape(-1)
    batch_col = np.tile(np.repeat(np.arange(MB), local), T).astype(np.int32)
    hit = (rank_col[None, :] == rank_q[:, None]) & (batch_col[None, :] == batch_q[:, None])
    perm = hit.astype(BF)
    back = (
        (rank_col[:, None] == rank_q[None, :]) & (batch_col[:, None] == batch_q[None, :])
    ).astype(BF)
    ends = jnp.cumsum(lengths, axis=1)
    starts = ends - lengths

    def documents(position, ends_of, starts_of):
        inside = position[..., None] >= ends_of
        document = jnp.sum(inside.astype(jnp.int32), axis=-1)
        start = jnp.max(jnp.where(position[..., None] >= starts_of, starts_of, 0), axis=-1)
        return document, position - start

    position_col = np.tile(np.arange(rows).reshape(T, 1, local), (1, MB, 1)).reshape(-1).astype(np.int32)
    position = jnp.sum(jnp.where(hit, position_col[None, :], 0), axis=1)
    ends_q = jnp.where(batch_q[:, None] == 0, ends[0][None], ends[1][None])
    starts_q = jnp.where(batch_q[:, None] == 0, starts[0][None], starts[1][None])
    _, offset = documents(position, ends_q, starts_q)
    freqs = 10000.0 ** (-jnp.arange(0, HS, 2).astype(F32) / HS)
    angles = offset.astype(F32)[:, None] * freqs[None, :]
    cos, sin = jnp.cos(angles), jnp.sin(angles)
    cosine = jnp.concatenate([cos] * 4, axis=1)
    sine = jnp.concatenate([-sin, sin, -sin, sin], axis=1)
    counts = [jnp.sum((depth >= level + 1).astype(jnp.int32), axis=1) for level in range(RECUR)]
    masks, act = [], []
    for level in range(RECUR):
        ranks = level_ranks[level]
        at = jnp.sum(jnp.where(rank[:, None, :] == ranks[None, :, None], index[None, None, :], 0), axis=2)
        document, _ = documents(at, ends[:, None, :], starts[:, None, :])
        ok = (document[:, :, None] == document[:, None, :]) & (at[:, None, :] <= at[:, :, None])
        ok = ok & (ranks[None, None, :] < counts[level][:, None, None])
        ok = ok | np.eye(len(ranks), dtype=bool)[None]
        masks.append(ok.astype(F32))
        limit = jnp.where(batch_q == 0, counts[level][0], counts[level][1])
        act.append((rank_q < limit).astype(F32))
    act = jnp.stack(act)
    return perm, back, cosine, sine, masks, act


def forward(n, tokens, cotangent, joined, gains, tables, tensor_index):
    perm, back, cosine, sine, masks, act = tables
    width = tokens.shape[-1]
    act_own = lax.dynamic_slice_in_dim(act, tensor_index * OWN[0], OWN[0], axis=1)[:, :, None]
    hidden_cols = (COLS - GU) // 3
    vmem = pl.BlockSpec(memory_space=pltpu.VMEM)
    hbm = pl.BlockSpec(memory_space=pl.ANY)

    def saved_shapes(own):
        count = T * own
        return {
            "normed": ((T, own, width), BF),
            "qkv": ((count, 640), BF),
            "att": ((count, 512), BF),
            "mixed": ((T, own, width), BF),
            "gu": ((count, 2 * hidden_cols), BF),
            "prod": ((count, hidden_cols), BF),
            "hidden": ((own, width), F32),
            "first": ((own, width), F32),
        }

    shapes = [((width, COLS), BF), ((8, width), F32), ((OWN[0], width), BF), ((OWN[0], width), F32), ((T, OWN[2], width), BF)]
    specs = [hbm, vmem, hbm, hbm, vmem]
    for own in OWN:
        for entry in saved_shapes(own).values():
            shapes.append(entry)
            specs.append(hbm)
    scratch = [pltpu.VMEM((width, COLS), BF), pltpu.VMEM((n, 8, 128), F32), pltpu.VMEM((T, n, 8, 128), F32)]
    scratch += [pltpu.VMEM((T,) + tokens.shape, BF)] * 2
    for own in OWN:
        scratch += [pltpu.VMEM(*entry) for entry in saved_shapes(own).values()]
    scratch += [pltpu.VMEM((OWN[0], width), F32), pltpu.VMEM((OWN[0], width), BF), pltpu.VMEM((OWN[0], width), F32)]
    scratch += [pltpu.VMEM((2, 2, OWN[0], width), BF), pltpu.VMEM((OWN[0], width), BF)]
    for own in OWN:
        for _ in range(2):
            scratch += [pltpu.VMEM((2, own, width), BF), pltpu.VMEM((own, width), BF)]
    dma = pltpu.SemaphoreType.DMA
    count = len(RANGES) + 1
    scratch += [dma((count,))] + [dma((count, n // 2))] * 6
    chunks = width // DC
    scratch += [dma((2 * RECUR, chunks))] * 4 + [dma((2 * RECUR, 3))] * 2
    scratch += [dma((3, 4)), dma((3, 3)), dma((40,))]
    outs = pl.pallas_call(
        functools.partial(forward_kernel, n),
        out_shape=[jax.ShapeDtypeStruct(*entry) for entry in shapes],
        in_specs=[hbm, hbm, hbm, hbm] + [vmem] * 7,
        out_specs=specs,
        scratch_shapes=scratch,
        compiler_params=pltpu.CompilerParams(
            collective_id=1, has_side_effects=True, vmem_limit_bytes=62 << 20
        ),
    )(tokens, cotangent, joined, gains, perm, cosine, sine, *masks, act_own)
    w_all, gain, fin, cot_own, cot_all = outs[:5]
    names = list(saved_shapes(1))
    saved = [dict(zip(names, outs[5 + 8 * level : 13 + 8 * level])) for level in range(RECUR)]
    return w_all, gain, fin, cot_own, cot_all, saved


def join_weights(w_query, w_key, w_value, w_out, w_gate, w_up, w_down):
    rows, hidden = w_gate.shape
    pair = jnp.stack(
        [w_gate.reshape(rows, hidden // 128, 128), w_up.reshape(rows, hidden // 128, 128)], axis=2
    ).reshape(rows, 2 * hidden)
    return jnp.concatenate([w_query, w_key, w_value, w_out.T, pair, w_down.T], axis=1)


def place_gains(n, attn_gain, mlp_gain):
    each = attn_gain.shape[0]
    number = lax.axis_index("dp") * T + lax.axis_index("tensor")
    block = jnp.zeros((8, 128), F32)
    both = jnp.stack([attn_gain, mlp_gain])
    return lax.dynamic_update_slice(block, both, (0, lax.rem(number * each, 128)))


def attention_back(rotated, attended_grad, cos, sin, allowed, own):
    half = T * own // 2
    grads = []
    split = split_batches(rotated, own)
    upstream = split_batches(attended_grad, own)
    for b in range(MB):
        block = split[b]
        query, key, value = block[:, 0:512].astype(BF), block[:, 512:576].astype(BF), block[:, 576:640].astype(BF)
        up_all = upstream[b].astype(BF)
        query_grads, key_grad, value_grad = [], 0.0, 0.0
        for start in range(0, 512, HEADS * HS):
            stacked, shares = attention_shares(query[:, start : start + HEADS * HS], key, allowed[b])
            up = stack_heads(up_all[:, start : start + HEADS * HS])
            low = shares.astype(BF).reshape(HEADS * half, half)
            shares_grad = dot(up, value, NT).reshape(HEADS, half, half)
            value_grad += dot(low, up, TN)
            spread = jnp.sum(shares * shares_grad, axis=-1, keepdims=True)
            score_grad = (shares * (shares_grad - spread)).astype(BF).reshape(HEADS * half, half)
            query_grads.append(unstack_heads(dot(score_grad, key, NN), half) * SCALE)
            key_grad += dot(score_grad, stacked, TN) * SCALE
        query_grad = jnp.concatenate(query_grads, axis=1)
        grads.append(jnp.concatenate([query_grad, key_grad, value_grad], axis=1))
    joined = join_batches(grads, own)
    tiles = []
    for j in range(5):
        tile = joined[:, j * 128 : (j + 1) * 128]
        turned = tile * cos - swap_halves(tile) * sin
        if j == 4:
            lane = lax.broadcasted_iota(jnp.int32, tile.shape, 1)
            turned = jnp.where(lane < HS, turned, tile)
        tiles.append(turned)
    return jnp.concatenate(tiles, axis=1)


def level_rows(table, own):
    return jnp.concatenate([table[owner * OWN[0] : owner * OWN[0] + own, :] for owner in range(T)], axis=0)


def norm_back(source, gain, upstream):
    inverse = lax.rsqrt(mean_square(source) + 1e-05)
    unit = source * inverse
    gain_part = jnp.sum(upstream * unit, axis=0, keepdims=True)
    scaled = upstream * gain
    return inverse * (scaled - unit * jnp.mean(scaled * unit, axis=-1, keepdims=True)), gain_part


def backward_kernel(n, *refs):
    it = iter(refs)
    (w_all, gain, cot_own, cot_all, cosine, sine, act_own, act_last) = [next(it) for _ in range(8)]
    allowed = [None] + [next(it) for _ in range(2)]
    saved_in = []
    for level in range(RECUR):
        names = ("gu", "first") if level == 0 else ("gu", "first", "qkv", "hidden")
        saved_in.append({k: next(it) for k in names})
    dg_out = [next(it) for _ in range(3)]
    gug_out = [next(it) for _ in range(3)]
    og_out = [None] + [next(it) for _ in range(2)]
    qkvg_out = [None] + [next(it) for _ in range(2)]
    grad_out, gain_part = next(it), next(it)
    w = next(it)
    saved = []
    for level in range(RECUR):
        saved.append({k: next(it) for k in saved_in[level]})
    dg = [next(it) for _ in range(3)]
    gug = [next(it) for _ in range(3)]
    og = [None] + [next(it) for _ in range(2)]
    qkvg = [None] + [next(it) for _ in range(2)]
    grad, upstream = next(it), next(it)
    part, relay = next(it), next(it)
    sums = [(next(it), next(it)) for _ in range(5)]
    row_sems = [next(it) for _ in range(6)]
    insem, outsem = next(it), next(it)

    p = Place(n)
    width = w.shape[0]
    rows = Rows(p, part, relay, sums, row_sems)
    hidden_cols = (COLS - GU) // 3
    loads, writes = {}, []

    def load(name, src, dst):
        copy = pltpu.make_async_copy(src, dst, insem.at[len(loads)])
        copy.start()
        loads[name] = copy

    def write(src, dst):
        copy = pltpu.make_async_copy(src, dst, outsem.at[len(writes)])
        copy.start()
        writes.append(copy)

    def columns(start, size):
        load(("w", start), w_all.at[:, pl.ds(start, size)], w.at[:, pl.ds(start, size)])

    columns(WD, hidden_cols)
    load("grad", cot_own, grad)
    last = RECUR - 1
    load(("gu", last), saved_in[last]["gu"], saved[last]["gu"])
    columns(GU, 2 * hidden_cols)
    load(("first", last), saved_in[last]["first"], saved[last]["first"])
    columns(WO, 512)
    for name in ("qkv", "hidden"):
        load((name, last), saved_in[last][name], saved[last][name])
    columns(QKV, 640)
    for level in (1, 0):
        for name in saved_in[level]:
            load((name, level), saved_in[level][name], saved[level][name])
    p.barrier(False)
    gain_part[...] = jnp.zeros_like(gain_part)

    for level in range(last, -1, -1):
        own = OWN[level]
        count = T * own
        s = saved[level]
        base = 2 * (last - level)
        present = act_own[level, 0:own, :]
        if level == last:
            dg[level][...] = (cot_all[...].astype(F32).reshape(count, width) * act_last[...]).astype(BF).reshape(
                T, own, width
            )
            loads["grad"].wait()
        else:
            dg[level][p.t] = (present * grad[0:own, :]).astype(BF)
            view = dg[level].reshape(2, 2, own, width)
            rows.gather_start(base, view)
            rows.gather_finish(base, view)
        write(dg[level], dg_out[level])
        if level == last:
            loads["w", WD].wait()
        loads["gu", level].wait()

        def hidden_block(start, size):
            wcols = pl.ds(pl.multiple_of(WD + start, 128), size)
            product_grad = dot(dg[level][...].reshape(count, width), w[:, wcols], NN)
            for h in range(size // 128):
                at = pl.multiple_of(2 * start + 256 * h, 256)
                gate = s["gu"][:, pl.ds(at, 128)].astype(F32)
                upward = s["gu"][:, pl.ds(at + 128, 128)].astype(F32)
                sigma = jax.nn.sigmoid(gate)
                up = product_grad[:, 128 * h : 128 * h + 128]
                gug[level][:, pl.ds(at, 128)] = (up * upward * sigma * (1.0 + gate * (1.0 - sigma))).astype(BF)
                gug[level][:, pl.ds(at + 128, 128)] = (up * gate * sigma).astype(BF)

        @pl.loop(0, hidden_cols // 256)
        def _(j):
            hidden_block(j * 256, 256)

        if hidden_cols % 256:
            hidden_block(hidden_cols // 256 * 256, 128)
        write(gug[level], gug_out[level])
        if level == last:
            loads["w", GU].wait()

        def mlp_tile(cols):
            return dot(gug[level][...], w[cols, GU : GU + 2 * hidden_cols], NT)

        def take(cols, total):
            upstream[0:own, cols] = total

        rows.reduce(base, own, mlp_tile, take)
        loads["first", level].wait()
        update, add = norm_back(s["first"][...], gain[1:2, :], upstream[0:own, :])
        grad[0:own, :] += update
        gain_part[1:2, :] += add
        if level == 0:
            break
        og[level][p.t] = (present * grad[0:own, :]).astype(BF)
        view = og[level].reshape(2, 2, own, width)
        rows.gather_start(base + 1, view)
        rows.gather_finish(base + 1, view)
        write(og[level], og_out[level])
        if level == last:
            loads["w", WO].wait()
        loads["qkv", level].wait()
        attended_grad = dot(og[level][...].reshape(count, width), w[:, WO : WO + 512], NN)
        cos, sin = level_rows(cosine, own), level_rows(sine, own)
        qkvg[level][...] = attention_back(
            s["qkv"][...].astype(F32), attended_grad, cos, sin, allowed[level], own
        ).astype(BF)
        write(qkvg[level], qkvg_out[level])
        if level == last:
            loads["w", QKV].wait()

        def attention_tile(cols):
            return dot(qkvg[level][...], w[cols, QKV : QKV + 640], NT)

        rows.reduce(base + 1, own, attention_tile, take)
        loads["hidden", level].wait()
        update, add = norm_back(s["hidden"][...], gain[0:1, :], upstream[0:own, :])
        grad[0:own, :] += update
        gain_part[0:1, :] += add

    write(grad, grad_out)
    for copy in writes:
        copy.wait()


def backward(n, w_all, gain, cot_own, cot_all, tables, saved, tensor_index):
    perm, back, cosine, sine, masks, act = tables
    width = w_all.shape[0]
    act_own = lax.dynamic_slice_in_dim(act, tensor_index * OWN[0], OWN[0], axis=1)[:, :, None]
    act_last = act[RECUR - 1].reshape(T, OWN[0])[:, : OWN[2]].reshape(-1)[:, None]
    hidden_cols = (COLS - GU) // 3
    vmem = pl.BlockSpec(memory_space=pltpu.VMEM)
    hbm = pl.BlockSpec(memory_space=pl.ANY)
    operands = [w_all, gain, cot_own, cot_all, cosine, sine, act_own, act_last, masks[1], masks[2]]
    specs = [hbm, vmem, hbm] + [vmem] * 7
    used = []
    for level in range(RECUR):
        for name in ("gu", "first") if level == 0 else ("gu", "first", "qkv", "hidden"):
            operands.append(saved[level][name])
            specs.append(hbm)
            used.append(saved[level][name])
    outs = [((T, own, width), BF) for own in OWN]
    outs += [((T * own, 2 * hidden_cols), BF) for own in OWN]
    outs += [((T, own, width), BF) for own in OWN[1:]]
    outs += [((T * own, 640), BF) for own in OWN[1:]]
    scratch = [pltpu.VMEM(w_all.shape, BF)] + [pltpu.VMEM(u.shape, u.dtype) for u in used]
    scratch += [pltpu.VMEM(*entry) for entry in outs]
    outs += [((OWN[0], width), F32), ((8, width), F32)]
    out_specs = [hbm] * (len(outs) - 1) + [vmem]
    scratch += [pltpu.VMEM((OWN[0], width), F32)] * 2
    scratch += [pltpu.VMEM((2, 2, OWN[0], width), BF), pltpu.VMEM((OWN[0], width), BF)]
    for own in (OWN[2], OWN[2], OWN[1], OWN[1], OWN[0]):
        scratch += [pltpu.VMEM((2, own, width), BF), pltpu.VMEM((own, width), BF)]
    dma = pltpu.SemaphoreType.DMA
    chunks = width // DC
    scratch += [dma((5, chunks))] * 4 + [dma((5, 3))] * 2 + [dma((24,)), dma((16,))]
    res = pl.pallas_call(
        functools.partial(backward_kernel, n),
        out_shape=[jax.ShapeDtypeStruct(*entry) for entry in outs],
        in_specs=specs,
        out_specs=out_specs,
        scratch_shapes=scratch,
        compiler_params=pltpu.CompilerParams(
            collective_id=2, has_side_effects=True, vmem_limit_bytes=62 << 20
        ),
    )(*operands)
    return {
        "dg": res[0:3],
        "gug": res[3:6],
        "og": res[6:8],
        "qkvg": res[8:10],
        "grad": res[10],
        "gain_part": res[11],
    }


GRADS = (
    ("down", 0, 768),
    ("down", 768, 640),
    ("gu", 0, 768),
    ("gu", 768, 768),
    ("gu", 1536, 768),
    ("gu", 2304, 512),
    ("out", 0, 512),
    ("qkv", 0, 384),
    ("qkv", 384, 256),
)
WIDEST = 768
DEPTH = 2


def gradient_kernel(n, *refs):
    it = iter(refs)
    (w_all, gain, cosine, sine, act_own, allowed, back) = [next(it) for _ in range(7)]
    grad_in, gain_in, fin_in, hidden_in, qkv_in = [next(it) for _ in range(5)]
    x_in = {name: [next(it) for _ in range(3)] for name in ("down", "gu", "qkv")}
    x_in["out"] = [None] + [next(it) for _ in range(2)]
    y_in = {name: [next(it) for _ in range(3)] for name in ("down", "gu", "out")}
    y_in["qkv"] = [None] + [next(it) for _ in range(2)]
    (act_out, tok_out, dq, dk, dv, dwo, dgate, dup, dwd, gain_sum) = [next(it) for _ in range(10)]
    og_hbm, fin_all, grad_all = [next(it) for _ in range(3)]
    w = next(it)
    y = {name: next(it) for name in ("down", "gu", "out", "qkv")}
    xm, xl = next(it), next(it)
    og, hidden, qkv, grad, upstream, gains = [next(it) for _ in range(6)]
    gpeers = next(it)
    stage, landed, across, across_own = [next(it) for _ in range(4)]
    window_tmp = next(it)
    gmate_stage, gmate, gline, gline_own = [next(it) for _ in range(4)]
    final = [next(it) for _ in range(2)]
    finalt = next(it)
    chunk_in, chunk_out = next(it), next(it)
    fin_chunk = next(it)
    part, relay = next(it), next(it)
    sums = [(next(it), next(it))]
    row_sems = [next(it) for _ in range(6)]
    msend, mrecv, lsend, lrecv, lrecv2 = [next(it) for _ in range(5)]
    tsend, trecv = next(it), next(it)
    insem, xsem, outsem, finsem, loadsem = [next(it) for _ in range(5)]

    p = Place(n)
    width = w.shape[0]
    line = p.line
    chunk_rows = width // n
    window = max(128, chunk_rows)
    rows = Rows(p, part, relay, sums, row_sems)
    own = OWN[0]
    count = T * own
    starts = [0, T * OWN[0], T * (OWN[0] + OWN[1])]
    total_rows = T * sum(OWN)
    loads, writes = {}, []

    def load(name, src, dst):
        copy = pltpu.make_async_copy(src, dst, insem.at[len(loads)])
        copy.start()
        loads[name] = copy

    def write(src, dst):
        copy = pltpu.make_async_copy(src, dst, outsem.at[len(writes)])
        copy.start()
        writes.append(copy)

    load("grad", grad_in, grad)
    for name in ("down", "gu"):
        for level in range(RECUR):
            load((name, level), y_in[name][level], y[name].at[pl.ds(starts[level], T * OWN[level])])
    load("w", w_all.at[:, pl.ds(0, GU)], w)
    load("qkv", qkv_in, qkv)
    load("hidden", hidden_in, hidden)
    for level in range(RECUR):
        load(("out", level), y_in["out"][level], y["out"].at[pl.ds(starts[level], T * OWN[level])])
    for level in (1, 2):
        load(("qkv", level), y_in["qkv"][level], y["qkv"].at[pl.ds(starts[level], T * OWN[level])])
    p.barrier(True)

    for which in range(3):
        peers_copy(p, fin_in, fin_all, tsend.at[0], trecv.at[0], which).start()
    pltpu.make_async_copy(fin_in, fin_all.at[p.t], tsend.at[0, 3]).start()

    def x_source(which, level):
        return og_hbm if which == "out" and level == 0 else x_in[which][level]

    def level_slice(level):
        return pl.ds(sum(OWN[:level]) * T, OWN[level] * T)

    def x_copy(which, chunk, buffer, slot, level, sem):
        start = pl.multiple_of(chunk * chunk_rows // window * window, window)
        src = x_source(which, level).reshape(T * OWN[level], width)
        return pltpu.make_async_copy(
            src.at[:, pl.ds(start, window)], buffer.at[slot, level_slice(level)], sem.at[slot, level]
        )

    def x_start(which, parity, buffer, sem):
        @pl.loop(0, line)
        def _(i):
            for level in range(RECUR):
                x_copy(which, 2 * i + parity, buffer, i, level, sem).start()

    def tile(k, chunk, buffer, slot, sem):
        which, start, cols = GRADS[k]
        for level in range(RECUR):
            x_copy(which, chunk, buffer, slot, level, sem).wait()
        value = dot(buffer[slot], y[which][:, start : start + cols], TN)
        if window == chunk_rows:
            return value
        window_tmp[:, 0:cols] = value
        shift = pl.multiple_of(lax.rem(chunk, window // chunk_rows) * chunk_rows, chunk_rows)
        return window_tmp[pl.ds(shift, chunk_rows), 0:cols]

    offsets = np.cumsum([0] + [cols for _, _, cols in GRADS])

    def mate_copy(k, i):
        cols = GRADS[k][2]
        return remote(
            stage.at[k % DEPTH, i, :, pl.ds(0, cols)],
            landed.at[i, :, pl.ds(int(offsets[k]), cols)],
            msend.at[k, i],
            mrecv.at[k, i],
            p.mate,
        )

    def mates(k):
        which, start, cols = GRADS[k]
        x_start(which, 1 - p.b, xm, xsem.at[0])
        if k >= DEPTH:

            @pl.loop(0, line)
            def _(i):
                mate_copy(k - DEPTH, i).wait_send()

        @pl.loop(0, line)
        def _(i):
            stage[k % DEPTH, i, :, 0:cols] = tile(k, 2 * i + 1 - p.b, xm, i, xsem.at[0]).astype(BF)
            mate_copy(k, i).start()

    def along(k, i, right):
        cols = GRADS[k][2]
        piece = pl.ds(int(offsets[k]), cols)
        dst = across.at[i, :, piece]
        return remote(
            landed.at[i, :, piece], dst, lsend.at[k, i], lrecv.at[k, i], p.right if right else p.left
        )

    def along_last(k, i):
        cols = GRADS[k][2]
        piece = pl.ds(int(offsets[k]), cols)
        return remote(
            landed.at[i, :, piece], across_own.at[:, piece], lsend.at[k, i], lrecv2.at[k], p.left
        )

    def lines(k, finish):
        which, start, cols = GRADS[k]
        piece = pl.ds(int(offsets[k]), cols)

        @pl.loop(0, line)
        def _(step):
            odd = lax.rem(step, 2)
            i = jnp.where(odd == 1, step // 2, line - 1 - step // 2)

            @pl.when(i != p.a)
            def _():
                value = tile(k, 2 * i + p.b, xl, i, xsem.at[1])
                mate_copy(k, i).wait_recv()
                value = value + landed[i, :, piece].astype(F32)

                def passed(value):
                    landed[i, :, piece] = value.astype(BF)

                inner = ((i > p.a) & p.has_left) | ((i < p.a) & p.has_right)

                @pl.when(inner)
                def _():
                    along(k, i, True).wait_recv()
                    passed(value + across[i, :, piece].astype(F32))

                @pl.when(jnp.logical_not(inner))
                def _():
                    passed(value)

                @pl.when(i > p.a)
                def _():
                    along(k, i, True).start()

                @pl.when((i < p.a) & (i < p.a - 1))
                def _():
                    along(k, i, False).start()

                @pl.when((i < p.a) & (i == p.a - 1))
                def _():
                    along_last(k, i).start()

        value = tile(k, 2 * p.a + p.b, xl, p.a, xsem.at[1])
        mate_copy(k, p.a).wait_recv()
        finish(value + landed[p.a, :, piece].astype(F32))

        @pl.when(p.has_left)
        def _():
            along(k, p.a, True).wait_recv()
            finish(across[p.a, :, piece].astype(F32), True)

        @pl.when(p.has_right)
        def _():
            along_last(k, p.a).wait_recv()
            finish(across_own[:, piece].astype(F32), True)

    def drain(k):
        @pl.loop(0, line)
        def _(i):
            if k >= len(GRADS) - DEPTH:
                mate_copy(k, i).wait_send()

            @pl.when(i != p.a)
            def _():
                along(k, i, True).wait_send()

    staged, turned = {}, []

    def store(k):
        which, start, cols = GRADS[k]
        buffer = final[k % 2]
        for copy in staged.pop(k - 2, ()):
            copy.wait()

        def finish(value, more=False):
            if more:
                buffer[:, 0:cols] += value
            else:
                buffer[:, 0:cols] = value

        lines(k, finish)
        copies = []

        def out(src, dst):
            copy = pltpu.make_async_copy(src, dst, finsem.at[k, len(copies)])
            copy.start()
            copies.append(copy)

        if which in ("down", "out"):
            while turned:
                turned.pop().wait()
            finalt[0:cols, :] = buffer[:, 0:cols].T
            target = dwd if which == "down" else dwo
            out(finalt.at[pl.ds(0, cols)], target.at[pl.ds(start, cols)])
            turned.extend(copies)
            return
        if which == "gu":
            for j in range(cols // 256):
                at = start // 2 + j * 128
                out(buffer.at[:, pl.ds(j * 256, 128)], dgate.at[:, pl.ds(at, 128)])
                out(buffer.at[:, pl.ds(j * 256 + 128, 128)], dup.at[:, pl.ds(at, 128)])
        elif start == 0:
            out(buffer.at[:, pl.ds(0, cols)], dq.at[:, pl.ds(0, cols)])
        else:
            out(buffer.at[:, pl.ds(0, 128)], dq.at[:, pl.ds(start, 128)])
            dk[...] = buffer[:, 128:192]
            dv[...] = buffer[:, 192:256]
        staged[k] = copies

    loads["grad"].wait()
    present = act_own[0, 0:own, :]
    og[p.t] = (present * grad[...]).astype(BF)
    view = og.reshape(2, 2, own, width)
    rows.gather_start(0, view)
    for level in range(RECUR):
        loads["down", level].wait()
    mates(0)
    rows.gather_finish(0, view)
    write(og, og_hbm)
    mates(1)
    loads["w"].wait()
    loads["qkv"].wait()
    attended_grad = dot(og[...].reshape(count, width), w[:, WO : WO + 512], NN)
    y["qkv"][0:count, :] = attention_back(
        qkv[...].astype(F32), attended_grad, cosine[...], sine[...], allowed, own
    ).astype(BF)

    def attention_tile(cols):
        return dot(y["qkv"][0:count, :], w[cols, QKV : QKV + 640], NT)

    def take(cols, total):
        upstream[:, cols] = total

    rows.reduce(0, own, attention_tile, take)
    loads["hidden"].wait()
    update, add = norm_back(hidden[...], gain[0:1, :], upstream[...])
    grad[...] += update
    gains[...] = gain_in[...]
    gains[0:1, :] += add
    for which in range(3):
        peers_copy(p, grad, grad_all, tsend.at[1], trecv.at[1], which).start()
        peers_copy(p, gains, gpeers, tsend.at[2], trecv.at[2], which).start()
    pltpu.make_async_copy(grad, grad_all.at[p.t], tsend.at[1, 3]).start()
    gpeers[p.t] = gains[...]
    for level in range(RECUR):
        loads["gu", level].wait()
        loads["out", level].wait()
    for level in (1, 2):
        loads["qkv", level].wait()
    for copy in writes:
        copy.wait()

    def wait_peers(i, src, dst, local=True):
        for which in range(3):
            copy = peers_copy(p, src, dst, tsend.at[i], trecv.at[i], which)
            copy.wait_recv()
            copy.wait_send()
        if local:
            pltpu.make_async_copy(src, dst.at[p.t], tsend.at[i, 3]).wait()

    def outputs():
        wait_peers(0, fin_in, fin_all)
        wait_peers(1, grad, grad_all)
        mine = back[pl.ds(pl.multiple_of(p.t * own, own), own), :]

        @pl.loop(0, width // OC)
        def _(c):
            cols = pl.ds(pl.multiple_of(c * OC, OC), OC)
            first = pltpu.make_async_copy(fin_all.at[:, :, cols], fin_chunk, loadsem.at[0])
            second = pltpu.make_async_copy(grad_all.at[:, :, cols], chunk_in, loadsem.at[1])
            first.start()
            second.start()
            first.wait()
            second.wait()
            act_out[:, :, cols] = dot(mine, fin_chunk[...].reshape(count, OC), NN).astype(BF).reshape(
                MB, own // MB, OC
            )
            value = chunk_in[...].reshape(count, OC)
            high = value.astype(BF)
            rest = value - high.astype(F32)
            middle = rest.astype(BF)
            low = (rest - middle.astype(F32)).astype(BF)
            total = dot(mine, high, NN) + (dot(mine, middle, NN) + dot(mine, low, NN))
            tok_out[:, :, cols] = total.reshape(MB, own // MB, OC)

    def gain_tile(chunk):
        start = pl.multiple_of(chunk * chunk_rows // window * window, window)
        return (
            gpeers[0, :, pl.ds(start, window)]
            + gpeers[1, :, pl.ds(start, window)]
            + gpeers[2, :, pl.ds(start, window)]
            + gpeers[3, :, pl.ds(start, window)]
        )

    last = len(GRADS)

    def gain_mate(i):
        return remote(gmate_stage.at[i], gmate.at[i], msend.at[last, i], mrecv.at[last, i], p.mate)

    def gain_along(i, right):
        return remote(
            gmate.at[i], gline.at[i], lsend.at[last, i], lrecv.at[last, i], p.right if right else p.left
        )

    def gain_last(i):
        return remote(gmate.at[i], gline_own, lsend.at[last, i], lrecv2.at[last], p.left)

    def gain_mates():
        wait_peers(2, gains, gpeers, False)

        @pl.loop(0, line)
        def _(i):
            gmate_stage[i] = gain_tile(2 * i + 1 - p.b)
            gain_mate(i).start()

    def gain_lines():
        @pl.loop(0, line)
        def _(step):
            odd = lax.rem(step, 2)
            i = jnp.where(odd == 1, step // 2, line - 1 - step // 2)

            @pl.when(i != p.a)
            def _():
                gain_mate(i).wait_recv()
                gmate[i] += gain_tile(2 * i + p.b)

                @pl.when(((i > p.a) & p.has_left) | ((i < p.a) & p.has_right))
                def _():
                    gain_along(i, True).wait_recv()
                    gmate[i] += gline[i]

                pl.when(i > p.a)(lambda: gain_along(i, True).start())
                pl.when(i < p.a - 1)(lambda: gain_along(i, False).start())
                pl.when(i == p.a - 1)(lambda: gain_last(i).start())

        gain_mate(p.a).wait_recv()
        gain_sum[...] = gain_tile(2 * p.a + p.b) + gmate[p.a]

        @pl.when(p.has_left)
        def _():
            gain_along(p.a, True).wait_recv()
            gain_sum[...] += gline[p.a]

        @pl.when(p.has_right)
        def _():
            gain_last(p.a).wait_recv()
            gain_sum[...] += gline_own[...]

        @pl.loop(0, line)
        def _(i):
            gain_mate(i).wait_send()
            pl.when(i != p.a)(lambda: gain_along(i, True).wait_send())

    for k in range(len(GRADS)):
        x_start(GRADS[k][0], p.b, xl, xsem.at[1])
        if k + DEPTH < len(GRADS):
            mates(k + DEPTH)
        if k == 1:
            gain_mates()
        if k == 2:
            gain_lines()
        if k == 3:
            outputs()
        store(k)
    for k in range(len(GRADS)):
        drain(k)
    for copies in list(staged.values()) + [turned]:
        for copy in copies:
            copy.wait()


def gradients(n, w_all, gain, tables, saved, bwd, fin, tensor_index):
    perm, back, cosine, sine, masks, act = tables
    width = w_all.shape[0]
    act_own = lax.dynamic_slice_in_dim(act, tensor_index * OWN[0], OWN[0], axis=1)[:, :, None]
    hidden_cols = (COLS - GU) // 3
    line = n // 2
    chunk_rows = width // n
    window = max(128, chunk_rows)
    vmem = pl.BlockSpec(memory_space=pltpu.VMEM)
    hbm = pl.BlockSpec(memory_space=pl.ANY)
    total_rows = T * sum(OWN)
    own = OWN[0]
    operands = [w_all, gain, cosine, sine, act_own, masks[0], back]
    specs = [hbm] + [vmem] * 6
    operands += [bwd["grad"], bwd["gain_part"], fin, saved[0]["hidden"], saved[0]["qkv"]]
    specs += [hbm, vmem, hbm, hbm, hbm]
    streams = list(bwd["dg"]) + [s["mixed"] for s in saved] + [s["normed"] for s in saved] + list(bwd["og"])
    streams += [s["prod"] for s in saved] + list(bwd["gug"]) + [s["att"] for s in saved] + list(bwd["qkvg"])
    operands += streams
    specs += [hbm] * len(streams)
    outs = [
        ((MB, own // MB, width), BF),
        ((MB, own // MB, width), F32),
        ((chunk_rows, 512), F32),
        ((chunk_rows, HS), F32),
        ((chunk_rows, HS), F32),
        ((512, chunk_rows), F32),
        ((chunk_rows, hidden_cols), F32),
        ((chunk_rows, hidden_cols), F32),
        ((hidden_cols, chunk_rows), F32),
        ((8, window), F32),
        ((T, own, width), BF),
        ((T, own, width), BF),
        ((T, own, width), F32),
    ]
    out_specs = [vmem, vmem, hbm, vmem, vmem, hbm, hbm, hbm, hbm, vmem, hbm, hbm, hbm]
    scratch = [pltpu.VMEM((width, GU), BF)]
    scratch += [pltpu.VMEM((total_rows, c), BF) for c in (hidden_cols, 2 * hidden_cols, 512, 640)]
    scratch += [pltpu.VMEM((line, total_rows, window), BF)] * 2
    scratch += [
        pltpu.VMEM((T, own, width), BF),
        pltpu.VMEM((own, width), F32),
        pltpu.VMEM((T * own, 640), BF),
        pltpu.VMEM((own, width), F32),
        pltpu.VMEM((own, width), F32),
        pltpu.VMEM((8, width), F32),
        pltpu.VMEM((T, 8, width), F32),
    ]
    scratch += [
        pltpu.VMEM((DEPTH, line, chunk_rows, WIDEST), BF),
        pltpu.VMEM((line, chunk_rows, COLS), BF),
        pltpu.VMEM((line, chunk_rows, COLS), BF),
        pltpu.VMEM((chunk_rows, COLS), BF),
        pltpu.VMEM((window, WIDEST) if window > chunk_rows else (8, 128), F32),
    ]
    scratch += [pltpu.VMEM((line, 8, window), F32)] * 3 + [pltpu.VMEM((8, window), F32)]
    scratch += [pltpu.VMEM((chunk_rows, WIDEST), F32)] * 2
    scratch += [pltpu.VMEM((WIDEST, chunk_rows), F32)]
    scratch += [pltpu.VMEM((T, own, OC), F32), pltpu.VMEM((8, 128), F32), pltpu.VMEM((T, own, OC), BF)]
    scratch += [pltpu.VMEM((2, 2, own, width), BF), pltpu.VMEM((own, width), BF)]
    scratch += [pltpu.VMEM((2, own, width), BF), pltpu.VMEM((own, width), BF)]
    dma = pltpu.SemaphoreType.DMA
    chunks = width // DC
    k = len(GRADS) + 1
    scratch += [dma((1, chunks))] * 4 + [dma((1, 3))] * 2
    scratch += [dma((k, line))] * 4 + [dma((k,))]
    scratch += [dma((3, 4)), dma((3, 3))]
    scratch += [dma((24,)), dma((2, line, RECUR)), dma((4,)), dma((k, 8)), dma((2,))]
    res = pl.pallas_call(
        functools.partial(gradient_kernel, n),
        out_shape=[jax.ShapeDtypeStruct(*entry) for entry in outs],
        in_specs=specs,
        out_specs=out_specs,
        scratch_shapes=scratch,
        compiler_params=pltpu.CompilerParams(
            collective_id=3, has_side_effects=True, vmem_limit_bytes=63 << 20
        ),
    )(*operands)
    return res


def shards(n, *args):
    tokens, depth, lengths, cotangent = args[:4]
    attn_gain, mlp_gain = args[11:]
    index = lax.axis_index("tensor")
    tables = prologue(depth, lengths[:, 0], index)
    joined = join_weights(*args[4:11])
    gains = place_gains(n, attn_gain, mlp_gain)
    w_all, gain, fin, cot_own, cot_all, saved = forward(n, tokens, cotangent, joined, gains, tables, index)
    bwd = backward(n, w_all, gain, cot_own, cot_all, tables, saved, index)
    res = gradients(n, w_all, gain, tables, saved, bwd, fin, index)
    activations, tokens_grad, dq, dk, dv, dwo, dgate, dup, dwd, gain_sum = res[:10]
    each = attn_gain.shape[0]
    window = gain_sum.shape[1]
    start = lax.rem((lax.axis_index("dp") * T + index) * each, window)
    both = lax.dynamic_slice_in_dim(gain_sum, start, each, axis=1)
    return (activations, tokens_grad, dq, dk, dv, dwo, dgate, dup, dwd, both[0], both[1])


def solution(mesh):
    rows = P(None, ("dp", "tensor"), None)
    weight_specs = (P("dp", "tensor"),) * 3 + (P("tensor", "dp"),) + (P("dp", "tensor"),) * 2 + (P("tensor", "dp"),)
    gain_specs = (P(("dp", "tensor")),) * 2
    return jax.shard_map(
        functools.partial(shards, mesh.shape["dp"]),
        mesh=mesh,
        in_specs=(rows, P(None, "dp"), P(None, "dp", None), rows) + weight_specs + gain_specs,
        out_specs=(rows, rows) + weight_specs + gain_specs,
        check_vma=False,
    )
```

time: 2110 us -> 922 us (0.44)
  waiting for transfers between devices: 875 us -> 0 us
  Pallas kernels: 0 us -> 860 us
  matrix products: 403 us -> 0 us
  blocking collectives: 355 us -> 0 us
  other arithmetic: 282 us -> 22.2 us
  local copies, waits for them, and re-layouts: 158 us -> 29.6 us
    pallas_call x0 -> x3, Pallas kernels: none -> 860 us  [the longest x1 369 us: gradients(): pl.pallas_call(functools.partial(gradient_kernel, n), out_shape=[jax.Shap...]
    reduce_scatter x31 -> x0, waiting for transfers between devices: 614 us -> none  [the longest x1 111 us: shards(): lax.psum_scatter(grad_total[6].astype(jnp.bfloat16), 'dp', scatter_dimens...]
    dot_general x162 -> x0, matrix products: 403 us -> none  [the longest x42 175 us: left_times(): jnp.einsum('ca,cb->ab', left, right, preferred_element_type=jnp.float32)]
    all_gather x26 -> x0, blocking collectives: 271 us -> none  [the longest x12 105 us: spread_rows(): return lax.all_gather(values, 'tensor', axis=0, tiled=True)]
    all_gather x5 -> x0, waiting for transfers between devices: 257 us -> none  [the longest x1 88.2 us: shards(): lax.all_gather(w_down, 'dp', axis=1, tiled=True)]
    convert_element_type x79 -> x6, other arithmetic: 112 us -> 8.95 us  [the longest x1 4.57 us: prologue(): act.append((rank_q < limit).astype(F32))]
    scatter-add x30 -> x0, other arithmetic: 100 us -> none  [the longest x12 46.6 us: shards(): jnp.zeros((compact_rows, width), jnp.float32).at[chosen].add(branch)]
    unnamed x2 -> x0, blocking collectives: 83.8 us -> none
  transfers between devices with their start and end apart: 36 -> 0, of which waited for: 21 -> 0; matrix products, arithmetic and copies ran while one was open for 26% -> 0% of each run, Pallas kernels for 0% -> 0%
where the time goes in v1:
time: 922 us; the launch traced here: 913 us
  Pallas kernels  860 us (93%)
  local copies, waits for them, and re-layouts  29.6 us (3%)
  other arithmetic  22.2 us (2%)
    pallas_call x1, Pallas kernels, gradients(): pl.pallas_call(functools.partial(gradient_kernel, n), out_shape=[jax.Shap...  369 us
    pallas_call x1, Pallas kernels, forward(): pl.pallas_call(functools.partial(forward_kernel, n), out_shape=[jax.Shape...  363 us
    pallas_call x1, Pallas kernels, backward(): pl.pallas_call(functools.partial(backward_kernel, n), out_shape=[jax.Shap...  127 us
    unnamed x43, local copies, waits for them, and re-layouts  18.9 us

profile of v1, /device:TPU:0, one launch (start us, length us, event | category | flops | bytes accessed | tf_op | source)
XLA Modules:
  0.0 912.6 jit_solution(18354029255839958005)
XLA Ops:
  0.7 0.9 reduce_window_sum.11
  1.5 0.7 sub.10
  2.2 0.1 copy.104
  2.3 0.7 pad_maximum_fusion.3
  3.0 0.8 fusion.8
  3.8 0.7 broadcast_compare_fusion.2
  4.5 0.8 broadcast_compare_fusion.1
  5.3 0.6 fusion.17
  5.9 0.8 broadcast_compare_fusion
  6.6 0.6 fusion.15
  7.2 4.6 fusion.14
  11.8 0.1 fusion.11
  11.9 0.1 reshape_squeeze_stack.3
  12.0 0.3 dynamic_update_slice.3.refs_3_
  12.2 0.0 copy-start.12
  12.3 0.8 copy.125
  13.1 0.8 copy.124
  13.9 1.0 convert_reduce_fusion
  14.9 0.8 select_reduce_fusion.3
  15.8 0.1 fusion.5
  15.9 0.9 select_reduce_fusion.2
  16.8 0.9 select_reduce_fusion.1
  17.7 0.1 reshape.167
  17.8 0.1 eq.126
  17.9 1.2 select_reduce_fusion
  19.1 0.7 fusion.4
  19.8 0.1 fusion.2
  19.9 0.1 fusion.3
  20.0 0.9 copy.100
  20.9 0.9 copy.101
  21.7 1.5 or_convert_fusion.2.refs_9_
  23.2 0.8 broadcast_in_dim_reshape.6.refs_7_
  24.0 0.8 copy.107.refs_10_.refs_6_.refs_4_
  24.8 1.1 copy.95
  25.9 0.9 or_convert_fusion.1.refs_8_
  26.8 0.9 or_convert_fusion.refs_7_.refs_5_
  27.7 0.8 fusion.1
  28.5 0.0 copy-start.5
  28.5 1.1 pad_maximum_fusion.1
  29.6 1.1 and_convert_fusion
  30.7 0.3 copy.96
  31.0 0.3 copy.97
  31.3 0.1 pad_maximum_fusion
  31.5 2.1 copy.98
  33.6 0.6 reshape.166
  34.2 0.0 copy-start.9
  34.2 1.5 copy.99
  35.7 3.2 concatenate.9.refs_2_
  38.9 363.3 %shard_map.383 = (bf16[2048,5376]{1,0:T(8,128)(2,1)}, f32[8,2048]{1,0:T(8,128)}, bf16[96,2048]{1,0:T(8,128)(2,1)}, f32[96,2048]{1,0:T(8,128)}, bf16[4,48,2048]{2...) custom-call(bf16[2,48,2048]{2,1,0:T(8,128)(2,1)} %refs_0_.1, ...), custom_call_target="tpu_custom_call" | custom-call | tf_op jit(solution)/shard_map/pallas_call | solution.py:620
  402.2 127.3 %shard_map.384 = (bf16[4,96,2048]{2,1,0:T(8,128)(2,1)}, bf16[4,80,2048]{2,1,0:T(8,128)(2,1)}, bf16[4,48,2048]{2,1,0:T(8,128)(2,1)}, bf16[384,2816]{1,0:T(8,128)(...) custom-call(bf16[2048,5376]{1,0:T(8,128)(2,1)} %get-tuple-element.62, ...), custom_call_target="tpu_custom_call" | custom-call | tf_op jit(solution)/shard_map/pallas_call | solution.py:878
  529.6 368.9 %shard_map.385 = (bf16[2,48,2048]{2,1,0:T(8,128)(2,1)}, f32[2,48,2048]{2,1,0:T(8,128)}, f32[256,512]{1,0:T(8,128)}, f32[256,64]{1,0:T(8,128)}, f32[256,64]{1,0:T...) custom-call(bf16[2048,5376]{1,0:T(8,128)(2,1)} %get-tuple-element.62, ...), custom_call_target="tpu_custom_call" | custom-call | tf_op jit(solution)/shard_map/pallas_call | solution.py:1390
  898.5 0.9 constant_dynamic-slice_fusion
  899.4 0.5 slice_bitcast_fusion
  899.9 1.6 copy.111
  901.5 1.6 copy.112
  903.1 1.8 copy.126
  904.9 0.9 copy.127
  905.8 0.8 copy.128
  906.6 0.8 copy.129
  907.4 1.1 copy.130
  908.5 0.8 copy-done.1
  909.2 1.1 copy.131
  910.3 0.8 copy-done
  911.1 1.1 copy.132
  (30 shorter events, 0.1 us)
Async XLA Ops:
  12.2 16.3 %copy-start.12 = (f32[8,128]{1,0:T(8,128)}, f32[8,128]{1,0:T(8,128)S(1)}, u32[]{:S(2)}) copy-start(f32[8,128]{1,0:T(8,128)S(1)} %dynamic_update_slice.3.refs_3_) | copy-start | bytes 12292
  24.8 4.9 copy-start.6
  24.8 4.9 copy-start.10
  24.8 4.9 copy-start.11
  26.8 3.9 copy-start.4
  28.5 2.5 copy-start.5
  34.2 1.5 copy-start.9
  898.5 6.4 copy-start.3
  898.5 7.3 copy-start.8
  904.9 1.7 copy-start.7
  904.9 2.5 copy-start.2
  907.4 1.9 copy-start.1
  909.2 1.9 copy-start

commit v2 on v1

--- a/solution.py
+++ b/solution.py
@@ -26,17 +26,7 @@
 T = 4
 DC = 512
 OC = 256
-HEADS = 4
-
-
-def own_table():
-    batch, place, seen = [], [], [0, 0]
-    for _, rows, b in PIECES:
-        for _ in range(rows):
-            batch.append(b)
-            place.append(seen[b])
-            seen[b] += 1
-    return np.array(batch), np.array(place)
+HEADS = 2
 
 
 def split_batches(values, own):
@@ -72,7 +62,7 @@
     group = query.shape[1] // HS
     stacked = stack_heads(query)
     scores = dot(stacked, key, NT).reshape(group, rows, rows) * SCALE
-    scores = jnp.where(allowed[None] > 0, scores, -1e30)
+    scores = jnp.where(allowed.astype(F32)[None] > 0, scores, -1e30)
     raised = jnp.exp(scores - jnp.max(scores, axis=-1, keepdims=True))
     return stacked, raised * (1.0 / jnp.sum(raised, axis=-1, keepdims=True))
 
@@ -137,45 +127,54 @@
     def __init__(self, place, pieces, sems):
         self.p = place
         self.pieces = pieces
-        self.local, self.msend, self.mrecv, self.rsend, self.rrecv, self.lsend, self.lrecv = sems
-
-    def toward_left(self, w, k, src, chunk):
-        dst = self.pieces[w][1](chunk)
-        return remote(src, dst, self.lsend.at[w, k], self.lrecv.at[w, k], self.p.left)
-
-    def toward_right(self, w, k, src, chunk):
-        dst = self.pieces[w][1](chunk)
-        return remote(src, dst, self.rsend.at[w, k], self.rrecv.at[w, k], self.p.right)
-
-    def toward_mate(self, w, k, src, chunk):
-        dst = self.pieces[w][1](chunk)
-        return remote(src, dst, self.msend.at[w, k], self.mrecv.at[w, k], self.p.mate)
+        self.msend, self.mrecv, self.rsend, self.rrecv, self.lsend, self.lrecv = sems
+
+    def toward_left(self, w, k, chunk):
+        ref = self.pieces[w][1](chunk)
+        return remote(ref, ref, self.lsend.at[w, k], self.lrecv.at[w, k], self.p.left)
+
+    def toward_right(self, w, k, chunk):
+        ref = self.pieces[w][1](chunk)
+        return remote(ref, ref, self.rsend.at[w, k], self.rrecv.at[w, k], self.p.right)
+
+    def toward_mate(self, w, k, chunk):
+        ref = self.pieces[w][1](chunk)
+        return remote(ref, ref, self.msend.at[w, k], self.mrecv.at[w, k], self.p.mate)
+
+    def first(self, w):
+        p = self.p
+        return p.a * 2 + 1 - p.b if self.pieces[w][0] == "other" else p.dp
 
     def own(self, w):
         p = self.p
-        src, dst = self.pieces[w]
-        pltpu.make_async_copy(src, dst(p.dp), self.local.at[w]).start()
-        pl.when(p.has_left)(lambda: self.toward_left(w, 0, src, p.dp).start())
-        pl.when(p.has_right)(lambda: self.toward_right(w, 0, src, p.dp).start())
-        self.toward_mate(w, p.a, src, p.dp).start()
+        kind = self.pieces[w][0]
+        chunk = self.first(w)
+        if kind == "other":
+            self.toward_mate(w - 1, p.a, chunk).wait_recv()
+        pl.when(p.has_left)(lambda: self.toward_left(w, 0, chunk).start())
+        pl.when(p.has_right)(lambda: self.toward_right(w, 0, chunk).start())
+        if kind != "other":
+            self.toward_mate(w, p.a, chunk).start()
 
     def step(self, w, k):
         p = self.p
-        dst = self.pieces[w][1]
+        normal = self.pieces[w][0] == "normal"
 
         @pl.when(p.a + k < p.line)
         def _():
-            chunk = p.dp + 2 * k
-            self.toward_left(w, k - 1, dst(chunk), chunk).wait_recv()
-            pl.when(p.has_left)(lambda: self.toward_left(w, k, dst(chunk), chunk).start())
-            self.toward_mate(w, p.a + k, dst(chunk), chunk).start()
+            chunk = self.first(w) + 2 * k
+            self.toward_left(w, k - 1, chunk).wait_recv()
+            pl.when(p.has_left)(lambda: self.toward_left(w, k, chunk).start())
+            if normal:
+                self.toward_mate(w, p.a + k, chunk).start()
 
         @pl.when(p.a - k >= 0)
         def _():
-            chunk = p.dp - 2 * k
-            self.toward_right(w, k - 1, dst(chunk), chunk).wait_recv()
-            pl.when(p.has_right)(lambda: self.toward_right(w, k, dst(chunk), chunk).start())
-            self.toward_mate(w, p.a - k, dst(chunk), chunk).start()
+            chunk = self.first(w) - 2 * k
+            self.toward_right(w, k - 1, chunk).wait_recv()
+            pl.when(p.has_right)(lambda: self.toward_right(w, k, chunk).start())
+            if normal:
+                self.toward_mate(w, p.a - k, chunk).start()
 
     def steps(self, w):
         for k in range(1, self.p.line):
@@ -183,19 +182,20 @@
 
     def arrive(self, w):
         p = self.p
-        src, dst = self.pieces[w]
-        pltpu.make_async_copy(src, dst(p.dp), self.local.at[w]).wait()
-        for i in range(p.line):
-            chunk = 2 * i + 1 - p.b
-            self.toward_mate(w, i, dst(chunk), chunk).wait_recv()
+        if self.pieces[w][0] == "normal":
+            for i in range(p.line):
+                self.toward_mate(w, i, 2 * i + 1 - p.b).wait_recv()
 
     def drain(self, w):
         p = self.p
-        dst = self.pieces[w][1]
+        kind = self.pieces[w][0]
+        if kind == "own":
+            self.toward_mate(w, p.a, p.dp).wait_send()
         for i in range(p.line):
-            self.toward_mate(w, i, dst(p.dp), p.dp).wait_send()
-            pl.when(p.has_left & (p.a + i < p.line))(lambda: self.toward_left(w, i, dst(p.dp), p.dp).wait_send())
-            pl.when(p.has_right & (p.a - i >= 0))(lambda: self.toward_right(w, i, dst(p.dp), p.dp).wait_send())
+            if kind == "normal":
+                self.toward_mate(w, i, p.dp).wait_send()
+            pl.when(p.has_left & (p.a + i < p.line))(lambda: self.toward_left(w, i, p.dp).wait_send())
+            pl.when(p.has_right & (p.a - i >= 0))(lambda: self.toward_right(w, i, p.dp).wait_send())
 
 
 class Rows:
@@ -232,19 +232,21 @@
         r1, r2 = self.sums[i]
         chunks = part.shape[-1] // DC
 
+        def pass_on(c):
+            cols = pl.ds(pl.multiple_of(c * DC, DC), DC)
+            self.first_copy(i, own, c).wait_recv()
+            mine = part[1 - p.hi, p.lo, 0:own, cols].astype(F32)
+            relay[0:own, cols] = (mine + r1[1 - p.hi, :, cols].astype(F32)).astype(BF)
+            self.second_copy(i, own, c).start()
+
         @pl.loop(0, chunks)
         def _(c):
             cols = pl.ds(pl.multiple_of(c * DC, DC), DC)
             part[:, :, 0:own, cols] = tile(cols).astype(BF).reshape(2, 2, own, DC)
             self.first_copy(i, own, c).start()
-
-        @pl.loop(0, chunks)
-        def _(c):
-            cols = pl.ds(pl.multiple_of(c * DC, DC), DC)
-            self.first_copy(i, own, c).wait_recv()
-            mine = part[1 - p.hi, p.lo, 0:own, cols].astype(F32)
-            relay[0:own, cols] = (mine + r1[1 - p.hi, :, cols].astype(F32)).astype(BF)
-            self.second_copy(i, own, c).start()
+            pl.when(c > 0)(lambda: pass_on(c - 1))
+
+        pass_on(chunks - 1)
 
         @pl.loop(0, chunks)
         def _(c):
@@ -301,41 +303,161 @@
 
 QKV, WO, GU, WD = 0, 640, 1152, 3968
 COLS = 5376
-RANGES = ((0, 640), (640, 512), (1152, 1536), (2688, 1280), (3968, 768), (4736, 640))
+RANGES = (
+    ("along", 0, 640),
+    ("along", 640, 512),
+    ("along", 1152, 1408),
+    ("along", 2560, 1408),
+    ("along", 3968, 512),
+    ("across", 4480, 896),
+)
+
+
+def ones(condition):
+    return jnp.where(condition, 1.0, 0.0)
+
+
+def iota(size, axis):
+    shape = (size, 1) if axis == 0 else (1, size)
+    return lax.broadcasted_iota(jnp.int32, shape, axis).astype(F32)
+
+
+def quotient(index, step, most):
+    total = ones(index >= step)
+    for i in range(2, most):
+        total = total + ones(index >= step * i)
+    return total
+
+
+def own_places(own_index):
+    batch, place, seen = 0.0 * own_index, 0.0 * own_index, [0, 0]
+    for start, rows, b in PIECES:
+        inside = (own_index >= start) & (own_index < start + rows)
+        batch = jnp.where(inside, float(b), batch)
+        place = jnp.where(inside, own_index - start + seen[b], place)
+        seen[b] += rows
+    return batch, place
+
+
+def fill_tables(p, depth_row, depth_col, lengths, freqs, perm, back, back_own, cosine, sine, allowed, act_own, act_last):
+    local = OWN[0] // MB
+    total = T * OWN[0]
+
+    def columns(index):
+        tensor = quotient(index, OWN[0], T)
+        inside = index - tensor * OWN[0]
+        batch = ones(inside >= local)
+        return batch, tensor * local + inside - batch * local
+
+    batch_row, pos_row = columns(iota(total, 1))
+    batch_col, pos_col = columns(iota(total, 0))
+    same = batch_row == batch_col
+    rank_row = jnp.sum(
+        ones(same & ((depth_col > depth_row) | ((depth_col == depth_row) & (pos_col < pos_row)))), axis=0, keepdims=True
+    )
+    rank_col = jnp.sum(
+        ones(same & ((depth_row > depth_col) | ((depth_row == depth_col) & (pos_row < pos_col)))), axis=1, keepdims=True
+    )
+
+    def compact(index):
+        owner = quotient(index, OWN[0], T)
+        batch, place = own_places(index - owner * OWN[0])
+        return batch, place * T + owner
+
+    batch_q, rank_q = compact(iota(total, 0))
+    hit = (rank_row == rank_q) & (batch_row == batch_q)
+    perm[...] = ones(hit).astype(BF)
+    batch_p, rank_p = compact(iota(total, 1))
+    back[...] = ones((rank_col == rank_p) & (batch_col == batch_p)).astype(BF)
+    back_own[...] = back[pl.ds(pl.multiple_of(p.t * OWN[0], OWN[0]), OWN[0]), :]
+
+    ends = []
+    for b in range(MB):
+        first = lengths[b : b + 1, 0:1].astype(F32)
+        ends.append((first, first + lengths[b : b + 1, 1:2].astype(F32)))
+    position = jnp.sum(jnp.where(hit, pos_row, 0.0), axis=1, keepdims=True)
+    end = [jnp.where(batch_q == 0.0, ends[0][i], ends[1][i]) for i in range(2)]
+    start = jnp.where(position >= end[1], end[1], jnp.where(position >= end[0], end[0], 0.0))
+    angles = (position - start) * freqs
+    cosine[...] = jnp.cos(angles)
+    lane = lax.broadcasted_iota(jnp.int32, angles.shape, 1)
+    value = jnp.sin(angles)
+    sine[...] = jnp.where((lane & 63) < 32, -value, value)
+
+    own_batch, own_place = own_places(iota(OWN[0], 0))
+    own_rank = own_place * T + p.t.astype(F32)
+    for level in range(RECUR):
+        own = OWN[level]
+        half = T * own // MB
+        counts = [
+            jnp.sum(ones((batch_row == float(b)) & (depth_row >= level + 1.0)), axis=1, keepdims=True) for b in range(MB)
+        ]
+        act_own[level] = ones(own_rank < jnp.where(own_batch == 0.0, counts[0], counts[1]))
+        if level == RECUR - 1:
+            index = iota(T * own, 0)
+            owner = quotient(index, own, T)
+            batch, place = own_places(index - owner * own)
+            act_last[...] = ones(place * T + owner < jnp.where(batch == 0.0, counts[0], counts[1]))
+
+        def order(index):
+            owner = quotient(index, own // MB, T)
+            return (index - owner * (own // MB)) * T + owner
+
+        index_col, index_row = iota(half, 0), iota(half, 1)
+        order_col, order_row = order(index_col), order(index_row)
+        for b in range(MB):
+            at_col = jnp.sum(
+                jnp.where((rank_row == order_col) & (batch_row == float(b)), pos_row, 0.0), axis=1, keepdims=True
+            )
+            at_row = jnp.sum(
+                jnp.where((rank_col == order_row) & (batch_col == float(b)), pos_col, 0.0), axis=0, keepdims=True
+            )
+            document_col = ones(at_col >= ends[b][0]) + ones(at_col >= ends[b][1])
+            document_row = ones(at_row >= ends[b][0]) + ones(at_row >= ends[b][1])
+            ok = (document_col == document_row) & (at_row <= at_col) & (order_row < counts[b])
+            allowed[level][b] = ones(ok | (index_col == index_row)).astype(BF)
 
 
 def forward_kernel(n, *refs):
     it = iter(refs)
-    (tokens, cotangent, weights, gains, perm, cosine, sine) = [next(it) for _ in range(7)]
+    tokens, cotangent, wq, wk, wv, wo, wg, wu, wd = [next(it) for _ in range(9)]
+    attn_gain, mlp_gain, depth_row, depth_col, lengths, freqs = [next(it) for _ in range(6)]
+    w_out, gain_out, fin_out, cot_own, cot_all = [next(it) for _ in range(5)]
+    cosine, sine, back_own, act_own, act_last = [next(it) for _ in range(5)]
     allowed = [next(it) for _ in range(RECUR)]
-    act_own = next(it)
-    w_out, gain_out, fin_out, cot_own, cot_all = [next(it) for _ in range(5)]
     names = ("normed", "qkv", "att", "mixed", "gu", "prod", "hidden", "first")
     saved_out = [dict((k, next(it)) for k in names) for _ in range(RECUR)]
     w = next(it)
+    perm, back, kv, wo_in, wd_in = [next(it) for _ in range(5)]
     gbuf, gall = next(it), next(it)
     tok, cot = next(it), next(it)
     saved = [dict((k, next(it)) for k in names) for _ in range(RECUR)]
     after, fin, cown = next(it), next(it), next(it)
     part, relay = next(it), next(it)
     sums = [(next(it), next(it)) for _ in range(2 * RECUR)]
-    line_sems = [next(it) for _ in range(7)]
+    line_sems = [next(it) for _ in range(6)]
     row_sems = [next(it) for _ in range(6)]
+    wsem = next(it)
     tsend, trecv, outsem = next(it), next(it), next(it)
 
     p = Place(n)
-    rows_chunk = weights.shape[0]
     width = tokens.shape[-1]
-
-    def piece(start, size):
-        return (
-            weights.at[:, pl.ds(start, size)],
-            lambda chunk: w.at[pl.ds(pl.multiple_of(chunk * rows_chunk, rows_chunk), rows_chunk), pl.ds(start, size)],
-        )
-
-    pieces = [(gains, lambda chunk: gbuf.at[chunk])] + [piece(*r) for r in RANGES]
+    rows_chunk = width // n
+
+    def chunk_at(chunk, start, size):
+        return w.at[pl.ds(pl.multiple_of(chunk * rows_chunk, rows_chunk), rows_chunk), pl.ds(start, size)]
+
+    pieces = [("normal", lambda chunk: gbuf.at[chunk])]
+    number = []
+    for kind, start, size in RANGES:
+        def at(chunk, start=start, size=size):
+            return chunk_at(chunk, start, size)
+
+        number.append(len(pieces))
+        pieces += [("own", at), ("other", at)] if kind == "across" else [("normal", at)]
     line = LineGather(p, pieces, line_sems)
     rows = Rows(p, part, relay, sums, row_sems)
+    hidden_cols = (COLS - GU) // 3
     writes = []
 
     def write(src, dst):
@@ -343,23 +465,58 @@
         copy.start()
         writes.append(copy)
 
+    local = [
+        pltpu.make_async_copy(wq, chunk_at(p.dp, QKV, 512), wsem.at[0]),
+        pltpu.make_async_copy(wk, kv.at[0], wsem.at[1]),
+        pltpu.make_async_copy(wv, kv.at[1], wsem.at[2]),
+        pltpu.make_async_copy(wo, wo_in, wsem.at[3]),
+        pltpu.make_async_copy(wg, chunk_at(p.dp, GU, hidden_cols), wsem.at[4]),
+        pltpu.make_async_copy(wu, chunk_at(p.dp, GU + hidden_cols, hidden_cols), wsem.at[5]),
+        pltpu.make_async_copy(wd, wd_in, wsem.at[6]),
+    ]
+    for copy in local:
+        copy.start()
+    mine_rows = pl.ds(pl.multiple_of(p.dp * rows_chunk, rows_chunk), rows_chunk)
+    each = attn_gain.shape[1]
+    lane = lax.broadcasted_iota(jnp.int32, (1, 128), 1)
+    spot = lax.rem(p.dp * T + p.t, 128 // each)
+    inside = (lane >= spot * each) & (lane < (spot + 1) * each)
+    for row, gain in enumerate((attn_gain, mlp_gain)):
+        value = jnp.concatenate([gain[...]] * (128 // each), axis=1)
+        gbuf[p.dp, row : row + 1, :] = jnp.where(inside, value, 0.0)
+    gbuf[p.dp, 2:8, :] = jnp.zeros((6, 128), F32)
     p.barrier(True)
     line.own(0)
-    line.own(1)
-    own_copies = []
+    for copy in local[0:3]:
+        copy.wait()
+    w[mine_rows, QKV + 512 : QKV + 640] = jnp.concatenate([kv[0], kv[1]], axis=1)
+    heads_piece, out_piece, gate_piece, up_piece, down_piece, down_last = number
+    line.own(heads_piece)
     for which in range(3):
         peers_copy(p, tokens, tok, tsend.at[0], trecv.at[0], which).start()
     pltpu.make_async_copy(tokens, tok.at[p.t], tsend.at[0, 3]).start()
-    line.own(2)
+    local[3].wait()
+    w[mine_rows, WO : WO + 512] = wo_in[...].T
+    line.own(out_piece)
     for which in range(3):
         peers_copy(p, cotangent, cot, tsend.at[1], trecv.at[1], which).start()
     pltpu.make_async_copy(cotangent, cot.at[p.t], tsend.at[1, 3]).start()
-    line.own(3)
+    for copy in local[4:6]:
+        copy.wait()
+    line.own(gate_piece)
     line.steps(0)
     line.arrive(0)
     for which in range(3):
         peers_copy(p, gbuf, gall, tsend.at[2], trecv.at[2], which).start()
     pltpu.make_async_copy(gbuf, gall.at[p.t], tsend.at[2, 3]).start()
+    fill_tables(
+        p, depth_row[...], depth_col[...], lengths, freqs[...], perm, back, back_own, cosine, sine, allowed, act_own, act_last
+    )
+    line.steps(heads_piece)
+    local[6].wait()
+    w[mine_rows, WD : WD + hidden_cols] = wd_in[...].T
+    line.own(up_piece)
+    line.steps(out_piece)
 
     def wait_peers(i, src, dst):
         for which in range(3):
@@ -390,10 +547,15 @@
     cown[...] = dot(mine, cot[...].reshape(T * own, width), NN)
     write(cown, cot_own)
 
-    line.steps(1)
-    line.own(4)
-    line.steps(2)
-    line.arrive(1)
+    line.own(down_piece)
+    line.own(down_last)
+
+    @pl.loop(0, T)
+    def _(owner):
+        picked = perm[pl.ds(pl.multiple_of(owner * OWN[0], 32), OWN[RECUR - 1]), :]
+        cot_all[owner] = dot(picked, cot[...].reshape(T * OWN[0], width), NN).astype(BF)
+
+    line.arrive(heads_piece)
 
     for level in range(RECUR):
         own = OWN[level]
@@ -427,12 +589,12 @@
             _, shares = attention_shares(query, key, allowed[level][b])
             out = dot(shares.astype(BF).reshape(8 * half, half), value, NN)
             heads.append(unstack_heads(out, half))
+            if level == 0:
+                line.step(gate_piece, 1) if b == 0 else [line.step(gate_piece, k) for k in range(2, p.line)]
         s["att"][...] = join_batches(heads, own).astype(BF)
         write(s["att"], saved_out[level]["att"])
         if level == 0:
-            line.own(5)
-            line.steps(3)
-            line.arrive(2)
+            line.arrive(out_piece)
         present = act_own[level, 0:own, :]
 
         def attention_tile(cols):
@@ -449,35 +611,40 @@
         rows.gather_start(2 * level, mixed)
         write(s["first"], saved_out[level]["first"])
         if level == 0:
-            line.own(6)
-            line.steps(4)
-            line.arrive(3)
+            line.steps(up_piece)
+            line.own(down_last + 1)
         rows.gather_finish(2 * level, mixed)
         write(s["mixed"], saved_out[level]["mixed"])
 
-        def gate_up(start, stop):
-            @pl.loop(start, stop)
-            def _(j):
-                cols = pl.ds(pl.multiple_of(j * 256, 256), 256)
-                wcols = pl.ds(pl.multiple_of(GU + j * 256, 128), 256)
-                pair = dot(s["mixed"][...].reshape(count, width), w[:, wcols], NN)
-                s["gu"][:, cols] = pair.astype(BF)
-                gate = pair[:, 0:128]
-                s["prod"][:, pl.ds(pl.multiple_of(j * 128, 128), 128)] = (
-                    gate * jax.nn.sigmoid(gate) * pair[:, 128:256]
-                ).astype(BF)
-
-        gate_up(0, 6)
+        def hidden_block(start, size):
+            x = s["mixed"][...].reshape(count, width)
+            gate = dot(x, w[:, pl.ds(pl.multiple_of(GU + start, 128), size)], NN)
+            upward = dot(x, w[:, pl.ds(pl.multiple_of(GU + hidden_cols + start, 128), size)], NN)
+            cols = pl.ds(pl.multiple_of(start, 128), size)
+            s["gu"][:, cols] = gate.astype(BF)
+            s["gu"][:, pl.ds(pl.multiple_of(hidden_cols + start, 128), size)] = upward.astype(BF)
+            s["prod"][:, cols] = (gate * jax.nn.sigmoid(gate) * upward).astype(BF)
+
         if level == 0:
-            line.steps(5)
-            line.arrive(4)
-        gate_up(6, 11)
+            line.steps(down_piece)
+            line.step(down_last, 1)
+            line.step(down_last + 1, 1)
+            line.arrive(gate_piece)
+            line.arrive(up_piece)
+
+        @pl.loop(0, hidden_cols // 256)
+        def _(j):
+            hidden_block(j * 256, 256)
+
+        if hidden_cols % 256:
+            hidden_block(hidden_cols // 256 * 256, 128)
         write(s["gu"], saved_out[level]["gu"])
         write(s["prod"], saved_out[level]["prod"])
         if level == 0:
-            line.steps(6)
-            line.arrive(5)
-            line.arrive(6)
+            for k in range(2, p.line):
+                line.step(down_last, k)
+                line.step(down_last + 1, k)
+            line.arrive(down_piece)
             write(w, w_out)
 
         def mlp_tile(cols):
@@ -499,14 +666,6 @@
             fin[0:own, :] = after[0:own, :].astype(BF)
         write(s["hidden"], saved_out[level]["hidden"])
         write(s["normed"], saved_out[level]["normed"])
-        if level == 0:
-            deepest = OWN[RECUR - 1]
-
-            @pl.loop(0, T)
-            def _(owner):
-                picked = perm[pl.ds(pl.multiple_of(owner * OWN[0], 32), deepest), :]
-                cot_all[owner] = dot(picked, cot[...].reshape(T * OWN[0], width), NN).astype(BF)
-
     write(fin, fin_out)
     for i in range(len(pieces)):
         line.drain(i)
@@ -514,72 +673,13 @@
         copy.wait()
 
 
-def static_tables():
-    batch, place = own_table()
-    batch_q = np.tile(batch, T)
-    rank_q = np.concatenate([place * T + t for t in range(T)])
-    level_ranks = []
-    for own in OWN:
-        level_ranks.append(np.concatenate([np.arange(own // 2) * T + t for t in range(T)]))
-    return batch_q.astype(np.int32), rank_q.astype(np.int32), [r.astype(np.int32) for r in level_ranks]
-
-
-def prologue(depth, lengths, tensor_index):
-    batch_q, rank_q, level_ranks = static_tables()
-    rows = depth.shape[1]
-    local = rows // T
-    index = jnp.arange(rows, dtype=jnp.int32)
-    earlier = (depth[:, None, :] > depth[:, :, None]) | (
-        (depth[:, None, :] == depth[:, :, None]) & (index[None, None, :] < index[None, :, None])
-    )
-    rank = jnp.sum(earlier.astype(jnp.int32), axis=2)
-    rank_col = rank.reshape(MB, T, local).transpose(1, 0, 2).reshape(-1)
-    batch_col = np.tile(np.repeat(np.arange(MB), local), T).astype(np.int32)
-    hit = (rank_col[None, :] == rank_q[:, None]) & (batch_col[None, :] == batch_q[:, None])
-    perm = hit.astype(BF)
-    back = (
-        (rank_col[:, None] == rank_q[None, :]) & (batch_col[:, None] == batch_q[None, :])
-    ).astype(BF)
-    ends = jnp.cumsum(lengths, axis=1)
-    starts = ends - lengths
-
-    def documents(position, ends_of, starts_of):
-        inside = position[..., None] >= ends_of
-        document = jnp.sum(inside.astype(jnp.int32), axis=-1)
-        start = jnp.max(jnp.where(position[..., None] >= starts_of, starts_of, 0), axis=-1)
-        return document, position - start
-
-    position_col = np.tile(np.arange(rows).reshape(T, 1, local), (1, MB, 1)).reshape(-1).astype(np.int32)
-    position = jnp.sum(jnp.where(hit, position_col[None, :], 0), axis=1)
-    ends_q = jnp.where(batch_q[:, None] == 0, ends[0][None], ends[1][None])
-    starts_q = jnp.where(batch_q[:, None] == 0, starts[0][None], starts[1][None])
-    _, offset = documents(position, ends_q, starts_q)
-    freqs = 10000.0 ** (-jnp.arange(0, HS, 2).astype(F32) / HS)
-    angles = offset.astype(F32)[:, None] * freqs[None, :]
-    cos, sin = jnp.cos(angles), jnp.sin(angles)
-    cosine = jnp.concatenate([cos] * 4, axis=1)
-    sine = jnp.concatenate([-sin, sin, -sin, sin], axis=1)
-    counts = [jnp.sum((depth >= level + 1).astype(jnp.int32), axis=1) for level in range(RECUR)]
-    masks, act = [], []
-    for level in range(RECUR):
-        ranks = level_ranks[level]
-        at = jnp.sum(jnp.where(rank[:, None, :] == ranks[None, :, None], index[None, None, :], 0), axis=2)
-        document, _ = documents(at, ends[:, None, :], starts[:, None, :])
-        ok = (document[:, :, None] == document[:, None, :]) & (at[:, None, :] <= at[:, :, None])
-        ok = ok & (ranks[None, None, :] < counts[level][:, None, None])
-        ok = ok | np.eye(len(ranks), dtype=bool)[None]
-        masks.append(ok.astype(F32))
-        limit = jnp.where(batch_q == 0, counts[level][0], counts[level][1])
-        act.append((rank_q < limit).astype(F32))
-    act = jnp.stack(act)
-    return perm, back, cosine, sine, masks, act
-
-
-def forward(n, tokens, cotangent, joined, gains, tables, tensor_index):
-    perm, back, cosine, sine, masks, act = tables
+def forward(n, tokens, depth, lengths, cotangent, weights, attn_gain, mlp_gain):
     width = tokens.shape[-1]
-    act_own = lax.dynamic_slice_in_dim(act, tensor_index * OWN[0], OWN[0], axis=1)[:, :, None]
-    hidden_cols = (COLS - GU) // 3
+    hidden_cols = weights[4].shape[1]
+    local = OWN[0] // MB
+    total = T * OWN[0]
+    ordered = depth.reshape(MB, T, local).transpose(1, 0, 2).astype(F32)
+    freqs = jnp.asarray(np.tile(10000.0 ** (-np.arange(0, HS, 2) / HS), 4)[None].astype(np.float32))
     vmem = pl.BlockSpec(memory_space=pltpu.VMEM)
     hbm = pl.BlockSpec(memory_space=pl.ANY)
 
@@ -598,11 +698,16 @@
 
     shapes = [((width, COLS), BF), ((8, width), F32), ((OWN[0], width), BF), ((OWN[0], width), F32), ((T, OWN[2], width), BF)]
     specs = [hbm, vmem, hbm, hbm, vmem]
+    shapes += [((total, 128), F32)] * 2 + [((OWN[0], total), BF), ((RECUR, OWN[0], 1), F32), ((T * OWN[2], 1), F32)]
+    shapes += [((MB, T * own // MB, T * own // MB), BF) for own in OWN]
+    specs += [vmem] * (5 + RECUR)
     for own in OWN:
         for entry in saved_shapes(own).values():
             shapes.append(entry)
             specs.append(hbm)
-    scratch = [pltpu.VMEM((width, COLS), BF), pltpu.VMEM((n, 8, 128), F32), pltpu.VMEM((T, n, 8, 128), F32)]
+    scratch = [pltpu.VMEM((width, COLS), BF)] + [pltpu.VMEM((total, total), BF)] * 2
+    scratch += [pltpu.VMEM((2,) + weights[1].shape, BF), pltpu.VMEM(weights[3].shape, BF), pltpu.VMEM(weights[6].shape, BF)]
+    scratch += [pltpu.VMEM((n, 8, 128), F32), pltpu.VMEM((T, n, 8, 128), F32)]
     scratch += [pltpu.VMEM((T,) + tokens.shape, BF)] * 2
     for own in OWN:
         scratch += [pltpu.VMEM(*entry) for entry in saved_shapes(own).values()]
@@ -612,44 +717,40 @@
         for _ in range(2):
             scratch += [pltpu.VMEM((2, own, width), BF), pltpu.VMEM((own, width), BF)]
     dma = pltpu.SemaphoreType.DMA
-    count = len(RANGES) + 1
-    scratch += [dma((count,))] + [dma((count, n // 2))] * 6
+    count = 1 + sum(2 if kind == "across" else 1 for kind, _, _ in RANGES)
+    scratch += [dma((count, n // 2))] * 6
     chunks = width // DC
     scratch += [dma((2 * RECUR, chunks))] * 4 + [dma((2 * RECUR, 3))] * 2
-    scratch += [dma((3, 4)), dma((3, 3)), dma((40,))]
+    scratch += [dma((7,)), dma((3, 4)), dma((3, 3)), dma((40,))]
     outs = pl.pallas_call(
         functools.partial(forward_kernel, n),
         out_shape=[jax.ShapeDtypeStruct(*entry) for entry in shapes],
-        in_specs=[hbm, hbm, hbm, hbm] + [vmem] * 7,
+        in_specs=[hbm] * 9 + [vmem] * 6,
         out_specs=specs,
         scratch_shapes=scratch,
         compiler_params=pltpu.CompilerParams(
             collective_id=1, has_side_effects=True, vmem_limit_bytes=62 << 20
         ),
-    )(tokens, cotangent, joined, gains, perm, cosine, sine, *masks, act_own)
+    )(
+        tokens,
+        cotangent,
+        *weights,
+        attn_gain[None],
+        mlp_gain[None],
+        ordered.reshape(1, total),
+        ordered.reshape(total, 1),
+        lengths,
+        freqs,
+    )
     w_all, gain, fin, cot_own, cot_all = outs[:5]
+    tables = dict(zip(("cosine", "sine", "back", "act", "act_last"), outs[5:10]))
+    tables["masks"] = outs[10:13]
     names = list(saved_shapes(1))
-    saved = [dict(zip(names, outs[5 + 8 * level : 13 + 8 * level])) for level in range(RECUR)]
-    return w_all, gain, fin, cot_own, cot_all, saved
-
-
-def join_weights(w_query, w_key, w_value, w_out, w_gate, w_up, w_down):
-    rows, hidden = w_gate.shape
-    pair = jnp.stack(
-        [w_gate.reshape(rows, hidden // 128, 128), w_up.reshape(rows, hidden // 128, 128)], axis=2
-    ).reshape(rows, 2 * hidden)
-    return jnp.concatenate([w_query, w_key, w_value, w_out.T, pair, w_down.T], axis=1)
-
-
-def place_gains(n, attn_gain, mlp_gain):
-    each = attn_gain.shape[0]
-    number = lax.axis_index("dp") * T + lax.axis_index("tensor")
-    block = jnp.zeros((8, 128), F32)
-    both = jnp.stack([attn_gain, mlp_gain])
-    return lax.dynamic_update_slice(block, both, (0, lax.rem(number * each, 128)))
-
-
-def attention_back(rotated, attended_grad, cos, sin, allowed, own):
+    saved = [dict(zip(names, outs[13 + 8 * level : 21 + 8 * level])) for level in range(RECUR)]
+    return w_all, gain, fin, cot_own, cot_all, tables, saved
+
+
+def attention_back(rotated, attended_grad, cos, sin, allowed, own, between=None):
     half = T * own // 2
     grads = []
     split = split_batches(rotated, own)
@@ -671,6 +772,8 @@
             key_grad += dot(score_grad, stacked, TN) * SCALE
         query_grad = jnp.concatenate(query_grads, axis=1)
         grads.append(jnp.concatenate([query_grad, key_grad, value_grad], axis=1))
+        if between is not None:
+            between()
     joined = join_batches(grads, own)
     tiles = []
     for j in range(5):
@@ -781,14 +884,13 @@
         def hidden_block(start, size):
             wcols = pl.ds(pl.multiple_of(WD + start, 128), size)
             product_grad = dot(dg[level][...].reshape(count, width), w[:, wcols], NN)
-            for h in range(size // 128):
-                at = pl.multiple_of(2 * start + 256 * h, 256)
-                gate = s["gu"][:, pl.ds(at, 128)].astype(F32)
-                upward = s["gu"][:, pl.ds(at + 128, 128)].astype(F32)
-                sigma = jax.nn.sigmoid(gate)
-                up = product_grad[:, 128 * h : 128 * h + 128]
-                gug[level][:, pl.ds(at, 128)] = (up * upward * sigma * (1.0 + gate * (1.0 - sigma))).astype(BF)
-                gug[level][:, pl.ds(at + 128, 128)] = (up * gate * sigma).astype(BF)
+            low = pl.ds(pl.multiple_of(start, 128), size)
+            high = pl.ds(pl.multiple_of(hidden_cols + start, 128), size)
+            gate = s["gu"][:, low].astype(F32)
+            upward = s["gu"][:, high].astype(F32)
+            sigma = jax.nn.sigmoid(gate)
+            gug[level][:, low] = (product_grad * upward * sigma * (1.0 + gate * (1.0 - sigma))).astype(BF)
+            gug[level][:, high] = (product_grad * gate * sigma).astype(BF)
 
         @pl.loop(0, hidden_cols // 256)
         def _(j):
@@ -844,15 +946,13 @@
         copy.wait()
 
 
-def backward(n, w_all, gain, cot_own, cot_all, tables, saved, tensor_index):
-    perm, back, cosine, sine, masks, act = tables
+def backward(n, w_all, gain, cot_own, cot_all, tables, saved):
     width = w_all.shape[0]
-    act_own = lax.dynamic_slice_in_dim(act, tensor_index * OWN[0], OWN[0], axis=1)[:, :, None]
-    act_last = act[RECUR - 1].reshape(T, OWN[0])[:, : OWN[2]].reshape(-1)[:, None]
     hidden_cols = (COLS - GU) // 3
     vmem = pl.BlockSpec(memory_space=pltpu.VMEM)
     hbm = pl.BlockSpec(memory_space=pl.ANY)
-    operands = [w_all, gain, cot_own, cot_all, cosine, sine, act_own, act_last, masks[1], masks[2]]
+    operands = [w_all, gain, cot_own, cot_all, tables["cosine"], tables["sine"], tables["act"], tables["act_last"]]
+    operands += list(tables["masks"][1:])
     specs = [hbm, vmem, hbm] + [vmem] * 7
     used = []
     for level in range(RECUR):
@@ -895,19 +995,25 @@
     }
 
 
-GRADS = (
-    ("down", 0, 768),
-    ("down", 768, 640),
-    ("gu", 0, 768),
-    ("gu", 768, 768),
-    ("gu", 1536, 768),
-    ("gu", 2304, 512),
-    ("out", 0, 512),
-    ("qkv", 0, 384),
-    ("qkv", 384, 256),
-)
-WIDEST = 768
-DEPTH = 2
+PIECE = 384
+SEGMENTS = (("down", 1408), ("gu", 2816), ("out", 512), ("qkv", 640))
+DEPTH = 3
+FIRST = 2
+PLACES = COLS // PIECE + FIRST
+
+
+def cut_pieces():
+    pieces = [[] for _ in range(COLS // PIECE)]
+    at = 0
+    for which, size in SEGMENTS:
+        done = 0
+        while done < size:
+            k, inside = divmod(at, PIECE)
+            cols = min(size - done, PIECE - inside)
+            pieces[k].append((which, done, cols, inside))
+            done += cols
+            at += cols
+    return pieces
 
 
 def gradient_kernel(n, *refs):
@@ -922,16 +1028,14 @@
     og_hbm, fin_all, grad_all = [next(it) for _ in range(3)]
     w = next(it)
     y = {name: next(it) for name in ("down", "gu", "out", "qkv")}
-    xm, xl = next(it), next(it)
+    xm, xl, xraw = next(it), next(it), next(it)
     og, hidden, qkv, grad, upstream, gains = [next(it) for _ in range(6)]
     gpeers = next(it)
     stage, landed, across, across_own = [next(it) for _ in range(4)]
     window_tmp = next(it)
     gmate_stage, gmate, gline, gline_own = [next(it) for _ in range(4)]
-    final = [next(it) for _ in range(2)]
-    finalt = next(it)
-    chunk_in, chunk_out = next(it), next(it)
-    fin_chunk = next(it)
+    final, turned, last_stage, last_landed, fsend, frecv = [next(it) for _ in range(6)]
+    chunk_in, fin_chunk, act_chunk, tok_chunk = [next(it) for _ in range(4)]
     part, relay = next(it), next(it)
     sums = [(next(it), next(it))]
     row_sems = [next(it) for _ in range(6)]
@@ -949,6 +1053,7 @@
     count = T * own
     starts = [0, T * OWN[0], T * (OWN[0] + OWN[1])]
     total_rows = T * sum(OWN)
+    hidden_cols = (COLS - GU) // 3
     loads, writes = {}, []
 
     def load(name, src, dst):
@@ -984,151 +1089,181 @@
     def level_slice(level):
         return pl.ds(sum(OWN[:level]) * T, OWN[level] * T)
 
-    def x_copy(which, chunk, buffer, slot, level, sem):
+    def x_copy(which, chunk, slot, level, sem):
         start = pl.multiple_of(chunk * chunk_rows // window * window, window)
         src = x_source(which, level).reshape(T * OWN[level], width)
         return pltpu.make_async_copy(
-            src.at[:, pl.ds(start, window)], buffer.at[slot, level_slice(level)], sem.at[slot, level]
+            src.at[:, pl.ds(start, window)], xraw.at[slot, level_slice(level)], sem.at[slot, level]
         )
 
-    def x_start(which, parity, buffer, sem):
+    pieces = cut_pieces()
+    count_pieces = len(pieces)
+    held = {}
+
+    def x_load(which, parity, buffer, sem):
+        if held.get(id(buffer)) == which:
+            return
+        held[id(buffer)] = which
+
         @pl.loop(0, line)
         def _(i):
             for level in range(RECUR):
-                x_copy(which, 2 * i + parity, buffer, i, level, sem).start()
-
-    def tile(k, chunk, buffer, slot, sem):
-        which, start, cols = GRADS[k]
-        for level in range(RECUR):
-            x_copy(which, chunk, buffer, slot, level, sem).wait()
-        value = dot(buffer[slot], y[which][:, start : start + cols], TN)
+                x_copy(which, 2 * i + parity, 0, level, sem).start()
+            for level in range(RECUR):
+                x_copy(which, 2 * i + parity, 0, level, sem).wait()
+            buffer[i] = xraw[0].T
+
+    def product(which, start, cols, chunk, buffer, slot):
+        value = dot(buffer[slot], y[which][:, start : start + cols], NN)
         if window == chunk_rows:
             return value
         window_tmp[:, 0:cols] = value
         shift = pl.multiple_of(lax.rem(chunk, window // chunk_rows) * chunk_rows, chunk_rows)
         return window_tmp[pl.ds(shift, chunk_rows), 0:cols]
 
-    offsets = np.cumsum([0] + [cols for _, _, cols in GRADS])
-
-    def mate_copy(k, i):
-        cols = GRADS[k][2]
+    places = []
+    for k in range(count_pieces):
+        places += [("own", k), ("other", k)] if k < FIRST else [("normal", k)]
+
+    def columns(q):
+        return pl.ds(pl.multiple_of(q * PIECE, 128), PIECE)
+
+    def mate_copy(q, i):
         return remote(
-            stage.at[k % DEPTH, i, :, pl.ds(0, cols)],
-            landed.at[i, :, pl.ds(int(offsets[k]), cols)],
-            msend.at[k, i],
-            mrecv.at[k, i],
-            p.mate,
+            stage.at[lax.rem(q, DEPTH), i], landed.at[i, :, columns(q)], msend.at[q, i], mrecv.at[q, i], p.mate
         )
 
     def mates(k):
-        which, start, cols = GRADS[k]
-        x_start(which, 1 - p.b, xm, xsem.at[0])
-        if k >= DEPTH:
+        q = k + FIRST
+        if q >= 2 * FIRST + DEPTH:
 
             @pl.loop(0, line)
             def _(i):
-                mate_copy(k - DEPTH, i).wait_send()
-
-        @pl.loop(0, line)
-        def _(i):
-            stage[k % DEPTH, i, :, 0:cols] = tile(k, 2 * i + 1 - p.b, xm, i, xsem.at[0]).astype(BF)
-            mate_copy(k, i).start()
-
-    def along(k, i, right):
-        cols = GRADS[k][2]
-        piece = pl.ds(int(offsets[k]), cols)
-        dst = across.at[i, :, piece]
+                mate_copy(q - DEPTH, i).wait_send()
+
+        for number, (which, start, cols, inside) in enumerate(pieces[k]):
+            x_load(which, 1 - p.b, xm, xsem.at[0])
+
+            @pl.loop(0, line)
+            def _(i):
+                value = product(which, start, cols, 2 * i + 1 - p.b, xm, i)
+                stage[q % DEPTH, i, :, inside : inside + cols] = value.astype(BF)
+                if number == len(pieces[k]) - 1:
+                    mate_copy(q, i).start()
+
+    def own_terms(q):
+        kind, k = places[q]
+        for number, (which, start, cols, inside) in enumerate(pieces[k]):
+            parity = 1 - p.b if kind == "other" else p.b
+            buffer, sem = (xm, xsem.at[0]) if kind == "other" else (xl, xsem.at[1])
+            x_load(which, parity, buffer, sem)
+            at = pl.ds(q * PIECE + inside, cols)
+
+            @pl.loop(0, line)
+            def _(i):
+                value = product(which, start, cols, 2 * i + parity, buffer, i)
+                if kind == "normal":
+                    if number == 0:
+                        mate_copy(q, i).wait_recv()
+                    value = value + landed[i, :, at].astype(F32)
+                landed[i, :, at] = value.astype(BF)
+
+    def along(q, i, right):
         return remote(
-            landed.at[i, :, piece], dst, lsend.at[k, i], lrecv.at[k, i], p.right if right else p.left
+            landed.at[i, :, columns(q)],
+            across.at[i, :, columns(q)],
+            lsend.at[q, i],
+            lrecv.at[q, i],
+            p.right if right else p.left,
         )
 
-    def along_last(k, i):
-        cols = GRADS[k][2]
-        piece = pl.ds(int(offsets[k]), cols)
+    def along_last(q, i):
         return remote(
-            landed.at[i, :, piece], across_own.at[:, piece], lsend.at[k, i], lrecv2.at[k], p.left
+            landed.at[i, :, columns(q)], across_own.at[:, columns(q)], lsend.at[q, i], lrecv2.at[q], p.left
         )
 
-    def lines(k, finish):
-        which, start, cols = GRADS[k]
-        piece = pl.ds(int(offsets[k]), cols)
-
-        @pl.loop(0, line)
-        def _(step):
-            odd = lax.rem(step, 2)
-            i = jnp.where(odd == 1, step // 2, line - 1 - step // 2)
-
-            @pl.when(i != p.a)
-            def _():
-                value = tile(k, 2 * i + p.b, xl, i, xsem.at[1])
-                mate_copy(k, i).wait_recv()
-                value = value + landed[i, :, piece].astype(F32)
-
-                def passed(value):
-                    landed[i, :, piece] = value.astype(BF)
-
-                inner = ((i > p.a) & p.has_left) | ((i < p.a) & p.has_right)
-
-                @pl.when(inner)
-                def _():
-                    along(k, i, True).wait_recv()
-                    passed(value + across[i, :, piece].astype(F32))
-
-                @pl.when(jnp.logical_not(inner))
-                def _():
-                    passed(value)
+    def relay_step(q, i, receives):
+        @pl.when(receives)
+        def _():
+            along(q, i, True).wait_recv()
+            landed[i, :, columns(q)] = (
+                landed[i, :, columns(q)].astype(F32) + across[i, :, columns(q)].astype(F32)
+            ).astype(BF)
+
+    def relay_pieces(slot):
+        q_right = slot - p.a
+        q_left = slot - (line - 1 - p.a)
+
+        @pl.when((q_right >= 0) & (q_right < PLACES))
+        def _():
+            @pl.loop(0, line)
+            def _(step):
+                i = line - 1 - step
 
                 @pl.when(i > p.a)
                 def _():
-                    along(k, i, True).start()
-
-                @pl.when((i < p.a) & (i < p.a - 1))
+                    relay_step(q_right, i, p.has_left)
+                    along(q_right, i, True).start()
+
+        @pl.when((q_left >= 0) & (q_left < PLACES))
+        def _():
+            @pl.loop(0, line)
+            def _(i):
+                @pl.when(i < p.a)
                 def _():
-                    along(k, i, False).start()
-
-                @pl.when((i < p.a) & (i == p.a - 1))
-                def _():
-                    along_last(k, i).start()
-
-        value = tile(k, 2 * p.a + p.b, xl, p.a, xsem.at[1])
-        mate_copy(k, p.a).wait_recv()
-        finish(value + landed[p.a, :, piece].astype(F32))
+                    relay_step(q_left, i, p.has_right)
+                    pl.when(i < p.a - 1)(lambda: along(q_left, i, False).start())
+                    pl.when(i == p.a - 1)(lambda: along_last(q_left, i).start())
+
+    def last_copy(j):
+        return remote(last_stage.at[j], last_landed.at[j], fsend.at[j], frecv.at[j], p.mate)
+
+    staged, turning = [], []
+
+    def line_sum(q, buffer):
+        here = pl.ds(q * PIECE, PIECE)
+        buffer[...] = landed[p.a, :, here].astype(F32)
 
         @pl.when(p.has_left)
         def _():
-            along(k, p.a, True).wait_recv()
-            finish(across[p.a, :, piece].astype(F32), True)
+            along(q, p.a, True).wait_recv()
+            buffer[...] += across[p.a, :, here].astype(F32)
 
         @pl.when(p.has_right)
         def _():
-            along_last(k, p.a).wait_recv()
-            finish(across_own[:, piece].astype(F32), True)
-
-    def drain(k):
-        @pl.loop(0, line)
-        def _(i):
-            if k >= len(GRADS) - DEPTH:
-                mate_copy(k, i).wait_send()
-
-            @pl.when(i != p.a)
-            def _():
-                along(k, i, True).wait_send()
-
-    staged, turned = {}, []
-
-    def store(k):
-        which, start, cols = GRADS[k]
-        buffer = final[k % 2]
-        for copy in staged.pop(k - 2, ()):
-            copy.wait()
-
-        def finish(value, more=False):
-            if more:
-                buffer[:, 0:cols] += value
-            else:
-                buffer[:, 0:cols] = value
-
-        lines(k, finish)
+            along_last(q, p.a).wait_recv()
+            buffer[...] += across_own[:, here].astype(F32)
+
+    def finish(q):
+        kind, k = places[q]
+        if kind == "own":
+            return
+        if kind == "other":
+            if len(staged) >= 2:
+                for copy in staged[len(staged) - 2]:
+                    copy.wait()
+                staged[len(staged) - 2] = []
+            buffer = final.at[len(staged) % 2]
+            line_sum(q, buffer)
+            last_stage[k] = buffer[...].astype(BF)
+            last_copy(k).start()
+        else:
+            results(q)
+        if q >= 3 and places[q - 3][0] == "own":
+            results(q - 3)
+
+    def results(q):
+        kind, k = places[q]
+        number = len(staged)
+        if number >= 2:
+            for copy in staged[number - 2]:
+                copy.wait()
+        buffer = final.at[number % 2]
+        line_sum(q, buffer)
+        if kind == "own":
+            last_copy(k).wait_recv()
+            buffer[...] += last_landed[k].astype(F32)
+            last_copy(k).wait_send()
         copies = []
 
         def out(src, dst):
@@ -1136,26 +1271,43 @@
             copy.start()
             copies.append(copy)
 
-        if which in ("down", "out"):
-            while turned:
-                turned.pop().wait()
-            finalt[0:cols, :] = buffer[:, 0:cols].T
-            target = dwd if which == "down" else dwo
-            out(finalt.at[pl.ds(0, cols)], target.at[pl.ds(start, cols)])
-            turned.extend(copies)
-            return
-        if which == "gu":
-            for j in range(cols // 256):
-                at = start // 2 + j * 128
-                out(buffer.at[:, pl.ds(j * 256, 128)], dgate.at[:, pl.ds(at, 128)])
-                out(buffer.at[:, pl.ds(j * 256 + 128, 128)], dup.at[:, pl.ds(at, 128)])
-        elif start == 0:
-            out(buffer.at[:, pl.ds(0, cols)], dq.at[:, pl.ds(0, cols)])
-        else:
-            out(buffer.at[:, pl.ds(0, 128)], dq.at[:, pl.ds(start, 128)])
-            dk[...] = buffer[:, 128:192]
-            dv[...] = buffer[:, 192:256]
-        staged[k] = copies
+        for which, start, cols, inside in pieces[k]:
+            if which in ("down", "out"):
+                for copy in turning:
+                    copy.wait()
+                turning.clear()
+                turned[inside : inside + cols, :] = buffer[:, inside : inside + cols].T
+                target = dwd if which == "down" else dwo
+                copy = pltpu.make_async_copy(
+                    turned.at[pl.ds(inside, cols)], target.at[pl.ds(start, cols)], finsem.at[k, 7]
+                )
+                copy.start()
+                turning.append(copy)
+            elif which == "gu":
+                middle = min(max(hidden_cols - start, 0), cols)
+                if middle:
+                    out(buffer.at[:, pl.ds(inside, middle)], dgate.at[:, pl.ds(start, middle)])
+                if middle < cols:
+                    out(
+                        buffer.at[:, pl.ds(inside + middle, cols - middle)],
+                        dup.at[:, pl.ds(start + middle - hidden_cols, cols - middle)],
+                    )
+            else:
+                queries = min(max(512 - start, 0), cols)
+                if queries:
+                    out(buffer.at[:, pl.ds(inside, queries)], dq.at[:, pl.ds(start, queries)])
+                if queries < cols:
+                    dk[...] = buffer[:, inside + queries : inside + queries + HS]
+                    dv[...] = buffer[:, inside + queries + HS : inside + queries + 2 * HS]
+        staged.append(copies)
+
+    def drain():
+        @pl.loop(0, PLACES)
+        def _(q):
+            @pl.loop(0, line)
+            def _(i):
+                pl.when(q >= max(PLACES - DEPTH, 2 * FIRST))(lambda: mate_copy(q, i).wait_send())
+                pl.when(i != p.a)(lambda: along(q, i, True).wait_send())
 
     loads["grad"].wait()
     present = act_own[0, 0:own, :]
@@ -1164,16 +1316,40 @@
     rows.gather_start(0, view)
     for level in range(RECUR):
         loads["down", level].wait()
-    mates(0)
+    sent = [FIRST]
+
+    def mates_upto(k):
+        while sent[0] <= min(k, count_pieces - 1):
+            mates(sent[0])
+            sent[0] += 1
+
+    slots = [0]
+
+    def slot():
+        s = slots[0]
+        slots[0] += 1
+        if s < PLACES:
+            own_terms(s)
+        relay_pieces(s)
+        if 0 <= s - line + 1 < PLACES:
+            finish(s - line + 1)
+        mates_upto(s - FIRST + DEPTH)
+
+    mates(FIRST)
+    sent[0] += 1
+    slot()
     rows.gather_finish(0, view)
     write(og, og_hbm)
-    mates(1)
+    for level in range(RECUR):
+        loads["gu", level].wait()
+    mates_upto(FIRST + 2)
     loads["w"].wait()
     loads["qkv"].wait()
     attended_grad = dot(og[...].reshape(count, width), w[:, WO : WO + 512], NN)
     y["qkv"][0:count, :] = attention_back(
-        qkv[...].astype(F32), attended_grad, cosine[...], sine[...], allowed, own
+        qkv[...].astype(F32), attended_grad, cosine[...], sine[...], allowed, own, slot
     ).astype(BF)
+    slot()
 
     def attention_tile(cols):
         return dot(y["qkv"][0:count, :], w[cols, QKV : QKV + 640], NT)
@@ -1193,7 +1369,6 @@
     pltpu.make_async_copy(grad, grad_all.at[p.t], tsend.at[1, 3]).start()
     gpeers[p.t] = gains[...]
     for level in range(RECUR):
-        loads["gu", level].wait()
         loads["out", level].wait()
     for level in (1, 2):
         loads["qkv", level].wait()
@@ -1211,7 +1386,7 @@
     def outputs():
         wait_peers(0, fin_in, fin_all)
         wait_peers(1, grad, grad_all)
-        mine = back[pl.ds(pl.multiple_of(p.t * own, own), own), :]
+        mine = back[...]
 
         @pl.loop(0, width // OC)
         def _(c):
@@ -1222,7 +1397,7 @@
             second.start()
             first.wait()
             second.wait()
-            act_out[:, :, cols] = dot(mine, fin_chunk[...].reshape(count, OC), NN).astype(BF).reshape(
+            act_chunk[...] = dot(mine, fin_chunk[...].reshape(count, OC), NN).astype(BF).reshape(
                 MB, own // MB, OC
             )
             value = chunk_in[...].reshape(count, OC)
@@ -1231,7 +1406,13 @@
             middle = rest.astype(BF)
             low = (rest - middle.astype(F32)).astype(BF)
             total = dot(mine, high, NN) + (dot(mine, middle, NN) + dot(mine, low, NN))
-            tok_out[:, :, cols] = total.reshape(MB, own // MB, OC)
+            tok_chunk[...] = total.reshape(MB, own // MB, OC)
+            third = pltpu.make_async_copy(act_chunk, act_out.at[:, :, cols], loadsem.at[0])
+            fourth = pltpu.make_async_copy(tok_chunk, tok_out.at[:, :, cols], loadsem.at[1])
+            third.start()
+            fourth.start()
+            third.wait()
+            fourth.wait()
 
     def gain_tile(chunk):
         start = pl.multiple_of(chunk * chunk_rows // window * window, window)
@@ -1242,7 +1423,7 @@
             + gpeers[3, :, pl.ds(start, window)]
         )
 
-    last = len(GRADS)
+    last = PLACES
 
     def gain_mate(i):
         return remote(gmate_stage.at[i], gmate.at[i], msend.at[last, i], mrecv.at[last, i], p.mate)
@@ -1301,28 +1482,22 @@
             gain_mate(i).wait_send()
             pl.when(i != p.a)(lambda: gain_along(i, True).wait_send())
 
-    for k in range(len(GRADS)):
-        x_start(GRADS[k][0], p.b, xl, xsem.at[1])
-        if k + DEPTH < len(GRADS):
-            mates(k + DEPTH)
-        if k == 1:
+    for s in range(slots[0], PLACES + line - 1):
+        slot()
+        if s == 5:
             gain_mates()
-        if k == 2:
+        if s == 6:
             gain_lines()
-        if k == 3:
+        if s == 8:
             outputs()
-        store(k)
-    for k in range(len(GRADS)):
-        drain(k)
-    for copies in list(staged.values()) + [turned]:
+    drain()
+    for copies in staged[-2:] + [turning]:
         for copy in copies:
             copy.wait()
 
 
-def gradients(n, w_all, gain, tables, saved, bwd, fin, tensor_index):
-    perm, back, cosine, sine, masks, act = tables
+def gradients(n, w_all, gain, tables, saved, bwd, fin):
     width = w_all.shape[0]
-    act_own = lax.dynamic_slice_in_dim(act, tensor_index * OWN[0], OWN[0], axis=1)[:, :, None]
     hidden_cols = (COLS - GU) // 3
     line = n // 2
     chunk_rows = width // n
@@ -1331,7 +1506,7 @@
     hbm = pl.BlockSpec(memory_space=pl.ANY)
     total_rows = T * sum(OWN)
     own = OWN[0]
-    operands = [w_all, gain, cosine, sine, act_own, masks[0], back]
+    operands = [w_all, gain, tables["cosine"], tables["sine"], tables["act"], tables["masks"][0], tables["back"]]
     specs = [hbm] + [vmem] * 6
     operands += [bwd["grad"], bwd["gain_part"], fin, saved[0]["hidden"], saved[0]["qkv"]]
     specs += [hbm, vmem, hbm, hbm, hbm]
@@ -1354,10 +1529,10 @@
         ((T, own, width), BF),
         ((T, own, width), F32),
     ]
-    out_specs = [vmem, vmem, hbm, vmem, vmem, hbm, hbm, hbm, hbm, vmem, hbm, hbm, hbm]
+    out_specs = [hbm, hbm, hbm, vmem, vmem, hbm, hbm, hbm, hbm, vmem, hbm, hbm, hbm]
     scratch = [pltpu.VMEM((width, GU), BF)]
     scratch += [pltpu.VMEM((total_rows, c), BF) for c in (hidden_cols, 2 * hidden_cols, 512, 640)]
-    scratch += [pltpu.VMEM((line, total_rows, window), BF)] * 2
+    scratch += [pltpu.VMEM((line, window, total_rows), BF)] * 2 + [pltpu.VMEM((1, total_rows, window), BF)]
     scratch += [
         pltpu.VMEM((T, own, width), BF),
         pltpu.VMEM((own, width), F32),
@@ -1368,25 +1543,27 @@
         pltpu.VMEM((T, 8, width), F32),
     ]
     scratch += [
-        pltpu.VMEM((DEPTH, line, chunk_rows, WIDEST), BF),
-        pltpu.VMEM((line, chunk_rows, COLS), BF),
-        pltpu.VMEM((line, chunk_rows, COLS), BF),
-        pltpu.VMEM((chunk_rows, COLS), BF),
-        pltpu.VMEM((window, WIDEST) if window > chunk_rows else (8, 128), F32),
+        pltpu.VMEM((DEPTH, line, chunk_rows, PIECE), BF),
+        pltpu.VMEM((line, chunk_rows, PLACES * PIECE), BF),
+        pltpu.VMEM((line, chunk_rows, PLACES * PIECE), BF),
+        pltpu.VMEM((chunk_rows, PLACES * PIECE), BF),
+        pltpu.VMEM((window, PIECE) if window > chunk_rows else (8, 128), F32),
     ]
     scratch += [pltpu.VMEM((line, 8, window), F32)] * 3 + [pltpu.VMEM((8, window), F32)]
-    scratch += [pltpu.VMEM((chunk_rows, WIDEST), F32)] * 2
-    scratch += [pltpu.VMEM((WIDEST, chunk_rows), F32)]
-    scratch += [pltpu.VMEM((T, own, OC), F32), pltpu.VMEM((8, 128), F32), pltpu.VMEM((T, own, OC), BF)]
+    scratch += [pltpu.VMEM((2, chunk_rows, PIECE), F32), pltpu.VMEM((PIECE, chunk_rows), F32)]
+    scratch += [pltpu.VMEM((FIRST, chunk_rows, PIECE), BF)] * 2
+    scratch += [pltpu.SemaphoreType.DMA((FIRST,))] * 2
+    scratch += [pltpu.VMEM((T, own, OC), F32), pltpu.VMEM((T, own, OC), BF)]
+    scratch += [pltpu.VMEM((MB, own // MB, OC), BF), pltpu.VMEM((MB, own // MB, OC), F32)]
     scratch += [pltpu.VMEM((2, 2, own, width), BF), pltpu.VMEM((own, width), BF)]
     scratch += [pltpu.VMEM((2, own, width), BF), pltpu.VMEM((own, width), BF)]
     dma = pltpu.SemaphoreType.DMA
     chunks = width // DC
-    k = len(GRADS) + 1
+    k = PLACES + 1
     scratch += [dma((1, chunks))] * 4 + [dma((1, 3))] * 2
     scratch += [dma((k, line))] * 4 + [dma((k,))]
     scratch += [dma((3, 4)), dma((3, 3))]
-    scratch += [dma((24,)), dma((2, line, RECUR)), dma((4,)), dma((k, 8)), dma((2,))]
+    scratch += [dma((24,)), dma((2, 2, RECUR)), dma((4,)), dma((k, 8)), dma((2,))]
     res = pl.pallas_call(
         functools.partial(gradient_kernel, n),
         out_shape=[jax.ShapeDtypeStruct(*entry) for entry in outs],
@@ -1404,12 +1581,11 @@
     tokens, depth, lengths, cotangent = args[:4]
     attn_gain, mlp_gain = args[11:]
     index = lax.axis_index("tensor")
-    tables = prologue(depth, lengths[:, 0], index)
-    joined = join_weights(*args[4:11])
-    gains = place_gains(n, attn_gain, mlp_gain)
-    w_all, gain, fin, cot_own, cot_all, saved = forward(n, tokens, cotangent, joined, gains, tables, index)
-    bwd = backward(n, w_all, gain, cot_own, cot_all, tables, saved, index)
-    res = gradients(n, w_all, gain, tables, saved, bwd, fin, index)
+    w_all, gain, fin, cot_own, cot_all, tables, saved = forward(
+        n, tokens, depth, lengths[:, 0], cotangent, args[4:11], attn_gain, mlp_gain
+    )
+    bwd = backward(n, w_all, gain, cot_own, cot_all, tables, saved)
+    res = gradients(n, w_all, gain, tables, saved, bwd, fin)
     activations, tokens_grad, dq, dk, dv, dwo, dgate, dup, dwd, gain_sum = res[:10]
     each = attn_gain.shape[0]
     window = gain_sum.shape[1]

time: 922 us -> 765 us (0.83)
  Pallas kernels: 860 us -> 736 us
  other arithmetic: 22.2 us -> 0.68 us
  local copies, waits for them, and re-layouts: 29.6 us -> 18.2 us
    pallas_call x1, Pallas kernels: 369 us -> 279 us  [gradients(): pl.pallas_call(functools.partial(gradient_kernel, n), out_shape=[jax.Shap...]
    pallas_call x1, Pallas kernels: 363 us -> 333 us  [forward(): pl.pallas_call(functools.partial(forward_kernel, n), out_shape=[jax.Shape...]
    unnamed x43 -> x23, local copies, waits for them, and re-layouts: 18.9 us -> 15.3 us
where the time goes in v2:
time: 765 us; the launch traced here: 756 us
  Pallas kernels  736 us (96%)
  local copies, waits for them, and re-layouts  18.2 us (2%)
    pallas_call x1, Pallas kernels, forward(): pl.pallas_call(functools.partial(forward_kernel, n), out_shape=[jax.Shape...  333 us
    pallas_call x1, Pallas kernels, gradients(): pl.pallas_call(functools.partial(gradient_kernel, n), out_shape=[jax.Shap...  279 us
    pallas_call x1, Pallas kernels, backward(): pl.pallas_call(functools.partial(backward_kernel, n), out_shape=[jax.Shap...  124 us
    unnamed x23, local copies, waits for them, and re-layouts  15.3 us

profile of v2, /device:TPU:0, one launch (start us, length us, event | category | flops | bytes accessed | tf_op | source)
XLA Modules:
  0.0 755.6 jit_solution(18401435519264216076)
XLA Ops:
  0.6 0.7 convert_element_type.9
  1.3 0.1 convert_element_type.10
  1.4 0.8 reshape.32.refs_12_
  2.2 0.6 reshape.30.refs_11_
  2.9 1.5 copy.31.refs_3_
  4.4 1.5 copy.32.refs_4_
  5.9 332.8 %shard_map.221 = (bf16[2048,5376]{1,0:T(8,128)(2,1)}, f32[8,2048]{1,0:T(8,128)}, bf16[96,2048]{1,0:T(8,128)(2,1)}, f32[96,2048]{1,0:T(8,128)}, bf16[4,48,2048]{2...) custom-call(bf16[2,48,2048]{2,1,0:T(8,128)(2,1)} %refs_0_.1, ...), custom_call_target="tpu_custom_call" | custom-call | tf_op jit(solution)/shard_map/pallas_call | solution.py:725
  338.7 124.0 %shard_map.222 = (bf16[4,96,2048]{2,1,0:T(8,128)(2,1)}, bf16[4,80,2048]{2,1,0:T(8,128)(2,1)}, bf16[4,48,2048]{2,1,0:T(8,128)(2,1)}, bf16[384,2816]{1,0:T(8,128)(...) custom-call(bf16[2048,5376]{1,0:T(8,128)(2,1)} %get-tuple-element.70, ...), custom_call_target="tpu_custom_call" | custom-call | tf_op jit(solution)/shard_map/pallas_call | solution.py:978
  462.7 278.7 %shard_map.223 = (bf16[2,48,2048]{2,1,0:T(8,128)(2,1)}, f32[2,48,2048]{2,1,0:T(8,128)}, f32[256,512]{1,0:T(8,128)}, f32[256,64]{1,0:T(8,128)}, f32[256,64]{1,0:T...) custom-call(bf16[2048,5376]{1,0:T(8,128)(2,1)} %get-tuple-element.70, ...), custom_call_target="tpu_custom_call" | custom-call | tf_op jit(solution)/shard_map/pallas_call | solution.py:1567
  741.4 0.0 copy-start.3
  741.4 0.0 copy-start.5
  741.4 0.8 constant_dynamic-slice_fusion
  742.3 0.5 slice_bitcast_fusion
  742.8 1.6 copy.34
  744.4 1.6 copy.35
  746.0 1.8 copy.45
  747.8 0.0 copy-done.3
  747.8 0.0 copy-start.4
  747.8 0.9 copy.46
  748.7 0.0 copy-done.5
  748.7 0.0 copy-start.2
  748.7 0.8 copy.47
  749.5 0.0 copy-done.4
  749.5 0.8 copy.48
  750.3 0.0 copy-done.2
  750.3 0.0 copy-start.1
  750.3 1.1 copy.49
  751.4 0.8 copy-done.1
  752.2 0.0 copy-start
  752.2 1.1 copy.50
  753.3 0.8 copy-done
  754.1 1.1 copy.51
  (1 shorter events, 0.0 us)
Async XLA Ops:
  741.4 6.4 copy-start.3
  741.4 7.3 copy-start.5
  747.8 1.7 copy-start.4
  748.7 1.6 copy-start.2
  750.3 1.9 copy-start.1
  752.2 1.9 copy-start

commit v3 on v2

--- a/solution.py
+++ b/solution.py
@@ -489,7 +489,7 @@
     line.own(0)
     for copy in local[0:3]:
         copy.wait()
-    w[mine_rows, QKV + 512 : QKV + 640] = jnp.concatenate([kv[0], kv[1]], axis=1)
+    w[mine_rows, QKV + 512 : QKV + 640] = jnp.concatenate([kv[0], kv[1]], axis=0).T
     heads_piece, out_piece, gate_piece, up_piece, down_piece, down_last = number
     line.own(heads_piece)
     for which in range(3):
@@ -706,7 +706,7 @@
             shapes.append(entry)
             specs.append(hbm)
     scratch = [pltpu.VMEM((width, COLS), BF)] + [pltpu.VMEM((total, total), BF)] * 2
-    scratch += [pltpu.VMEM((2,) + weights[1].shape, BF), pltpu.VMEM(weights[3].shape, BF), pltpu.VMEM(weights[6].shape, BF)]
+    scratch += [pltpu.VMEM((2,) + weights[1].shape[::-1], BF), pltpu.VMEM(weights[3].shape, BF), pltpu.VMEM(weights[6].shape, BF)]
     scratch += [pltpu.VMEM((n, 8, 128), F32), pltpu.VMEM((T, n, 8, 128), F32)]
     scratch += [pltpu.VMEM((T,) + tokens.shape, BF)] * 2
     for own in OWN:
@@ -734,7 +734,10 @@
     )(
         tokens,
         cotangent,
-        *weights,
+        weights[0],
+        weights[1].T,
+        weights[2].T,
+        *weights[3:],
         attn_gain[None],
         mlp_gain[None],
         ordered.reshape(1, total),
@@ -998,7 +1001,8 @@
 PIECE = 384
 SEGMENTS = (("down", 1408), ("gu", 2816), ("out", 512), ("qkv", 640))
 DEPTH = 3
-FIRST = 2
+FIRST = 1
+JOINT = 4
 PLACES = COLS // PIECE + FIRST
 
 
@@ -1113,13 +1117,13 @@
                 x_copy(which, 2 * i + parity, 0, level, sem).wait()
             buffer[i] = xraw[0].T
 
-    def product(which, start, cols, chunk, buffer, slot):
-        value = dot(buffer[slot], y[which][:, start : start + cols], NN)
+    def product(which, start, cols, parity, buffer, j):
+        some = buffer[pl.ds(j * JOINT, JOINT)].reshape(JOINT * window, total_rows)
+        value = dot(some, y[which][:, start : start + cols], NN).reshape(JOINT, window, cols)
         if window == chunk_rows:
             return value
-        window_tmp[:, 0:cols] = value
-        shift = pl.multiple_of(lax.rem(chunk, window // chunk_rows) * chunk_rows, chunk_rows)
-        return window_tmp[pl.ds(shift, chunk_rows), 0:cols]
+        window_tmp[:, :, 0:cols] = value
+        return window_tmp[:, pl.ds(pl.multiple_of(parity * chunk_rows, chunk_rows), chunk_rows), 0:cols]
 
     places = []
     for k in range(count_pieces):
@@ -1144,12 +1148,16 @@
         for number, (which, start, cols, inside) in enumerate(pieces[k]):
             x_load(which, 1 - p.b, xm, xsem.at[0])
 
-            @pl.loop(0, line)
-            def _(i):
-                value = product(which, start, cols, 2 * i + 1 - p.b, xm, i)
-                stage[q % DEPTH, i, :, inside : inside + cols] = value.astype(BF)
-                if number == len(pieces[k]) - 1:
-                    mate_copy(q, i).start()
+            last_part = number == len(pieces[k]) - 1
+
+            @pl.loop(0, line // JOINT)
+            def _(j):
+                value = product(which, start, cols, 1 - p.b, xm, j)
+                some = pl.ds(j * JOINT, JOINT)
+                stage[q % DEPTH, some, :, inside : inside + cols] = value.astype(BF)
+                if last_part:
+                    for i in range(JOINT):
+                        mate_copy(q, j * JOINT + i).start()
 
     def own_terms(q):
         kind, k = places[q]
@@ -1159,14 +1167,16 @@
             x_load(which, parity, buffer, sem)
             at = pl.ds(q * PIECE + inside, cols)
 
-            @pl.loop(0, line)
-            def _(i):
-                value = product(which, start, cols, 2 * i + parity, buffer, i)
+            @pl.loop(0, line // JOINT)
+            def _(j):
+                value = product(which, start, cols, parity, buffer, j)
+                some = pl.ds(j * JOINT, JOINT)
                 if kind == "normal":
                     if number == 0:
-                        mate_copy(q, i).wait_recv()
-                    value = value + landed[i, :, at].astype(F32)
-                landed[i, :, at] = value.astype(BF)
+                        for i in range(JOINT):
+                            mate_copy(q, j * JOINT + i).wait_recv()
+                    value = value + landed[some, :, at].astype(F32)
+                landed[some, :, at] = value.astype(BF)
 
     def along(q, i, right):
         return remote(
@@ -1297,8 +1307,9 @@
                 if queries:
                     out(buffer.at[:, pl.ds(inside, queries)], dq.at[:, pl.ds(start, queries)])
                 if queries < cols:
-                    dk[...] = buffer[:, inside + queries : inside + queries + HS]
-                    dv[...] = buffer[:, inside + queries + HS : inside + queries + 2 * HS]
+                    both = buffer[:, inside + queries : inside + queries + 2 * HS].T
+                    dk[...] = both[0:HS]
+                    dv[...] = both[HS : 2 * HS]
         staged.append(copies)
 
     def drain():
@@ -1518,8 +1529,8 @@
         ((MB, own // MB, width), BF),
         ((MB, own // MB, width), F32),
         ((chunk_rows, 512), F32),
-        ((chunk_rows, HS), F32),
-        ((chunk_rows, HS), F32),
+        ((HS, chunk_rows), F32),
+        ((HS, chunk_rows), F32),
         ((512, chunk_rows), F32),
         ((chunk_rows, hidden_cols), F32),
         ((chunk_rows, hidden_cols), F32),
@@ -1547,7 +1558,7 @@
         pltpu.VMEM((line, chunk_rows, PLACES * PIECE), BF),
         pltpu.VMEM((line, chunk_rows, PLACES * PIECE), BF),
         pltpu.VMEM((chunk_rows, PLACES * PIECE), BF),
-        pltpu.VMEM((window, PIECE) if window > chunk_rows else (8, 128), F32),
+        pltpu.VMEM((JOINT, window, PIECE) if window > chunk_rows else (1, 8, 128), F32),
     ]
     scratch += [pltpu.VMEM((line, 8, window), F32)] * 3 + [pltpu.VMEM((8, window), F32)]
     scratch += [pltpu.VMEM((2, chunk_rows, PIECE), F32), pltpu.VMEM((PIECE, chunk_rows), F32)]
@@ -1577,6 +1588,23 @@
     return res
 
 
+def hand_out_kernel(count, *refs):
+    for i in range(count):
+        refs[count + i][...] = refs[i][...]
+
+
+def hand_out(values):
+    vmem = pl.BlockSpec(memory_space=pltpu.VMEM)
+    count = len(values)
+    return pl.pallas_call(
+        functools.partial(hand_out_kernel, count),
+        out_shape=[jax.ShapeDtypeStruct(v.shape, v.dtype) for v in values],
+        in_specs=[vmem] * count,
+        out_specs=[vmem] * count,
+        compiler_params=pltpu.CompilerParams(vmem_limit_bytes=40 << 20),
+    )(*values)
+
+
 def shards(n, *args):
     tokens, depth, lengths, cotangent = args[:4]
     attn_gain, mlp_gain = args[11:]
@@ -1586,12 +1614,13 @@
     )
     bwd = backward(n, w_all, gain, cot_own, cot_all, tables, saved)
     res = gradients(n, w_all, gain, tables, saved, bwd, fin)
-    activations, tokens_grad, dq, dk, dv, dwo, dgate, dup, dwd, gain_sum = res[:10]
+    gain_sum = res[9]
+    activations, tokens_grad, dq, dk, dv, dwo, dgate, dup, dwd = hand_out(res[:9])
     each = attn_gain.shape[0]
     window = gain_sum.shape[1]
     start = lax.rem((lax.axis_index("dp") * T + index) * each, window)
     both = lax.dynamic_slice_in_dim(gain_sum, start, each, axis=1)
-    return (activations, tokens_grad, dq, dk, dv, dwo, dgate, dup, dwd, both[0], both[1])
+    return (activations, tokens_grad, dq, dk.T, dv.T, dwo, dgate, dup, dwd, both[0], both[1])
 
 
 def solution(mesh):

time: 765 us -> 750 us (0.980)
  Pallas kernels: 736 us -> 727 us
    pallas_call x1, Pallas kernels: 279 us -> 267 us  [gradients(): pl.pallas_call(functools.partial(gradient_kernel, n), out_shape=[jax.Shap...]
    unnamed x23 -> x20, local copies, waits for them, and re-layouts: 15.3 us -> 9.97 us
where the time goes in v3:
time: 750 us; the launch traced here: 740 us
  Pallas kernels  727 us (97%)
  local copies, waits for them, and re-layouts  12.1 us (2%)
    pallas_call x1, Pallas kernels, forward(): pl.pallas_call(functools.partial(forward_kernel, n), out_shape=[jax.Shape...  333 us
    pallas_call x1, Pallas kernels, gradients(): pl.pallas_call(functools.partial(gradient_kernel, n), out_shape=[jax.Shap...  267 us
    pallas_call x1, Pallas kernels, backward(): pl.pallas_call(functools.partial(backward_kernel, n), out_shape=[jax.Shap...  124 us

profile of v3, /device:TPU:0, one launch (start us, length us, event | category | flops | bytes accessed | tf_op | source)
XLA Modules:
  0.0 740.5 jit_solution(13784122024572700647)
XLA Ops:
  0.6 0.7 convert_element_type.9
  1.3 0.1 convert_element_type.10
  1.4 0.8 reshape.32.refs_12_
  2.2 0.6 reshape.30.refs_11_
  2.9 332.8 %shard_map.221 = (bf16[2048,5376]{1,0:T(8,128)(2,1)}, f32[8,2048]{1,0:T(8,128)}, bf16[96,2048]{1,0:T(8,128)(2,1)}, f32[96,2048]{1,0:T(8,128)}, bf16[4,48,2048]{2...) custom-call(bf16[2,48,2048]{2,1,0:T(8,128)(2,1)} %refs_0_.1, ...), custom_call_target="tpu_custom_call" | custom-call | tf_op jit(solution)/shard_map/pallas_call | solution.py:725
  335.7 124.0 %shard_map.222 = (bf16[4,96,2048]{2,1,0:T(8,128)(2,1)}, bf16[4,80,2048]{2,1,0:T(8,128)(2,1)}, bf16[4,48,2048]{2,1,0:T(8,128)(2,1)}, bf16[384,2816]{1,0:T(8,128)(...) custom-call(bf16[2048,5376]{1,0:T(8,128)(2,1)} %get-tuple-element.79, ...), custom_call_target="tpu_custom_call" | custom-call | tf_op jit(solution)/shard_map/pallas_call | solution.py:981
  459.7 266.5 %shard_map.223 = (bf16[2,48,2048]{2,1,0:T(8,128)(2,1)}, f32[2,48,2048]{2,1,0:T(8,128)}, f32[256,512]{1,0:T(8,128)}, f32[64,256]{1,0:T(8,128)}, f32[64,256]{1,0:T...) custom-call(bf16[2048,5376]{1,0:T(8,128)(2,1)} %get-tuple-element.79, ...), custom_call_target="tpu_custom_call" | custom-call | tf_op jit(solution)/shard_map/pallas_call | solution.py:1578
  726.2 0.0 copy-start
  726.2 1.4 copy-done
  727.6 0.0 copy-start.1
  727.6 1.4 copy-done.1
  728.9 0.0 copy-start.2
  728.9 1.4 copy-done.2
  730.3 0.0 copy-start.3
  730.3 1.1 copy-done.3
  731.4 0.0 copy-start.4
  731.4 1.0 copy-done.4
  732.5 0.0 copy-start.5
  732.5 1.0 copy-done.5
  733.5 0.0 copy-start.6
  733.5 1.0 copy-done.6
  734.5 0.0 copy-start.7
  734.5 0.8 copy-done.7
  735.4 0.0 copy-start.8
  735.4 0.8 copy-done.8
  736.2 0.0 copy-start.9
  736.2 3.3 shard_map.224
  739.4 0.0 copy-done.9
  739.5 0.1 constant_dynamic-slice_fusion
  739.5 0.5 slice_bitcast_fusion
  (1 shorter events, 0.0 us)
Async XLA Ops:
  726.2 1.4 copy-start
  727.6 1.4 copy-start.1
  728.9 1.4 copy-start.2
  730.3 1.1 copy-start.3
  731.4 1.0 copy-start.4
  732.5 1.0 copy-start.5
  733.5 1.0 copy-start.6
  734.5 0.8 copy-start.7
  735.4 0.8 copy-start.8
  736.2 3.3 copy-start.9

commit v4 on v3

--- a/solution.py
+++ b/solution.py
@@ -209,7 +209,7 @@
         cols = pl.ds(pl.multiple_of(c * DC, DC), DC)
         return remote(
             self.part.at[:, 1 - p.lo, pl.ds(0, own), cols],
-            self.sums[i][0].at[:, :, cols],
+            self.sums[i][0].at[:, pl.ds(0, own), cols],
             self.s1.at[i, c],
             self.q1.at[i, c],
             p.near,
@@ -220,7 +220,7 @@
         cols = pl.ds(pl.multiple_of(c * DC, DC), DC)
         return remote(
             self.relay.at[pl.ds(0, own), cols],
-            self.sums[i][1].at[:, cols],
+            self.sums[i][1].at[pl.ds(0, own), cols],
             self.s2.at[i, c],
             self.q2.at[i, c],
             p.far,
@@ -236,7 +236,7 @@
             cols = pl.ds(pl.multiple_of(c * DC, DC), DC)
             self.first_copy(i, own, c).wait_recv()
             mine = part[1 - p.hi, p.lo, 0:own, cols].astype(F32)
-            relay[0:own, cols] = (mine + r1[1 - p.hi, :, cols].astype(F32)).astype(BF)
+            relay[0:own, cols] = (mine + r1[1 - p.hi, 0:own, cols].astype(F32)).astype(BF)
             self.second_copy(i, own, c).start()
 
         @pl.loop(0, chunks)
@@ -253,7 +253,7 @@
             cols = pl.ds(pl.multiple_of(c * DC, DC), DC)
             self.second_copy(i, own, c).wait_recv()
             mine = part[p.hi, p.lo, 0:own, cols].astype(F32)
-            finish(cols, mine + r1[p.hi, :, cols].astype(F32) + r2[:, cols].astype(F32))
+            finish(cols, mine + r1[p.hi, 0:own, cols].astype(F32) + r2[0:own, cols].astype(F32))
 
         @pl.loop(0, chunks)
         def _(c):
@@ -647,14 +647,15 @@
             line.arrive(down_piece)
             write(w, w_out)
 
-        def mlp_tile(cols):
-            return dot(s["prod"][...], w[cols, WD : WD + 1408], NT)
-
-        def mlp_finish(cols, total):
-            after[0:own, cols] = s["first"][:, cols] + present * total
-
-        rows.reduce(2 * level + 1, own, mlp_tile, mlp_finish)
         if level < RECUR - 1:
+
+            def mlp_tile(cols):
+                return dot(s["prod"][...], w[cols, WD : WD + 1408], NT)
+
+            def mlp_finish(cols, total):
+                after[0:own, cols] = s["first"][:, cols] + present * total
+
+            rows.reduce(2 * level + 1, own, mlp_tile, mlp_finish)
             deeper = OWN[level + 1]
             hidden = after[0:deeper, :]
             saved[level + 1]["hidden"][...] = hidden
@@ -662,10 +663,10 @@
             saved[level + 1]["normed"][p.t] = (hidden * inverse * gain_out[0:1, :]).astype(BF)
             rows.gather_start(2 * level + 1, saved[level + 1]["normed"].reshape(2, 2, deeper, width))
             fin[deeper:own, :] = after[deeper:own, :].astype(BF)
-        else:
-            fin[0:own, :] = after[0:own, :].astype(BF)
+
         write(s["hidden"], saved_out[level]["hidden"])
         write(s["normed"], saved_out[level]["normed"])
+    fin[0 : OWN[2], :] = jnp.zeros((OWN[2], width), BF)
     write(fin, fin_out)
     for i in range(len(pieces)):
         line.drain(i)
@@ -753,18 +754,21 @@
     return w_all, gain, fin, cot_own, cot_all, tables, saved
 
 
-def attention_back(rotated, attended_grad, cos, sin, allowed, own, between=None):
+def share_groups(block, allowed):
+    query, key = block[:, 0:512].astype(BF), block[:, 512:576].astype(BF)
+    for start in range(0, 512, HEADS * HS):
+        yield (start,) + attention_shares(query[:, start : start + HEADS * HS], key, allowed)
+
+
+def attention_back(rotated, groups, attended_grad, cos, sin, own, between=None):
     half = T * own // 2
     grads = []
-    split = split_batches(rotated, own)
     upstream = split_batches(attended_grad, own)
     for b in range(MB):
-        block = split[b]
-        query, key, value = block[:, 0:512].astype(BF), block[:, 512:576].astype(BF), block[:, 576:640].astype(BF)
+        key, value = rotated[b][:, 512:576].astype(BF), rotated[b][:, 576:640].astype(BF)
         up_all = upstream[b].astype(BF)
         query_grads, key_grad, value_grad = [], 0.0, 0.0
-        for start in range(0, 512, HEADS * HS):
-            stacked, shares = attention_shares(query[:, start : start + HEADS * HS], key, allowed[b])
+        for start, stacked, shares in groups[b]:
             up = stack_heads(up_all[:, start : start + HEADS * HS])
             low = shares.astype(BF).reshape(HEADS * half, half)
             shares_grad = dot(up, value, NT).reshape(HEADS, half, half)
@@ -822,7 +826,7 @@
     gug = [next(it) for _ in range(3)]
     og = [None] + [next(it) for _ in range(2)]
     qkvg = [None] + [next(it) for _ in range(2)]
-    grad, upstream = next(it), next(it)
+    grad, upstream, factors = next(it), next(it), next(it)
     part, relay = next(it), next(it)
     sums = [(next(it), next(it)) for _ in range(5)]
     row_sems = [next(it) for _ in range(6)]
@@ -878,22 +882,31 @@
             dg[level][p.t] = (present * grad[0:own, :]).astype(BF)
             view = dg[level].reshape(2, 2, own, width)
             rows.gather_start(base, view)
+        loads["gu", level].wait()
+
+        @pl.loop(0, hidden_cols // 128)
+        def _(j):
+            low = pl.ds(pl.multiple_of(j * 128, 128), 128)
+            high = pl.ds(pl.multiple_of(hidden_cols + j * 128, 128), 128)
+            gate = s["gu"][:, low].astype(F32)
+            upward = s["gu"][:, high].astype(F32)
+            sigma = jax.nn.sigmoid(gate)
+            factors[0:count, low] = upward * sigma * (1.0 + gate * (1.0 - sigma))
+            factors[0:count, high] = gate * sigma
+
+        if level == last:
+            loads["w", WD].wait()
+        else:
             rows.gather_finish(base, view)
         write(dg[level], dg_out[level])
-        if level == last:
-            loads["w", WD].wait()
-        loads["gu", level].wait()
 
         def hidden_block(start, size):
             wcols = pl.ds(pl.multiple_of(WD + start, 128), size)
             product_grad = dot(dg[level][...].reshape(count, width), w[:, wcols], NN)
             low = pl.ds(pl.multiple_of(start, 128), size)
             high = pl.ds(pl.multiple_of(hidden_cols + start, 128), size)
-            gate = s["gu"][:, low].astype(F32)
-            upward = s["gu"][:, high].astype(F32)
-            sigma = jax.nn.sigmoid(gate)
-            gug[level][:, low] = (product_grad * upward * sigma * (1.0 + gate * (1.0 - sigma))).astype(BF)
-            gug[level][:, high] = (product_grad * gate * sigma).astype(BF)
+            gug[level][:, low] = (product_grad * factors[0:count, low]).astype(BF)
+            gug[level][:, high] = (product_grad * factors[0:count, high]).astype(BF)
 
         @pl.loop(0, hidden_cols // 256)
         def _(j):
@@ -921,16 +934,16 @@
         og[level][p.t] = (present * grad[0:own, :]).astype(BF)
         view = og[level].reshape(2, 2, own, width)
         rows.gather_start(base + 1, view)
+        loads["qkv", level].wait()
+        rotated = split_batches(s["qkv"][...].astype(F32), own)
+        groups = [list(share_groups(rotated[b], allowed[level][b])) for b in range(MB)]
         rows.gather_finish(base + 1, view)
         write(og[level], og_out[level])
         if level == last:
             loads["w", WO].wait()
-        loads["qkv", level].wait()
         attended_grad = dot(og[level][...].reshape(count, width), w[:, WO : WO + 512], NN)
         cos, sin = level_rows(cosine, own), level_rows(sine, own)
-        qkvg[level][...] = attention_back(
-            s["qkv"][...].astype(F32), attended_grad, cos, sin, allowed[level], own
-        ).astype(BF)
+        qkvg[level][...] = attention_back(rotated, groups, attended_grad, cos, sin, own).astype(BF)
         write(qkvg[level], qkvg_out[level])
         if level == last:
             loads["w", QKV].wait()
@@ -971,7 +984,7 @@
     scratch += [pltpu.VMEM(*entry) for entry in outs]
     outs += [((OWN[0], width), F32), ((8, width), F32)]
     out_specs = [hbm] * (len(outs) - 1) + [vmem]
-    scratch += [pltpu.VMEM((OWN[0], width), F32)] * 2
+    scratch += [pltpu.VMEM((OWN[0], width), F32)] * 2 + [pltpu.VMEM((T * OWN[0], 2 * hidden_cols), F32)]
     scratch += [pltpu.VMEM((2, 2, OWN[0], width), BF), pltpu.VMEM((OWN[0], width), BF)]
     for own in (OWN[2], OWN[2], OWN[1], OWN[1], OWN[0]):
         scratch += [pltpu.VMEM((2, own, width), BF), pltpu.VMEM((own, width), BF)]
@@ -1002,7 +1015,7 @@
 SEGMENTS = (("down", 1408), ("gu", 2816), ("out", 512), ("qkv", 640))
 DEPTH = 3
 FIRST = 1
-JOINT = 4
+JOINT = 2
 PLACES = COLS // PIECE + FIRST
 
 
@@ -1023,7 +1036,7 @@
 def gradient_kernel(n, *refs):
     it = iter(refs)
     (w_all, gain, cosine, sine, act_own, allowed, back) = [next(it) for _ in range(7)]
-    grad_in, gain_in, fin_in, hidden_in, qkv_in = [next(it) for _ in range(5)]
+    grad_in, gain_in, fin_in, hidden_in, qkv_in, first_in = [next(it) for _ in range(6)]
     x_in = {name: [next(it) for _ in range(3)] for name in ("down", "gu", "qkv")}
     x_in["out"] = [None] + [next(it) for _ in range(2)]
     y_in = {name: [next(it) for _ in range(3)] for name in ("down", "gu", "out")}
@@ -1034,6 +1047,7 @@
     y = {name: next(it) for name in ("down", "gu", "out", "qkv")}
     xm, xl, xraw = next(it), next(it), next(it)
     og, hidden, qkv, grad, upstream, gains = [next(it) for _ in range(6)]
+    fin, first = next(it), next(it)
     gpeers = next(it)
     stage, landed, across, across_own = [next(it) for _ in range(4)]
     window_tmp = next(it)
@@ -1041,7 +1055,7 @@
     final, turned, last_stage, last_landed, fsend, frecv = [next(it) for _ in range(6)]
     chunk_in, fin_chunk, act_chunk, tok_chunk = [next(it) for _ in range(4)]
     part, relay = next(it), next(it)
-    sums = [(next(it), next(it))]
+    sums = [(next(it), next(it))] * 2
     row_sems = [next(it) for _ in range(6)]
     msend, mrecv, lsend, lrecv, lrecv2 = [next(it) for _ in range(5)]
     tsend, trecv = next(it), next(it)
@@ -1075,6 +1089,8 @@
         for level in range(RECUR):
             load((name, level), y_in[name][level], y[name].at[pl.ds(starts[level], T * OWN[level])])
     load("w", w_all.at[:, pl.ds(0, GU)], w)
+    load("fin", fin_in, fin)
+    load("first", first_in, first)
     load("qkv", qkv_in, qkv)
     load("hidden", hidden_in, hidden)
     for level in range(RECUR):
@@ -1083,10 +1099,6 @@
         load(("qkv", level), y_in["qkv"][level], y["qkv"].at[pl.ds(starts[level], T * OWN[level])])
     p.barrier(True)
 
-    for which in range(3):
-        peers_copy(p, fin_in, fin_all, tsend.at[0], trecv.at[0], which).start()
-    pltpu.make_async_copy(fin_in, fin_all.at[p.t], tsend.at[0, 3]).start()
-
     def x_source(which, level):
         return og_hbm if which == "out" and level == 0 else x_in[which][level]
 
@@ -1109,13 +1121,19 @@
             return
         held[id(buffer)] = which
 
+        for level in range(RECUR):
+            x_copy(which, parity, 0, level, sem).start()
+
         @pl.loop(0, line)
         def _(i):
+            @pl.when(i + 1 < line)
+            def _():
+                for level in range(RECUR):
+                    x_copy(which, 2 * (i + 1) + parity, lax.rem(i + 1, 2), level, sem).start()
+
             for level in range(RECUR):
-                x_copy(which, 2 * i + parity, 0, level, sem).start()
-            for level in range(RECUR):
-                x_copy(which, 2 * i + parity, 0, level, sem).wait()
-            buffer[i] = xraw[0].T
+                x_copy(which, 2 * i + parity, lax.rem(i, 2), level, sem).wait()
+            buffer[i] = xraw[lax.rem(i, 2)].T
 
     def product(which, start, cols, parity, buffer, j):
         some = buffer[pl.ds(j * JOINT, JOINT)].reshape(JOINT * window, total_rows)
@@ -1357,8 +1375,10 @@
     loads["w"].wait()
     loads["qkv"].wait()
     attended_grad = dot(og[...].reshape(count, width), w[:, WO : WO + 512], NN)
+    rotated = split_batches(qkv[...].astype(F32), own)
+    groups = [share_groups(rotated[b], allowed[b]) for b in range(MB)]
     y["qkv"][0:count, :] = attention_back(
-        qkv[...].astype(F32), attended_grad, cosine[...], sine[...], allowed, own, slot
+        rotated, groups, attended_grad, cosine[...], sine[...], own, slot
     ).astype(BF)
     slot()
 
@@ -1394,9 +1414,43 @@
         if local:
             pltpu.make_async_copy(src, dst.at[p.t], tsend.at[i, 3]).wait()
 
+    def last_branch():
+        wait_peers(1, grad, grad_all)
+        loads["fin"].wait()
+        loads["first"].wait()
+        deepest = OWN[2]
+        active = act_own[RECUR - 1, 0:deepest, :]
+
+        def fetch(src, dst, i):
+            return pltpu.make_async_copy(src, dst, loadsem.at[i])
+
+        def last_tile(cols):
+            some = pl.ds(cols.start, DC)
+            copies = (
+                fetch(w_all.at[some, pl.ds(WD, GU)], w.at[pl.ds(0, DC)], 0),
+                fetch(
+                    w_all.at[some, pl.ds(WD + GU, hidden_cols - GU)],
+                    w.at[pl.ds(DC, DC), pl.ds(0, hidden_cols - GU)],
+                    1,
+                ),
+            )
+            for copy in copies:
+                copy.start()
+            for copy in copies:
+                copy.wait()
+            left = y["down"][starts[2] : starts[2] + T * deepest, :]
+            return dot(left[:, 0:GU], w[0:DC, :], NT) + dot(left[:, GU:], w[DC : 2 * DC, 0 : hidden_cols - GU], NT)
+
+        def last_finish(cols, total):
+            fin[0:deepest, cols] = (first[:, cols] + active * total).astype(BF)
+
+        rows.reduce(1, deepest, last_tile, last_finish)
+        for which in range(3):
+            peers_copy(p, fin, fin_all, tsend.at[0], trecv.at[0], which).start()
+        pltpu.make_async_copy(fin, fin_all.at[p.t], tsend.at[0, 3]).start()
+
     def outputs():
-        wait_peers(0, fin_in, fin_all)
-        wait_peers(1, grad, grad_all)
+        wait_peers(0, fin, fin_all)
         mine = back[...]
 
         @pl.loop(0, width // OC)
@@ -1497,9 +1551,11 @@
         slot()
         if s == 5:
             gain_mates()
-        if s == 6:
+        if s == 7:
             gain_lines()
-        if s == 8:
+        if s == 9:
+            last_branch()
+        if s == 11:
             outputs()
     drain()
     for copies in staged[-2:] + [turning]:
@@ -1519,8 +1575,8 @@
     own = OWN[0]
     operands = [w_all, gain, tables["cosine"], tables["sine"], tables["act"], tables["masks"][0], tables["back"]]
     specs = [hbm] + [vmem] * 6
-    operands += [bwd["grad"], bwd["gain_part"], fin, saved[0]["hidden"], saved[0]["qkv"]]
-    specs += [hbm, vmem, hbm, hbm, hbm]
+    operands += [bwd["grad"], bwd["gain_part"], fin, saved[0]["hidden"], saved[0]["qkv"], saved[RECUR - 1]["first"]]
+    specs += [hbm, vmem, hbm, hbm, hbm, hbm]
     streams = list(bwd["dg"]) + [s["mixed"] for s in saved] + [s["normed"] for s in saved] + list(bwd["og"])
     streams += [s["prod"] for s in saved] + list(bwd["gug"]) + [s["att"] for s in saved] + list(bwd["qkvg"])
     operands += streams
@@ -1543,7 +1599,7 @@
     out_specs = [hbm, hbm, hbm, vmem, vmem, hbm, hbm, hbm, hbm, vmem, hbm, hbm, hbm]
     scratch = [pltpu.VMEM((width, GU), BF)]
     scratch += [pltpu.VMEM((total_rows, c), BF) for c in (hidden_cols, 2 * hidden_cols, 512, 640)]
-    scratch += [pltpu.VMEM((line, window, total_rows), BF)] * 2 + [pltpu.VMEM((1, total_rows, window), BF)]
+    scratch += [pltpu.VMEM((line, window, total_rows), BF)] * 2 + [pltpu.VMEM((2, total_rows, window), BF)]
     scratch += [
         pltpu.VMEM((T, own, width), BF),
         pltpu.VMEM((own, width), F32),
@@ -1551,6 +1607,8 @@
         pltpu.VMEM((own, width), F32),
         pltpu.VMEM((own, width), F32),
         pltpu.VMEM((8, width), F32),
+        pltpu.VMEM((own, width), BF),
+        pltpu.VMEM((OWN[2], width), F32),
         pltpu.VMEM((T, 8, width), F32),
     ]
     scratch += [
@@ -1571,7 +1629,7 @@
     dma = pltpu.SemaphoreType.DMA
     chunks = width // DC
     k = PLACES + 1
-    scratch += [dma((1, chunks))] * 4 + [dma((1, 3))] * 2
+    scratch += [dma((2, chunks))] * 4 + [dma((2, 3))] * 2
     scratch += [dma((k, line))] * 4 + [dma((k,))]
     scratch += [dma((3, 4)), dma((3, 3))]
     scratch += [dma((24,)), dma((2, 2, RECUR)), dma((4,)), dma((k, 8)), dma((2,))]

time: 750 us -> 730 us (0.973)
  Pallas kernels: 727 us -> 706 us
    pallas_call x1, Pallas kernels: 124 us -> 116 us  [backward(): pl.pallas_call(functools.partial(backward_kernel, n), out_shape=[jax.Shap...]
where the time goes in v4:
time: 730 us; the launch traced here: 720 us
  Pallas kernels  706 us (97%)
  local copies, waits for them, and re-layouts  12.1 us (2%)
    pallas_call x1, Pallas kernels, forward(): pl.pallas_call(functools.partial(forward_kernel, n), out_shape=[jax.Shape...  326 us
    pallas_call x1, Pallas kernels, gradients(): pl.pallas_call(functools.partial(gradient_kernel, n), out_shape=[jax.Shap...  260 us
    pallas_call x1, Pallas kernels, backward(): pl.pallas_call(functools.partial(backward_kernel, n), out_shape=[jax.Shap...  116 us

profile of v4, /device:TPU:0, one launch (start us, length us, event | category | flops | bytes accessed | tf_op | source)
XLA Modules:
  0.0 720.3 jit_solution(16054919180246548843)
XLA Ops:
  0.6 0.7 convert_element_type.9
  1.3 0.1 convert_element_type.10
  1.4 0.8 reshape.32.refs_12_
  2.2 0.6 reshape.30.refs_11_
  2.9 326.3 %shard_map.221 = (bf16[2048,5376]{1,0:T(8,128)(2,1)}, f32[8,2048]{1,0:T(8,128)}, bf16[96,2048]{1,0:T(8,128)(2,1)}, f32[96,2048]{1,0:T(8,128)}, bf16[4,48,2048]{2...) custom-call(bf16[2,48,2048]{2,1,0:T(8,128)(2,1)} %refs_0_.1, ...), custom_call_target="tpu_custom_call" | custom-call | tf_op jit(solution)/shard_map/pallas_call | solution.py:726
  329.2 116.5 %shard_map.222 = (bf16[4,96,2048]{2,1,0:T(8,128)(2,1)}, bf16[4,80,2048]{2,1,0:T(8,128)(2,1)}, bf16[4,48,2048]{2,1,0:T(8,128)(2,1)}, bf16[384,2816]{1,0:T(8,128)(...) custom-call(bf16[2048,5376]{1,0:T(8,128)(2,1)} %get-tuple-element.79, ...), custom_call_target="tpu_custom_call" | custom-call | tf_op jit(solution)/shard_map/pallas_call | solution.py:994
  445.6 260.4 %shard_map.223 = (bf16[2,48,2048]{2,1,0:T(8,128)(2,1)}, f32[2,48,2048]{2,1,0:T(8,128)}, f32[256,512]{1,0:T(8,128)}, f32[64,256]{1,0:T(8,128)}, f32[64,256]{1,0:T...) custom-call(bf16[2048,5376]{1,0:T(8,128)(2,1)} %get-tuple-element.79, ...), custom_call_target="tpu_custom_call" | custom-call | tf_op jit(solution)/shard_map/pallas_call | solution.py:1636
  706.0 0.0 copy-start
  706.1 1.4 copy-done
  707.4 0.0 copy-start.1
  707.4 1.4 copy-done.1
  708.8 0.0 copy-start.2
  708.8 1.4 copy-done.2
  710.1 0.0 copy-start.3
  710.1 1.1 copy-done.3
  711.3 0.0 copy-start.4
  711.3 1.0 copy-done.4
  712.3 0.0 copy-start.5
  712.3 1.0 copy-done.5
  713.4 0.0 copy-start.6
  713.4 1.0 copy-done.6
  714.4 0.0 copy-start.7
  714.4 0.8 copy-done.7
  715.2 0.0 copy-start.8
  715.2 0.8 copy-done.8
  716.0 0.0 copy-start.9
  716.0 3.3 shard_map.224
  719.3 0.0 copy-done.9
  719.3 0.1 constant_dynamic-slice_fusion
  719.4 0.5 slice_bitcast_fusion
  (1 shorter events, 0.0 us)
Async XLA Ops:
  706.0 1.4 copy-start
  707.4 1.4 copy-start.1
  708.8 1.4 copy-start.2
  710.1 1.1 copy-start.3
  711.3 1.0 copy-start.4
  712.3 1.0 copy-start.5
  713.4 1.0 copy-start.6
  714.4 0.8 copy-start.7
  715.2 0.8 copy-start.8
  716.0 3.3 copy-start.9

commit v5 on v4

--- a/solution.py
+++ b/solution.py
@@ -427,14 +427,16 @@
     allowed = [next(it) for _ in range(RECUR)]
     names = ("normed", "qkv", "att", "mixed", "gu", "prod", "hidden", "first")
     saved_out = [dict((k, next(it)) for k in names) for _ in range(RECUR)]
+    dg_out = next(it)
     w = next(it)
+    dg, product_grad = next(it), next(it)
     perm, back, kv, wo_in, wd_in = [next(it) for _ in range(5)]
     gbuf, gall = next(it), next(it)
     tok, cot = next(it), next(it)
     saved = [dict((k, next(it)) for k in names) for _ in range(RECUR)]
     after, fin, cown = next(it), next(it), next(it)
     part, relay = next(it), next(it)
-    sums = [(next(it), next(it)) for _ in range(2 * RECUR)]
+    sums = [(next(it), next(it)) for _ in range(2 * RECUR - 1)]
     line_sems = [next(it) for _ in range(6)]
     row_sems = [next(it) for _ in range(6)]
     wsem = next(it)
@@ -613,6 +615,21 @@
         if level == 0:
             line.steps(up_piece)
             line.own(down_last + 1)
+        if level == RECUR - 1:
+            dg[...] = (cot_all[...].astype(F32).reshape(count, width) * act_last[...]).astype(BF).reshape(T, own, width)
+            write(dg, dg_out)
+
+            def grad_block(start, size):
+                product_grad[:, pl.ds(pl.multiple_of(start, 128), size)] = dot(
+                    dg[...].reshape(count, width), w[:, pl.ds(pl.multiple_of(WD + start, 128), size)], NN
+                )
+
+            @pl.loop(0, hidden_cols // 256)
+            def _(j):
+                grad_block(j * 256, 256)
+
+            if hidden_cols % 256:
+                grad_block(hidden_cols // 256 * 256, 128)
         rows.gather_finish(2 * level, mixed)
         write(s["mixed"], saved_out[level]["mixed"])
 
@@ -621,9 +638,16 @@
             gate = dot(x, w[:, pl.ds(pl.multiple_of(GU + start, 128), size)], NN)
             upward = dot(x, w[:, pl.ds(pl.multiple_of(GU + hidden_cols + start, 128), size)], NN)
             cols = pl.ds(pl.multiple_of(start, 128), size)
-            s["gu"][:, cols] = gate.astype(BF)
-            s["gu"][:, pl.ds(pl.multiple_of(hidden_cols + start, 128), size)] = upward.astype(BF)
-            s["prod"][:, cols] = (gate * jax.nn.sigmoid(gate) * upward).astype(BF)
+            high = pl.ds(pl.multiple_of(hidden_cols + start, 128), size)
+            sigma = jax.nn.sigmoid(gate)
+            s["prod"][:, cols] = (gate * sigma * upward).astype(BF)
+            if level == RECUR - 1:
+                up = product_grad[:, cols]
+                s["gu"][:, cols] = (up * upward * sigma * (1.0 + gate * (1.0 - sigma))).astype(BF)
+                s["gu"][:, high] = (up * gate * sigma).astype(BF)
+            else:
+                s["gu"][:, cols] = gate.astype(BF)
+                s["gu"][:, high] = upward.astype(BF)
 
         if level == 0:
             line.steps(down_piece)
@@ -706,7 +730,10 @@
         for entry in saved_shapes(own).values():
             shapes.append(entry)
             specs.append(hbm)
-    scratch = [pltpu.VMEM((width, COLS), BF)] + [pltpu.VMEM((total, total), BF)] * 2
+    shapes.append(((T, OWN[2], width), BF))
+    specs.append(hbm)
+    scratch = [pltpu.VMEM((width, COLS), BF), pltpu.VMEM((T, OWN[2], width), BF), pltpu.VMEM((T * OWN[2], hidden_cols), F32)]
+    scratch += [pltpu.VMEM((total, total), BF)] * 2
     scratch += [pltpu.VMEM((2,) + weights[1].shape[::-1], BF), pltpu.VMEM(weights[3].shape, BF), pltpu.VMEM(weights[6].shape, BF)]
     scratch += [pltpu.VMEM((n, 8, 128), F32), pltpu.VMEM((T, n, 8, 128), F32)]
     scratch += [pltpu.VMEM((T,) + tokens.shape, BF)] * 2
@@ -714,9 +741,8 @@
         scratch += [pltpu.VMEM(*entry) for entry in saved_shapes(own).values()]
     scratch += [pltpu.VMEM((OWN[0], width), F32), pltpu.VMEM((OWN[0], width), BF), pltpu.VMEM((OWN[0], width), F32)]
     scratch += [pltpu.VMEM((2, 2, OWN[0], width), BF), pltpu.VMEM((OWN[0], width), BF)]
-    for own in OWN:
-        for _ in range(2):
-            scratch += [pltpu.VMEM((2, own, width), BF), pltpu.VMEM((own, width), BF)]
+    for own in [own for own in OWN for _ in range(2)][:-1]:
+        scratch += [pltpu.VMEM((2, own, width), BF), pltpu.VMEM((own, width), BF)]
     dma = pltpu.SemaphoreType.DMA
     count = 1 + sum(2 if kind == "across" else 1 for kind, _, _ in RANGES)
     scratch += [dma((count, n // 2))] * 6
@@ -746,12 +772,12 @@
         lengths,
         freqs,
     )
-    w_all, gain, fin, cot_own, cot_all = outs[:5]
+    w_all, gain, fin, cot_own = outs[:4]
     tables = dict(zip(("cosine", "sine", "back", "act", "act_last"), outs[5:10]))
     tables["masks"] = outs[10:13]
     names = list(saved_shapes(1))
     saved = [dict(zip(names, outs[13 + 8 * level : 21 + 8 * level])) for level in range(RECUR)]
-    return w_all, gain, fin, cot_own, cot_all, tables, saved
+    return w_all, gain, fin, cot_own, outs[37], tables, saved
 
 
 def share_groups(block, allowed):
@@ -807,14 +833,13 @@
 
 def backward_kernel(n, *refs):
     it = iter(refs)
-    (w_all, gain, cot_own, cot_all, cosine, sine, act_own, act_last) = [next(it) for _ in range(8)]
+    w_all, gain, cot_own, cosine, sine, act_own, last_gug = [next(it) for _ in range(7)]
     allowed = [None] + [next(it) for _ in range(2)]
     saved_in = []
     for level in range(RECUR):
-        names = ("gu", "first") if level == 0 else ("gu", "first", "qkv", "hidden")
-        saved_in.append({k: next(it) for k in names})
-    dg_out = [next(it) for _ in range(3)]
-    gug_out = [next(it) for _ in range(3)]
+        saved_in.append({k: next(it) for k in saved_names(level)})
+    dg_out = [next(it) for _ in range(2)]
+    gug_out = [next(it) for _ in range(2)]
     og_out = [None] + [next(it) for _ in range(2)]
     qkvg_out = [None] + [next(it) for _ in range(2)]
     grad_out, gain_part = next(it), next(it)
@@ -822,10 +847,11 @@
     saved = []
     for level in range(RECUR):
         saved.append({k: next(it) for k in saved_in[level]})
-    dg = [next(it) for _ in range(3)]
-    gug = [next(it) for _ in range(3)]
+    dg = [next(it) for _ in range(2)]
+    gug = [next(it) for _ in range(2)]
     og = [None] + [next(it) for _ in range(2)]
     qkvg = [None] + [next(it) for _ in range(2)]
+    gug.append(next(it))
     grad, upstream, factors = next(it), next(it), next(it)
     part, relay = next(it), next(it)
     sums = [(next(it), next(it)) for _ in range(5)]
@@ -851,16 +877,16 @@
     def columns(start, size):
         load(("w", start), w_all.at[:, pl.ds(start, size)], w.at[:, pl.ds(start, size)])
 
-    columns(WD, hidden_cols)
+    last = RECUR - 1
+    load("gug", last_gug, gug[last])
+    columns(GU, 2 * hidden_cols)
     load("grad", cot_own, grad)
-    last = RECUR - 1
-    load(("gu", last), saved_in[last]["gu"], saved[last]["gu"])
-    columns(GU, 2 * hidden_cols)
     load(("first", last), saved_in[last]["first"], saved[last]["first"])
     columns(WO, 512)
     for name in ("qkv", "hidden"):
         load((name, last), saved_in[last][name], saved[last][name])
     columns(QKV, 640)
+    columns(WD, hidden_cols)
     for level in (1, 0):
         for name in saved_in[level]:
             load((name, level), saved_in[level][name], saved[level][name])
@@ -874,49 +900,45 @@
         base = 2 * (last - level)
         present = act_own[level, 0:own, :]
         if level == last:
-            dg[level][...] = (cot_all[...].astype(F32).reshape(count, width) * act_last[...]).astype(BF).reshape(
-                T, own, width
-            )
             loads["grad"].wait()
+            loads["gug"].wait()
+            loads["w", GU].wait()
         else:
             dg[level][p.t] = (present * grad[0:own, :]).astype(BF)
             view = dg[level].reshape(2, 2, own, width)
             rows.gather_start(base, view)
-        loads["gu", level].wait()
-
-        @pl.loop(0, hidden_cols // 128)
-        def _(j):
-            low = pl.ds(pl.multiple_of(j * 128, 128), 128)
-            high = pl.ds(pl.multiple_of(hidden_cols + j * 128, 128), 128)
-            gate = s["gu"][:, low].astype(F32)
-            upward = s["gu"][:, high].astype(F32)
-            sigma = jax.nn.sigmoid(gate)
-            factors[0:count, low] = upward * sigma * (1.0 + gate * (1.0 - sigma))
-            factors[0:count, high] = gate * sigma
-
-        if level == last:
-            loads["w", WD].wait()
-        else:
+            loads["gu", level].wait()
+
+            @pl.loop(0, hidden_cols // 128)
+            def _(j):
+                low = pl.ds(pl.multiple_of(j * 128, 128), 128)
+                high = pl.ds(pl.multiple_of(hidden_cols + j * 128, 128), 128)
+                gate = s["gu"][:, low].astype(F32)
+                upward = s["gu"][:, high].astype(F32)
+                sigma = jax.nn.sigmoid(gate)
+                factors[0:count, low] = upward * sigma * (1.0 + gate * (1.0 - sigma))
+                factors[0:count, high] = gate * sigma
+
+            if level == 1:
+                loads["w", WD].wait()
             rows.gather_finish(base, view)
-        write(dg[level], dg_out[level])
-
-        def hidden_block(start, size):
-            wcols = pl.ds(pl.multiple_of(WD + start, 128), size)
-            product_grad = dot(dg[level][...].reshape(count, width), w[:, wcols], NN)
-            low = pl.ds(pl.multiple_of(start, 128), size)
-            high = pl.ds(pl.multiple_of(hidden_cols + start, 128), size)
-            gug[level][:, low] = (product_grad * factors[0:count, low]).astype(BF)
-            gug[level][:, high] = (product_grad * factors[0:count, high]).astype(BF)
-
-        @pl.loop(0, hidden_cols // 256)
-        def _(j):
-            hidden_block(j * 256, 256)
-
-        if hidden_cols % 256:
-            hidden_block(hidden_cols // 256 * 256, 128)
-        write(gug[level], gug_out[level])
-        if level == last:
-            loads["w", GU].wait()
+            write(dg[level], dg_out[level])
+
+            def hidden_block(start, size):
+                wcols = pl.ds(pl.multiple_of(WD + start, 128), size)
+                product_grad = dot(dg[level][...].reshape(count, width), w[:, wcols], NN)
+                low = pl.ds(pl.multiple_of(start, 128), size)
+                high = pl.ds(pl.multiple_of(hidden_cols + start, 128), size)
+                gug[level][:, low] = (product_grad * factors[0:count, low]).astype(BF)
+                gug[level][:, high] = (product_grad * factors[0:count, high]).astype(BF)
+
+            @pl.loop(0, hidden_cols // 256)
+            def _(j):
+                hidden_block(j * 256, 256)
+
+            if hidden_cols % 256:
+                hidden_block(hidden_cols // 256 * 256, 128)
+            write(gug[level], gug_out[level])
 
         def mlp_tile(cols):
             return dot(gug[level][...], w[cols, GU : GU + 2 * hidden_cols], NT)
@@ -962,26 +984,30 @@
         copy.wait()
 
 
-def backward(n, w_all, gain, cot_own, cot_all, tables, saved):
+def saved_names(level):
+    return (("gu", "first"), ("gu", "first", "qkv", "hidden"), ("first", "qkv", "hidden"))[level]
+
+
+def backward(n, w_all, gain, cot_own, tables, saved):
     width = w_all.shape[0]
     hidden_cols = (COLS - GU) // 3
     vmem = pl.BlockSpec(memory_space=pltpu.VMEM)
     hbm = pl.BlockSpec(memory_space=pl.ANY)
-    operands = [w_all, gain, cot_own, cot_all, tables["cosine"], tables["sine"], tables["act"], tables["act_last"]]
+    operands = [w_all, gain, cot_own, tables["cosine"], tables["sine"], tables["act"], saved[RECUR - 1]["gu"]]
     operands += list(tables["masks"][1:])
-    specs = [hbm, vmem, hbm] + [vmem] * 7
+    specs = [hbm, vmem, hbm] + [vmem] * 3 + [hbm] + [vmem] * 2
     used = []
     for level in range(RECUR):
-        for name in ("gu", "first") if level == 0 else ("gu", "first", "qkv", "hidden"):
+        for name in saved_names(level):
             operands.append(saved[level][name])
             specs.append(hbm)
             used.append(saved[level][name])
-    outs = [((T, own, width), BF) for own in OWN]
-    outs += [((T * own, 2 * hidden_cols), BF) for own in OWN]
+    outs = [((T, own, width), BF) for own in OWN[:2]]
+    outs += [((T * own, 2 * hidden_cols), BF) for own in OWN[:2]]
     outs += [((T, own, width), BF) for own in OWN[1:]]
     outs += [((T * own, 640), BF) for own in OWN[1:]]
     scratch = [pltpu.VMEM(w_all.shape, BF)] + [pltpu.VMEM(u.shape, u.dtype) for u in used]
-    scratch += [pltpu.VMEM(*entry) for entry in outs]
+    scratch += [pltpu.VMEM(*entry) for entry in outs] + [pltpu.VMEM((T * OWN[2], 2 * hidden_cols), BF)]
     outs += [((OWN[0], width), F32), ((8, width), F32)]
     out_specs = [hbm] * (len(outs) - 1) + [vmem]
     scratch += [pltpu.VMEM((OWN[0], width), F32)] * 2 + [pltpu.VMEM((T * OWN[0], 2 * hidden_cols), F32)]
@@ -1002,12 +1028,12 @@
         ),
     )(*operands)
     return {
-        "dg": res[0:3],
-        "gug": res[3:6],
-        "og": res[6:8],
-        "qkvg": res[8:10],
-        "grad": res[10],
-        "gain_part": res[11],
+        "dg": res[0:2],
+        "gug": res[2:4],
+        "og": res[4:6],
+        "qkvg": res[6:8],
+        "grad": res[8],
+        "gain_part": res[9],
     }
 
 
@@ -1647,19 +1673,28 @@
 
 
 def hand_out_kernel(count, *refs):
+    held, sems = refs[2 * count : 3 * count], refs[3 * count]
+    into = [pltpu.make_async_copy(refs[i], held[i], sems.at[0, i]) for i in range(count)]
+    out = [pltpu.make_async_copy(held[i], refs[count + i], sems.at[1, i]) for i in range(count)]
+    for copy in into:
+        copy.start()
     for i in range(count):
-        refs[count + i][...] = refs[i][...]
+        into[i].wait()
+        out[i].start()
+    for copy in out:
+        copy.wait()
 
 
 def hand_out(values):
-    vmem = pl.BlockSpec(memory_space=pltpu.VMEM)
+    hbm = pl.BlockSpec(memory_space=pl.ANY)
     count = len(values)
     return pl.pallas_call(
         functools.partial(hand_out_kernel, count),
         out_shape=[jax.ShapeDtypeStruct(v.shape, v.dtype) for v in values],
-        in_specs=[vmem] * count,
-        out_specs=[vmem] * count,
-        compiler_params=pltpu.CompilerParams(vmem_limit_bytes=40 << 20),
+        in_specs=[hbm] * count,
+        out_specs=[hbm] * count,
+        scratch_shapes=[pltpu.VMEM(v.shape, v.dtype) for v in values] + [pltpu.SemaphoreType.DMA((2, count))],
+        compiler_params=pltpu.CompilerParams(vmem_limit_bytes=62 << 20),
     )(*values)
 
 
@@ -1667,10 +1702,12 @@
     tokens, depth, lengths, cotangent = args[:4]
     attn_gain, mlp_gain = args[11:]
     index = lax.axis_index("tensor")
-    w_all, gain, fin, cot_own, cot_all, tables, saved = forward(
+    w_all, gain, fin, cot_own, last_dg, tables, saved = forward(
         n, tokens, depth, lengths[:, 0], cotangent, args[4:11], attn_gain, mlp_gain
     )
-    bwd = backward(n, w_all, gain, cot_own, cot_all, tables, saved)
+    bwd = backward(n, w_all, gain, cot_own, tables, saved)
+    bwd["dg"] = list(bwd["dg"]) + [last_dg]
+    bwd["gug"] = list(bwd["gug"]) + [saved[RECUR - 1]["gu"]]
     res = gradients(n, w_all, gain, tables, saved, bwd, fin)
     gain_sum = res[9]
     activations, tokens_grad, dq, dk, dv, dwo, dgate, dup, dwd = hand_out(res[:9])

time: 730 us -> 720 us (0.986)
  local copies, waits for them, and re-layouts: 12.1 us -> 2.15 us
    unnamed x20 -> x2, local copies, waits for them, and re-layouts: 9.97 us -> 0.01 us
where the time goes in v5:
time: 720 us; the launch traced here: 711 us
  Pallas kernels  707 us (98%)
    pallas_call x1, Pallas kernels, forward(): pl.pallas_call(functools.partial(forward_kernel, n), out_shape=[jax.Shape...  326 us
    pallas_call x1, Pallas kernels, gradients(): pl.pallas_call(functools.partial(gradient_kernel, n), out_shape=[jax.Shap...  260 us
    pallas_call x1, Pallas kernels, backward(): pl.pallas_call(functools.partial(backward_kernel, n), out_shape=[jax.Shap...  115 us

profile of v5, /device:TPU:0, one launch (start us, length us, event | category | flops | bytes accessed | tf_op | source)
XLA Modules:
  0.0 711.0 jit_solution(4270456812745182958)
XLA Ops:
  0.6 0.7 convert_element_type.9
  1.3 0.1 convert_element_type.10
  1.4 0.8 reshape.32.refs_12_
  2.2 0.6 reshape.30.refs_11_
  2.9 326.5 %shard_map.221 = (bf16[2048,5376]{1,0:T(8,128)(2,1)}, f32[8,2048]{1,0:T(8,128)}, bf16[96,2048]{1,0:T(8,128)(2,1)}, f32[96,2048]{1,0:T(8,128)}, bf16[4,48,2048]{2...) custom-call(bf16[2,48,2048]{2,1,0:T(8,128)(2,1)} %refs_0_.1, ...), custom_call_target="tpu_custom_call" | custom-call | tf_op jit(solution)/shard_map/pallas_call | solution.py:752
  329.3 114.6 %shard_map.222 = (bf16[4,96,2048]{2,1,0:T(8,128)(2,1)}, bf16[4,80,2048]{2,1,0:T(8,128)(2,1)}, bf16[384,2816]{1,0:T(8,128)(2,1)}, bf16[320,2816]{1,0:T(8,128)(2,1...) custom-call(bf16[2048,5376]{1,0:T(8,128)(2,1)} %get-tuple-element.76, ...), custom_call_target="tpu_custom_call" | custom-call | tf_op jit(solution)/shard_map/pallas_call | solution.py:1020
  443.9 260.4 %shard_map.223 = (bf16[2,48,2048]{2,1,0:T(8,128)(2,1)}, f32[2,48,2048]{2,1,0:T(8,128)}, f32[256,512]{1,0:T(8,128)}, f32[64,256]{1,0:T(8,128)}, f32[64,256]{1,0:T...) custom-call(bf16[2048,5376]{1,0:T(8,128)(2,1)} %get-tuple-element.76, ...), custom_call_target="tpu_custom_call" | custom-call | tf_op jit(solution)/shard_map/pallas_call | solution.py:1662
  704.3 0.0 copy-start
  704.4 5.6 shard_map.224
  710.0 0.0 copy-done
  710.0 0.1 constant_dynamic-slice_fusion
  710.0 0.5 slice_bitcast_fusion
  (1 shorter events, 0.0 us)
Async XLA Ops:
  704.3 5.6 copy-start

commit v6 on v5

--- a/solution.py
+++ b/solution.py
@@ -655,6 +655,7 @@
             line.step(down_last + 1, 1)
             line.arrive(gate_piece)
             line.arrive(up_piece)
+            write(w.at[:, pl.ds(0, WD)], w_out.at[:, pl.ds(0, WD)])
 
         @pl.loop(0, hidden_cols // 256)
         def _(j):
@@ -669,7 +670,7 @@
                 line.step(down_last, k)
                 line.step(down_last + 1, k)
             line.arrive(down_piece)
-            write(w, w_out)
+            write(w.at[:, pl.ds(WD, hidden_cols)], w_out.at[:, pl.ds(WD, hidden_cols)])
 
         if level < RECUR - 1:
 

time: 720 us -> 720 us (level)
  no operation moved by 1% of the time
where the time goes in v6:
time: 720 us; the launch traced here: 711 us
  Pallas kernels  707 us (98%)
    pallas_call x1, Pallas kernels, forward(): pl.pallas_call(functools.partial(forward_kernel, n), out_shape=[jax.Shape...  326 us
    pallas_call x1, Pallas kernels, gradients(): pl.pallas_call(functools.partial(gradient_kernel, n), out_shape=[jax.Shap...  260 us
    pallas_call x1, Pallas kernels, backward(): pl.pallas_call(functools.partial(backward_kernel, n), out_shape=[jax.Shap...  115 us

profile of v6, /device:TPU:0, one launch (start us, length us, event | category | flops | bytes accessed | tf_op | source)
XLA Modules:
  0.0 711.0 jit_solution(6788725099757223321)
XLA Ops:
  0.6 0.7 convert_element_type.9
  1.3 0.1 convert_element_type.10
  1.4 0.8 reshape.32.refs_12_
  2.2 0.6 reshape.30.refs_11_
  2.9 326.4 %shard_map.221 = (bf16[2048,5376]{1,0:T(8,128)(2,1)}, f32[8,2048]{1,0:T(8,128)}, bf16[96,2048]{1,0:T(8,128)(2,1)}, f32[96,2048]{1,0:T(8,128)}, bf16[4,48,2048]{2...) custom-call(bf16[2,48,2048]{2,1,0:T(8,128)(2,1)} %refs_0_.1, ...), custom_call_target="tpu_custom_call" | custom-call | tf_op jit(solution)/shard_map/pallas_call | solution.py:753
  329.3 114.6 %shard_map.222 = (bf16[4,96,2048]{2,1,0:T(8,128)(2,1)}, bf16[4,80,2048]{2,1,0:T(8,128)(2,1)}, bf16[384,2816]{1,0:T(8,128)(2,1)}, bf16[320,2816]{1,0:T(8,128)(2,1...) custom-call(bf16[2048,5376]{1,0:T(8,128)(2,1)} %get-tuple-element.76, ...), custom_call_target="tpu_custom_call" | custom-call | tf_op jit(solution)/shard_map/pallas_call | solution.py:1021
  443.9 260.4 %shard_map.223 = (bf16[2,48,2048]{2,1,0:T(8,128)(2,1)}, f32[2,48,2048]{2,1,0:T(8,128)}, f32[256,512]{1,0:T(8,128)}, f32[64,256]{1,0:T(8,128)}, f32[64,256]{1,0:T...) custom-call(bf16[2048,5376]{1,0:T(8,128)(2,1)} %get-tuple-element.76, ...), custom_call_target="tpu_custom_call" | custom-call | tf_op jit(solution)/shard_map/pallas_call | solution.py:1663
  704.3 0.0 copy-start
  704.4 5.6 shard_map.224
  710.0 0.0 copy-done
  710.0 0.1 constant_dynamic-slice_fusion
  710.0 0.5 slice_bitcast_fusion
  (1 shorter events, 0.0 us)
Async XLA Ops:
  704.3 5.6 copy-start
